TPU v7x, 512 devices: a whole 4x4x16 slice. The times are simulated.
512 devices in a mesh: mirror: 2 (over core), slab: 256 (over y, z, x).
Axes of the slice: x: 4, y: 4, z: 16, core: 2. Of those that a mesh axis runs over, the one named last changes fastest.
Arguments:
- density: float32 [1024, 8, 128], P('slab'), may hold values from 0.2 to 1
- load_mask: int32 [2, 1024, 8, 128], P('mirror', 'slab'), may hold values 0 or 1
- fixed_mask: int32 [2, 1024, 8, 128], P('mirror', 'slab'), may hold values 0 or 1
- sweeps: int32 [2], replicated, may hold values from 1 to 4, as said below
Outputs:
- displacement: float32 [2, 3, 1024, 8, 128], P('mirror', None, 'slab')
- residual: float32 [2, 3, 1024, 8, 128], P('mirror', None, 'slab')
- sensitivity: float32 [1024, 8, 128], P('slab')
Inputs may be any that keep to these rules, and one draw needn't show every extreme that they name: `sweeps`: one of the two counts is 4.
All inputs are finite; a program needn't handle non-finite values. No bound on the sum of `load_mask` or of `fixed_mask` on one device may be relied on, other than what follows from the above.
Results may differ from a plain program's by a relative error of at most 0.0003.
Values sent between devices are 32-bit elements; how exact they have to be, the bound alone decides.
No kernel may reach another device: no remote copies, remote signals or barrier semaphores. Data moves between devices by JAX's collectives and lax.ppermute only.
A program may use at most 64 MiB of HBM per device.

v0:
```python
import jax
import jax.numpy as jnp
import numpy as np
from jax import lax
from jax.sharding import PartitionSpec as P

SWEEPS = 4


MODULUS_FLOOR = 0.001
EIG_LOWER = 0.05
EIG_UPPER = 1.0


def passed_along(array, axis, by):
    length = lax.axis_size(axis)
    pairs = [(i, i + by) for i in range(length) if 0 <= i + by < length]
    return lax.ppermute(array, axis, pairs)


def element_matrix():
    poisson = 0.3
    lame_first = poisson / ((1.0 + poisson) * (1.0 - 2.0 * poisson))
    shear_modulus = 0.5 / (1.0 + poisson)
    elastic = np.zeros((6, 6))
    elastic[:3, :3] = lame_first
    for i in range(3):
        elastic[i, i] += 2.0 * shear_modulus
        elastic[i + 3, i + 3] = shear_modulus
    points = [0.5 - 0.5 / np.sqrt(3.0), 0.5 + 0.5 / np.sqrt(3.0)]
    stiffness = np.zeros((24, 24))
    for p in points:
        for q in points:
            for s in points:
                strain = np.zeros((6, 24))
                for corner in range(8):
                    z_bit, y_bit, x_bit = (corner // 4, corner // 2 % 2, corner % 2)
                    weight_z = p if z_bit else 1.0 - p
                    weight_y = q if y_bit else 1.0 - q
                    weight_x = s if x_bit else 1.0 - s
                    slope_z = 1.0 if z_bit else -1.0
                    slope_y = 1.0 if y_bit else -1.0
                    slope_x = 1.0 if x_bit else -1.0
                    grad_x = slope_x * weight_y * weight_z
                    grad_y = weight_x * slope_y * weight_z
                    grad_z = weight_x * weight_y * slope_z
                    c = 3 * corner
                    strain[0, c] = grad_x
                    strain[1, c + 1] = grad_y
                    strain[2, c + 2] = grad_z
                    strain[3, c] = grad_y
                    strain[3, c + 1] = grad_x
                    strain[4, c + 1] = grad_z
                    strain[4, c + 2] = grad_y
                    strain[5, c] = grad_z
                    strain[5, c + 2] = grad_x
                stiffness += strain.T @ elastic @ strain / 8.0
    return stiffness


def element_terms(extended, stiffness):
    planes, rows_y, cols_x = (extended.shape[1] - 1, extended.shape[2] - 1, extended.shape[3] - 1)
    blocks = []
    for corner in range(8):
        z_bit, y_bit, x_bit = (corner // 4, corner // 2 % 2, corner % 2)
        blocks.append(
            extended[:, z_bit : z_bit + planes, y_bit : y_bit + rows_y, x_bit : x_bit + cols_x]
        )
    local_dofs = jnp.concatenate(blocks, axis=0)
    forces = jnp.einsum("ij,jabc->iabc", stiffness, local_dofs, precision=lax.Precision.HIGHEST)
    return (local_dofs, forces)


def spread_corners(forces):
    summed = None
    for corner in range(8):
        z_bit, y_bit, x_bit = (corner // 4, corner // 2 % 2, corner % 2)
        padded = jnp.pad(
            forces[3 * corner : 3 * corner + 3],
            ((0, 0), (z_bit, 1 - z_bit), (y_bit, 1 - y_bit), (x_bit, 1 - x_bit)),
        )
        summed = padded if summed is None else summed + padded
    return summed


def extend_field(vector, use_slab):
    if use_slab:
        upper_plane = passed_along(vector[:, :1], "slab", -1)
    else:
        upper_plane = jnp.zeros_like(vector[:, :1])
    stacked = jnp.concatenate([vector, upper_plane], axis=1)
    column = passed_along(stacked[:, :, :, :1], "mirror", -1)
    widened = jnp.concatenate([stacked, column], axis=3)
    return jnp.pad(widened, ((0, 0), (0, 0), (0, 1), (0, 0)))


def gather_forces(spread, use_slab):
    planes, rows_y, cols_x = (spread.shape[1] - 1, spread.shape[2] - 1, spread.shape[3] - 1)
    interior = spread[:, :, :rows_y, :cols_x]
    incoming = passed_along(spread[:, :, :rows_y, cols_x:], "mirror", 1)
    interior = jnp.concatenate([interior[:, :, :, :1] + incoming, interior[:, :, :, 1:]], axis=3)
    owned = interior[:, :planes]
    if use_slab:
        arriving = passed_along(interior[:, planes:], "slab", 1)
        owned = jnp.concatenate([owned[:, :1] + arriving, owned[:, 1:]], axis=1)
    return owned


def operate(vector, modulus, stiffness, free_mask, use_slab):
    extended = extend_field(free_mask * vector, use_slab)
    _, forces = element_terms(extended, stiffness)
    owned = gather_forces(spread_corners(modulus[None] * forces), use_slab)
    return free_mask * owned + (1.0 - free_mask) * vector


def l1_diagonal(modulus, stiffness, free_mask, use_slab):
    row_abs = jnp.sum(jnp.abs(stiffness), axis=1)
    owned = gather_forces(spread_corners(row_abs[:, None, None, None] * modulus[None]), use_slab)
    return free_mask * owned + (1.0 - free_mask)


def make_operator(modulus, stiffness, free_mask, use_slab):

    def apply_plain(vector):
        return operate(vector, modulus, stiffness, free_mask, use_slab)

    return (apply_plain, l1_diagonal(modulus, stiffness, free_mask, use_slab))


def chebyshev(operator_fn, scaling, target, sweep_count):
    centre_eig = 0.5 * (EIG_UPPER + EIG_LOWER)
    half_width = 0.5 * (EIG_UPPER - EIG_LOWER)
    ratio_eig = centre_eig / half_width
    rho_now = 1.0 / ratio_eig
    update = target / (scaling * centre_eig)
    iterate = update
    for k in range(1, SWEEPS):
        defect = target - operator_fn(iterate)
        rho_next = 1.0 / (2.0 * ratio_eig - rho_now)
        update_next = rho_next * rho_now * update + 2.0 * rho_next / half_width * defect / scaling
        taken = k < sweep_count
        iterate = jnp.where(taken, iterate + update_next, iterate)
        update = jnp.where(taken, update_next, update)
        rho_now = rho_next
    return iterate


def restrict_sum(vector):
    comps, planes, rows_y, cols_x = vector.shape
    grouped = vector.reshape(comps, planes // 4, 4, rows_y // 4, 4, cols_x // 4, 4)
    return jnp.sum(grouped, axis=(2, 4, 6))


def coarse_modulus(modulus):
    planes, rows_y, cols_x = modulus.shape
    grouped = modulus.reshape(planes // 4, 4, rows_y // 4, 4, cols_x // 4, 4)
    return jnp.mean(grouped, axis=(1, 3, 5))


def prolong_copy(vector):
    return jnp.repeat(jnp.repeat(jnp.repeat(vector, 4, axis=1), 4, axis=2), 4, axis=3)


def window_solve(coarse_target, modulus_low, stiffness, sweep_count):
    own_planes = coarse_target.shape[1]
    depth = (SWEEPS + own_planes - 1) // own_planes
    margin = depth * own_planes
    packed = jnp.concatenate([coarse_target, modulus_low[None]], axis=0)
    offsets = list(range(depth, 0, -1)) + list(range(-1, -depth - 1, -1))
    pieces = [passed_along(packed, "slab", offset) for offset in offsets]
    window = jnp.concatenate(pieces[:depth] + [packed] + pieces[depth:], axis=1)
    total_planes = own_planes * lax.axis_size("slab")
    plane_ids = (
        lax.axis_index("slab") * own_planes - margin + jnp.arange(window.shape[1], dtype=jnp.int32)
    )
    inside = ((plane_ids >= 0) & (plane_ids < total_planes)).astype(jnp.float32)
    window_free = inside[None, :, None, None] * jnp.ones((1,) + window.shape[1:], jnp.float32)
    window_op, window_scale = make_operator(window[3], stiffness, window_free, False)
    solved = chebyshev(window_op, window_scale, window[:3] * window_free, sweep_count)
    return solved[:, margin : margin + own_planes]


def on_device(density, load_mask, fixed_mask, sweeps):
    stiffness = jnp.asarray(element_matrix(), jnp.float32)
    mirror_side = lax.axis_index("mirror")
    density_here = jnp.where(mirror_side == 1, density[..., ::-1], density)
    modulus = MODULUS_FLOOR + density_here**3 * (1.0 - MODULUS_FLOOR)
    free_mask = (1 - fixed_mask[0]).astype(jnp.float32)[None]
    loads = load_mask[0].astype(jnp.float32)[None]
    direction = jnp.array([0.4, -0.3, -1.0], jnp.float32)[:, None, None, None]
    right = free_mask * loads * direction
    fine_op, fine_scale = make_operator(modulus, stiffness, free_mask, True)
    smooth = chebyshev(fine_op, fine_scale, right, sweeps[0])
    leftover = right - fine_op(smooth)
    coarse_target = restrict_sum(leftover)
    modulus_low = coarse_modulus(modulus)
    coarse_stiff = 4.0 * stiffness
    coarse_sol = window_solve(coarse_target, modulus_low, coarse_stiff, sweeps[1])
    precond = smooth + free_mask * prolong_copy(coarse_sol)
    residual_dot = lax.psum(jnp.sum(right * precond), ("mirror", "slab"))
    image = fine_op(precond)
    curvature = lax.psum(jnp.sum(precond * image), ("mirror", "slab"))
    alpha = residual_dot / curvature
    moved = alpha * precond
    left_over = right - alpha * image
    extended = extend_field(moved, True)
    local_dofs, forces = element_terms(extended, stiffness)
    energy = jnp.sum(local_dofs * forces, axis=0)
    slope = -3.0 * density_here**2 * (1.0 - MODULUS_FLOOR) * energy
    slope_first = jnp.where(mirror_side == 1, slope[..., ::-1], slope)
    sensitivity = lax.psum(slope_first, "mirror")
    return (moved[None], left_over[None], sensitivity)


def solution(mesh):
    return jax.shard_map(
        on_device,
        mesh=mesh,
        in_specs=(
            P("slab", None, None),
            P("mirror", "slab", None, None),
            P("mirror", "slab", None, None),
            P(),
        ),
        out_specs=(
            P("mirror", None, "slab", None, None),
            P("mirror", None, "slab", None, None),
            P("slab", None, None),
        ),
        check_vma=False,
    )
```

profile of v0, /device:TPU:39, one launch (start us, length us, event | category | flops | bytes accessed | tf_op | source)
XLA Modules:
  0.0 337.5 jit_solution(11288202189194255143)
XLA Ops:
  1.8 1.3 collective-permute-start
  5.4 3.5 %collective-permute-start.1 = (f32[3,1,8,128]{3,0,2,1:T(4,128)S(1)}, f32[3,1,8,128]{3,0,2,1:T(4,128)S(1)}, u32[]{:S(2)}, u32[]{:S(2)}) collective-permute-start(f32[3,1,8,128]{3,0,2,1:T(4,128)S(1)} %pad_maximum_fusion.30), channel_id=1, source_target_pairs={{0,1},{1,2},{2,3},{3,4},{4,5},{5,6},{6,7},{7,8},{8,9},{9,10},{10,1... | collective-permute-start | bytes 36872 | tf_op jit(solution)/shard_map/ppermute | solution.py:18
  10.1 2.5 collective-permute-start.2
  12.6 4.2 %collective-permute-done.2 = f32[3,1,8,128]{3,0,2,1:T(4,128)S(1)} collective-permute-done((f32[3,1,8,128]{3,0,2,1:T(4,128)S(1)}, f32[3,1,8,128]{3,0,2,1:T(4,128)S(1)}, u32[]{:S(2)}, u32[]{:S(2)}) %collective-permute-start.2) | collective-permute-done | bytes 12320 | tf_op jit(solution)/shard_map/ppermute | solution.py:18
  16.8 4.9 %collective-permute-start.3 = (f32[3,5,8,1]{3,0,2,1:T(4,128)S(1)}, f32[3,5,8,1]{3,0,2,1:T(4,128)S(1)}, u32[]{:S(2)}, u32[]{:S(2)}) collective-permute-start(f32[3,5,8,1]{3,0,2,1:T(4,128)S(1)} %slice_maximum_fusion.5), channel_id=1, source_target_pairs={{256,0},{257,1},{258,2},{259,3},{260,4},{261,5},{262,6},{263,7},{2... | collective-permute-start | bytes 1448 | tf_op jit(solution)/shard_map/ppermute | solution.py:18
  24.6 1.3 collective-permute-start.4
  27.8 3.5 %collective-permute-start.5 = (f32[3,1,8,128]{3,0,2,1:T(4,128)S(1)}, f32[3,1,8,128]{3,0,2,1:T(4,128)S(1)}, u32[]{:S(2)}, u32[]{:S(2)}) collective-permute-start(f32[3,1,8,128]{3,0,2,1:T(4,128)S(1)} %pad_maximum_fusion.29), channel_id=1, source_target_pairs={{0,1},{1,2},{2,3},{3,4},{4,5},{5,6},{6,7},{7,8},{8,9},{9,10},{10,1... | collective-permute-start | bytes 36872 | tf_op jit(solution)/shard_map/ppermute | solution.py:18
  32.5 1.9 collective-permute-start.6
  34.5 4.8 %collective-permute-done.6 = f32[3,1,8,128]{3,0,2,1:T(4,128)S(1)} collective-permute-done((f32[3,1,8,128]{3,0,2,1:T(4,128)S(1)}, f32[3,1,8,128]{3,0,2,1:T(4,128)S(1)}, u32[]{:S(2)}, u32[]{:S(2)}) %collective-permute-start.6) | collective-permute-done | bytes 12320 | tf_op jit(solution)/shard_map/ppermute | solution.py:18
  39.3 4.7 %collective-permute-start.7 = (f32[3,5,8,1]{3,0,2,1:T(4,128)S(1)}, f32[3,5,8,1]{3,0,2,1:T(4,128)S(1)}, u32[]{:S(2)}, u32[]{:S(2)}) collective-permute-start(f32[3,5,8,1]{3,0,2,1:T(4,128)S(1)} %slice_maximum_fusion.4), channel_id=1, source_target_pairs={{256,0},{257,1},{258,2},{259,3},{260,4},{261,5},{262,6},{263,7},{2... | collective-permute-start | bytes 1448 | tf_op jit(solution)/shard_map/ppermute | solution.py:18
  46.8 1.3 collective-permute-start.8
  50.1 3.5 %collective-permute-start.9 = (f32[3,1,8,128]{3,0,2,1:T(4,128)S(1)}, f32[3,1,8,128]{3,0,2,1:T(4,128)S(1)}, u32[]{:S(2)}, u32[]{:S(2)}) collective-permute-start(f32[3,1,8,128]{3,0,2,1:T(4,128)S(1)} %pad_maximum_fusion.28), channel_id=1, source_target_pairs={{0,1},{1,2},{2,3},{3,4},{4,5},{5,6},{6,7},{7,8},{8,9},{9,10},{10,1... | collective-permute-start | bytes 36872 | tf_op jit(solution)/shard_map/ppermute | solution.py:18
  54.8 1.9 collective-permute-start.10
  56.8 4.7 %collective-permute-done.10 = f32[3,1,8,128]{3,0,2,1:T(4,128)S(1)} collective-permute-done((f32[3,1,8,128]{3,0,2,1:T(4,128)S(1)}, f32[3,1,8,128]{3,0,2,1:T(4,128)S(1)}, u32[]{:S(2)}, u32[]{:S(2)}) %collective-permute-start.10) | collective-permute-done | bytes 12320 | tf_op jit(solution)/shard_map/ppermute | solution.py:18
  61.5 4.4 %collective-permute-start.11 = (f32[3,5,8,1]{3,0,2,1:T(4,128)S(1)}, f32[3,5,8,1]{3,0,2,1:T(4,128)S(1)}, u32[]{:S(2)}, u32[]{:S(2)}) collective-permute-start(f32[3,5,8,1]{3,0,2,1:T(4,128)S(1)} %slice_maximum_fusion.3), channel_id=1, source_target_pairs={{256,0},{257,1},{258,2},{259,3},{260,4},{261,5},{262,6},{263,7},{2... | collective-permute-start | bytes 1448 | tf_op jit(solution)/shard_map/ppermute | solution.py:18
  68.7 1.3 collective-permute-start.12
  72.0 3.5 %collective-permute-start.13 = (f32[3,1,8,128]{3,0,2,1:T(4,128)S(1)}, f32[3,1,8,128]{3,0,2,1:T(4,128)S(1)}, u32[]{:S(2)}, u32[]{:S(2)}) collective-permute-start(f32[3,1,8,128]{3,0,2,1:T(4,128)S(1)} %pad_maximum_fusion.27), channel_id=1, source_target_pairs={{0,1},{1,2},{2,3},{3,4},{4,5},{5,6},{6,7},{7,8},{8,9},{9,10},{10,1... | collective-permute-start | bytes 36872 | tf_op jit(solution)/shard_map/ppermute | solution.py:18
  77.4 1.9 collective-permute-start.14
  93.0 3.4 %collective-permute-start.15 = (f32[3,5,8,1]{3,0,2,1:T(4,128)S(1)}, f32[3,5,8,1]{3,0,2,1:T(4,128)S(1)}, u32[]{:S(2)}, u32[]{:S(2)}) collective-permute-start(f32[3,5,8,1]{3,0,2,1:T(4,128)S(1)} %slice_maximum_fusion.2), channel_id=1, source_target_pairs={{256,0},{257,1},{258,2},{259,3},{260,4},{261,5},{262,6},{263,7},{2... | collective-permute-start | bytes 1448 | tf_op jit(solution)/shard_map/ppermute | solution.py:18
  99.0 1.3 collective-permute-start.16
  105.3 5.7 %collective-permute-start.17 = (f32[3,1,8,128]{3,0,2,1:T(4,128)S(1)}, f32[3,1,8,128]{3,0,2,1:T(4,128)S(1)}, u32[]{:S(2)}, u32[]{:S(2)}) collective-permute-start(f32[3,1,8,128]{3,0,2,1:T(4,128)S(1)} %pad_maximum_fusion.26), channel_id=1, source_target_pairs={{0,1},{1,2},{2,3},{3,4},{4,5},{5,6},{6,7},{7,8},{8,9},{9,10},{10,1... | collective-permute-start | bytes 36872 | tf_op jit(solution)/shard_map/ppermute | solution.py:18
  114.5 3.5 %collective-permute-start.18 = (f32[4,1,2,32]{3,0,2,1:T(4,128)S(1)}, f32[4,1,2,32]{3,0,2,1:T(4,128)S(1)}, u32[]{:S(2)}, u32[]{:S(2)}) collective-permute-start(f32[4,1,2,32]{3,0,2,1:T(4,128)S(1)} %pad_maximum_fusion.31), channel_id=1, source_target_pairs={{0,4},{1,5},{2,6},{3,7},{4,8},{5,9},{6,10},{7,11},{8,12},{9,13},{1... | collective-permute-start | bytes 3080 | tf_op jit(solution)/shard_map/ppermute | solution.py:18
  118.8 5.6 %collective-permute-start.19 = (f32[4,1,2,32]{3,0,2,1:T(4,128)S(1)}, f32[4,1,2,32]{3,0,2,1:T(4,128)S(1)}, u32[]{:S(2)}, u32[]{:S(2)}) collective-permute-start(f32[4,1,2,32]{3,0,2,1:T(4,128)S(1)} %pad_maximum_fusion.31), channel_id=1, source_target_pairs={{0,3},{1,4},{2,5},{3,6},{4,7},{5,8},{6,9},{7,10},{8,11},{9,12},{10... | collective-permute-start | bytes 3080 | tf_op jit(solution)/shard_map/ppermute | solution.py:18
  124.4 10.7 %collective-permute-start.20 = (f32[4,1,2,32]{3,0,2,1:T(4,128)S(1)}, f32[4,1,2,32]{3,0,2,1:T(4,128)S(1)}, u32[]{:S(2)}, u32[]{:S(2)}) collective-permute-start(f32[4,1,2,32]{3,0,2,1:T(4,128)S(1)} %pad_maximum_fusion.31), channel_id=1, source_target_pairs={{0,2},{1,3},{2,4},{3,5},{4,6},{5,7},{6,8},{7,9},{8,10},{9,11},{10,... | collective-permute-start | bytes 3080 | tf_op jit(solution)/shard_map/ppermute | solution.py:18
  135.1 1.9 collective-permute-start.21
  137.0 3.4 collective-permute-start.22
  140.4 1.9 collective-permute-start.23
  142.3 1.9 collective-permute-start.24
  144.3 1.9 collective-permute-start.25
  147.9 3.1 collective-permute-done.25
  151.6 1.3 collective-permute-start.26
  153.1 5.0 %collective-permute-done.26 = f32[3,10,2,1]{3,0,2,1:T(4,128)S(1)} collective-permute-done((f32[3,10,2,1]{3,0,2,1:T(4,128)S(1)}, f32[3,10,2,1]{3,0,2,1:T(4,128)S(1)}, u32[]{:S(2)}, u32[]{:S(2)}) %collective-permute-start.26) | collective-permute-done | bytes 272 | tf_op jit(solution)/shard_map/ppermute | solution.py:18
  158.4 2.1 collective-permute-start.27
  164.2 1.6 collective-permute-done.28
  166.0 2.1 collective-permute-start.29
  173.6 2.1 collective-permute-start.31
  177.9 1.5 collective-permute-start.32
  181.5 1.9 collective-permute-start.33
  184.2 3.9 %collective-permute-done.33 = f32[3,1,8,128]{3,0,2,1:T(4,128)S(1)} collective-permute-done((f32[3,1,8,128]{3,0,2,1:T(4,128)S(1)}, f32[3,1,8,128]{3,0,2,1:T(4,128)S(1)}, u32[]{:S(2)}, u32[]{:S(2)}) %collective-permute-start.33) | collective-permute-done | bytes 12320 | tf_op jit(solution)/shard_map/ppermute | solution.py:18
  188.1 3.2 collective-permute-start.34
  194.1 1.3 collective-permute-start.35
  197.6 1.9 collective-permute-start.36
  200.0 2.0 collective-permute-done.36
  203.4 115.8 %all-reduce.92 = (f32[]{:T(128)}, f32[]{:T(128)}) all-reduce(f32[]{:T(128)} %get-tuple-element.19, f32[]{:T(128)} %get-tuple-element.18), channel_id=1, replica_groups=mesh['mirror'=2,'slab'=256] {'mirror','slab'}, use_global_device_ids=true, to_apply=%region_6.7 | all-reduce | flops 2 | bytes 16 | tf_op jit(solution)/shard_map/psum | solution.py:200
  320.6 1.9 collective-permute-start.37
  324.1 3.1 collective-permute-done.37
  327.2 3.7 %collective-permute-start.38 = (f32[3,5,8,1]{3,0,2,1:T(4,128)S(1)}, f32[3,5,8,1]{3,0,2,1:T(4,128)S(1)}, u32[]{:S(2)}, u32[]{:S(2)}) collective-permute-start(f32[3,5,8,1]{3,0,2,1:T(4,128)S(1)} %slice_maximum_fusion), channel_id=1, source_target_pairs={{256,0},{257,1},{258,2},{259,3},{260,4},{261,5},{262,6},{263,7},{2... | collective-permute-start | bytes 1448 | tf_op jit(solution)/shard_map/ppermute | solution.py:18
  333.4 4.1 %psum.23 = f32[4,8,128]{2,1,0:T(8,128)} all-reduce(f32[4,8,128]{2,1,0:T(8,128)S(1)} %broadcast_select_fusion.1), channel_id=1, replica_groups=mesh['mirror'=2,'slab'=256] {'mirror'}, use_global_device_ids=true, to_apply=%region_10.11 | all-reduce | flops 4096 | bytes 32768 | tf_op jit(solution)/shard_map/psum | solution.py:211
  (301 shorter events, 72.0 us)
Async XLA Ops:
  0.6 9.4 %copy-start.10 = (f32[3]{0:T(128)S(1)}, f32[3]{0:T(128)}, u32[]{:S(2)}) copy-start(f32[3]{0:T(128)} %constant.76.clone) | copy-start | bytes 40
  1.8 3.4 %collective-permute-start = (f32[3,5,8,1]{3,0,2,1:T(4,128)S(1)}, f32[3,5,8,1]{3,0,2,1:T(4,128)S(1)}, u32[]{:S(2)}, u32[]{:S(2)}) collective-permute-start(f32[3,5,8,1]{3,0,2,1:T(4,128)S(1)} %broadcast.810), channel_id=1, source_target_pairs={{0,256},{1,257},{2,258},{3,259},{4,260},{5,261},{6,262},{7,263},{8... | collective-permute-start | bytes 1448 | tf_op jit(solution)/shard_map/ppermute | solution.py:18
  5.4 4.5 %collective-permute-start.1 = (f32[3,1,8,128]{3,0,2,1:T(4,128)S(1)}, f32[3,1,8,128]{3,0,2,1:T(4,128)S(1)}, u32[]{:S(2)}, u32[]{:S(2)}) collective-permute-start(f32[3,1,8,128]{3,0,2,1:T(4,128)S(1)} %pad_maximum_fusion.30), channel_id=1, source_target_pairs={{0,1},{1,2},{2,3},{3,4},{4,5},{5,6},{6,7},{7,8},{8,9},{9,10},{10,1... | collective-permute-start | bytes 36872 | tf_op jit(solution)/shard_map/ppermute | solution.py:18
  10.1 13.5 %copy-start.1 = (f32[24,24,1,1]{1,0,3,2:T(8,128)S(1)}, f32[24,24,1,1]{1,0,3,2:T(8,128)}, u32[]{:S(2)}) copy-start(f32[24,24,1,1]{1,0,3,2:T(8,128)} %constant.271) | copy-start | bytes 6916
  10.1 6.7 %collective-permute-start.2 = (f32[3,1,8,128]{3,0,2,1:T(4,128)S(1)}, f32[3,1,8,128]{3,0,2,1:T(4,128)S(1)}, u32[]{:S(2)}, u32[]{:S(2)}) collective-permute-start(f32[3,1,8,128]{3,0,2,1:T(4,128)S(1)} %slice.983), channel_id=1, source_target_pairs={{1,0},{2,1},{3,2},{4,3},{5,4},{6,5},{7,6},{8,7},{9,8},{10,9},{11,1... | collective-permute-start | bytes 36872 | tf_op jit(solution)/shard_map/ppermute | solution.py:18
  16.8 5.8 %collective-permute-start.3 = (f32[3,5,8,1]{3,0,2,1:T(4,128)S(1)}, f32[3,5,8,1]{3,0,2,1:T(4,128)S(1)}, u32[]{:S(2)}, u32[]{:S(2)}) collective-permute-start(f32[3,5,8,1]{3,0,2,1:T(4,128)S(1)} %slice_maximum_fusion.5), channel_id=1, source_target_pairs={{256,0},{257,1},{258,2},{259,3},{260,4},{261,5},{262,6},{263,7},{2... | collective-permute-start | bytes 1448 | tf_op jit(solution)/shard_map/ppermute | solution.py:18
  23.6 2.3 copy-start.11
  24.6 3.2 collective-permute-start.4
  27.8 4.5 %collective-permute-start.5 = (f32[3,1,8,128]{3,0,2,1:T(4,128)S(1)}, f32[3,1,8,128]{3,0,2,1:T(4,128)S(1)}, u32[]{:S(2)}, u32[]{:S(2)}) collective-permute-start(f32[3,1,8,128]{3,0,2,1:T(4,128)S(1)} %pad_maximum_fusion.29), channel_id=1, source_target_pairs={{0,1},{1,2},{2,3},{3,4},{4,5},{5,6},{6,7},{7,8},{8,9},{9,10},{10,1... | collective-permute-start | bytes 36872 | tf_op jit(solution)/shard_map/ppermute | solution.py:18
  32.5 6.7 %collective-permute-start.6 = (f32[3,1,8,128]{3,0,2,1:T(4,128)S(1)}, f32[3,1,8,128]{3,0,2,1:T(4,128)S(1)}, u32[]{:S(2)}, u32[]{:S(2)}) collective-permute-start(f32[3,1,8,128]{3,0,2,1:T(4,128)S(1)} %slice.999), channel_id=1, source_target_pairs={{1,0},{2,1},{3,2},{4,3},{5,4},{6,5},{7,6},{8,7},{9,8},{10,9},{11,1... | collective-permute-start | bytes 36872 | tf_op jit(solution)/shard_map/ppermute | solution.py:18
  39.3 5.6 %collective-permute-start.7 = (f32[3,5,8,1]{3,0,2,1:T(4,128)S(1)}, f32[3,5,8,1]{3,0,2,1:T(4,128)S(1)}, u32[]{:S(2)}, u32[]{:S(2)}) collective-permute-start(f32[3,5,8,1]{3,0,2,1:T(4,128)S(1)} %slice_maximum_fusion.4), channel_id=1, source_target_pairs={{256,0},{257,1},{258,2},{259,3},{260,4},{261,5},{262,6},{263,7},{2... | collective-permute-start | bytes 1448 | tf_op jit(solution)/shard_map/ppermute | solution.py:18
  46.8 3.2 collective-permute-start.8
  50.1 4.5 %collective-permute-start.9 = (f32[3,1,8,128]{3,0,2,1:T(4,128)S(1)}, f32[3,1,8,128]{3,0,2,1:T(4,128)S(1)}, u32[]{:S(2)}, u32[]{:S(2)}) collective-permute-start(f32[3,1,8,128]{3,0,2,1:T(4,128)S(1)} %pad_maximum_fusion.28), channel_id=1, source_target_pairs={{0,1},{1,2},{2,3},{3,4},{4,5},{5,6},{6,7},{7,8},{8,9},{9,10},{10,1... | collective-permute-start | bytes 36872 | tf_op jit(solution)/shard_map/ppermute | solution.py:18
  54.8 6.7 %collective-permute-start.10 = (f32[3,1,8,128]{3,0,2,1:T(4,128)S(1)}, f32[3,1,8,128]{3,0,2,1:T(4,128)S(1)}, u32[]{:S(2)}, u32[]{:S(2)}) collective-permute-start(f32[3,1,8,128]{3,0,2,1:T(4,128)S(1)} %slice.1015), channel_id=1, source_target_pairs={{1,0},{2,1},{3,2},{4,3},{5,4},{6,5},{7,6},{8,7},{9,8},{10,9},{11,1... | collective-permute-start | bytes 36872 | tf_op jit(solution)/shard_map/ppermute | solution.py:18
  61.5 5.3 %collective-permute-start.11 = (f32[3,5,8,1]{3,0,2,1:T(4,128)S(1)}, f32[3,5,8,1]{3,0,2,1:T(4,128)S(1)}, u32[]{:S(2)}, u32[]{:S(2)}) collective-permute-start(f32[3,5,8,1]{3,0,2,1:T(4,128)S(1)} %slice_maximum_fusion.3), channel_id=1, source_target_pairs={{256,0},{257,1},{258,2},{259,3},{260,4},{261,5},{262,6},{263,7},{2... | collective-permute-start | bytes 1448 | tf_op jit(solution)/shard_map/ppermute | solution.py:18
  68.7 3.2 collective-permute-start.12
  72.0 4.5 %collective-permute-start.13 = (f32[3,1,8,128]{3,0,2,1:T(4,128)S(1)}, f32[3,1,8,128]{3,0,2,1:T(4,128)S(1)}, u32[]{:S(2)}, u32[]{:S(2)}) collective-permute-start(f32[3,1,8,128]{3,0,2,1:T(4,128)S(1)} %pad_maximum_fusion.27), channel_id=1, source_target_pairs={{0,1},{1,2},{2,3},{3,4},{4,5},{5,6},{6,7},{7,8},{8,9},{9,10},{10,1... | collective-permute-start | bytes 36872 | tf_op jit(solution)/shard_map/ppermute | solution.py:18
  77.4 15.6 %collective-permute-start.14 = (f32[3,1,8,128]{3,0,2,1:T(4,128)S(1)}, f32[3,1,8,128]{3,0,2,1:T(4,128)S(1)}, u32[]{:S(2)}, u32[]{:S(2)}) collective-permute-start(f32[3,1,8,128]{3,0,2,1:T(4,128)S(1)} %slice.1031), channel_id=1, source_target_pairs={{1,0},{2,1},{3,2},{4,3},{5,4},{6,5},{7,6},{8,7},{9,8},{10,9},{11,1... | collective-permute-start | bytes 36872 | tf_op jit(solution)/shard_map/ppermute | solution.py:18
  93.0 4.1 %collective-permute-start.15 = (f32[3,5,8,1]{3,0,2,1:T(4,128)S(1)}, f32[3,5,8,1]{3,0,2,1:T(4,128)S(1)}, u32[]{:S(2)}, u32[]{:S(2)}) collective-permute-start(f32[3,5,8,1]{3,0,2,1:T(4,128)S(1)} %slice_maximum_fusion.2), channel_id=1, source_target_pairs={{256,0},{257,1},{258,2},{259,3},{260,4},{261,5},{262,6},{263,7},{2... | collective-permute-start | bytes 1448 | tf_op jit(solution)/shard_map/ppermute | solution.py:18
  99.0 6.2 %collective-permute-start.16 = (f32[3,5,8,1]{3,0,2,1:T(4,128)S(1)}, f32[3,5,8,1]{3,0,2,1:T(4,128)S(1)}, u32[]{:S(2)}, u32[]{:S(2)}) collective-permute-start(f32[3,5,8,1]{3,0,2,1:T(4,128)S(1)} %slice.1045), channel_id=1, source_target_pairs={{0,256},{1,257},{2,258},{3,259},{4,260},{5,261},{6,262},{7,263},{8... | collective-permute-start | bytes 1448 | tf_op jit(solution)/shard_map/ppermute | solution.py:18
  105.3 7.6 %collective-permute-start.17 = (f32[3,1,8,128]{3,0,2,1:T(4,128)S(1)}, f32[3,1,8,128]{3,0,2,1:T(4,128)S(1)}, u32[]{:S(2)}, u32[]{:S(2)}) collective-permute-start(f32[3,1,8,128]{3,0,2,1:T(4,128)S(1)} %pad_maximum_fusion.26), channel_id=1, source_target_pairs={{0,1},{1,2},{2,3},{3,4},{4,5},{5,6},{6,7},{7,8},{8,9},{9,10},{10,1... | collective-permute-start | bytes 36872 | tf_op jit(solution)/shard_map/ppermute | solution.py:18
  114.5 25.9 %collective-permute-start.18 = (f32[4,1,2,32]{3,0,2,1:T(4,128)S(1)}, f32[4,1,2,32]{3,0,2,1:T(4,128)S(1)}, u32[]{:S(2)}, u32[]{:S(2)}) collective-permute-start(f32[4,1,2,32]{3,0,2,1:T(4,128)S(1)} %pad_maximum_fusion.31), channel_id=1, source_target_pairs={{0,4},{1,5},{2,6},{3,7},{4,8},{5,9},{6,10},{7,11},{8,12},{9,13},{1... | collective-permute-start | bytes 3080 | tf_op jit(solution)/shard_map/ppermute | solution.py:18
  118.6 43.5 %copy-start.9 = (f32[24,24,1,1]{1,0,3,2:T(8,128)S(1)}, f32[24,24,1,1]{1,0,3,2:T(8,128)}, u32[]{:S(2)}) copy-start(f32[24,24,1,1]{1,0,3,2:T(8,128)} %constant.272) | copy-start | bytes 6916
  118.8 23.5 %collective-permute-start.19 = (f32[4,1,2,32]{3,0,2,1:T(4,128)S(1)}, f32[4,1,2,32]{3,0,2,1:T(4,128)S(1)}, u32[]{:S(2)}, u32[]{:S(2)}) collective-permute-start(f32[4,1,2,32]{3,0,2,1:T(4,128)S(1)} %pad_maximum_fusion.31), channel_id=1, source_target_pairs={{0,3},{1,4},{2,5},{3,6},{4,7},{5,8},{6,9},{7,10},{8,11},{9,12},{10... | collective-permute-start | bytes 3080 | tf_op jit(solution)/shard_map/ppermute | solution.py:18
  124.4 19.9 %collective-permute-start.20 = (f32[4,1,2,32]{3,0,2,1:T(4,128)S(1)}, f32[4,1,2,32]{3,0,2,1:T(4,128)S(1)}, u32[]{:S(2)}, u32[]{:S(2)}) collective-permute-start(f32[4,1,2,32]{3,0,2,1:T(4,128)S(1)} %pad_maximum_fusion.31), channel_id=1, source_target_pairs={{0,2},{1,3},{2,4},{3,5},{4,6},{5,7},{6,8},{7,9},{8,10},{9,11},{10,... | collective-permute-start | bytes 3080 | tf_op jit(solution)/shard_map/ppermute | solution.py:18
  135.1 11.2 %collective-permute-start.21 = (f32[4,1,2,32]{3,0,2,1:T(4,128)S(1)}, f32[4,1,2,32]{3,0,2,1:T(4,128)S(1)}, u32[]{:S(2)}, u32[]{:S(2)}) collective-permute-start(f32[4,1,2,32]{3,0,2,1:T(4,128)S(1)} %pad_maximum_fusion.31), channel_id=1, source_target_pairs={{0,1},{1,2},{2,3},{3,4},{4,5},{5,6},{6,7},{7,8},{8,9},{9,10},{10,1... | collective-permute-start | bytes 3080 | tf_op jit(solution)/shard_map/ppermute | solution.py:18
  137.0 9.3 %collective-permute-start.22 = (f32[4,1,2,32]{3,0,2,1:T(4,128)S(1)}, f32[4,1,2,32]{3,0,2,1:T(4,128)S(1)}, u32[]{:S(2)}, u32[]{:S(2)}) collective-permute-start(f32[4,1,2,32]{3,0,2,1:T(4,128)S(1)} %pad_maximum_fusion.31), channel_id=1, source_target_pairs={{1,0},{2,1},{3,2},{4,3},{5,4},{6,5},{7,6},{8,7},{9,8},{10,9},{11,1... | collective-permute-start | bytes 3080 | tf_op jit(solution)/shard_map/ppermute | solution.py:18
  140.4 6.8 %collective-permute-start.23 = (f32[4,1,2,32]{3,0,2,1:T(4,128)S(1)}, f32[4,1,2,32]{3,0,2,1:T(4,128)S(1)}, u32[]{:S(2)}, u32[]{:S(2)}) collective-permute-start(f32[4,1,2,32]{3,0,2,1:T(4,128)S(1)} %pad_maximum_fusion.31), channel_id=1, source_target_pairs={{2,0},{3,1},{4,2},{5,3},{6,4},{7,5},{8,6},{9,7},{10,8},{11,9},{12,... | collective-permute-start | bytes 3080 | tf_op jit(solution)/shard_map/ppermute | solution.py:18
  142.3 5.6 %collective-permute-start.24 = (f32[4,1,2,32]{3,0,2,1:T(4,128)S(1)}, f32[4,1,2,32]{3,0,2,1:T(4,128)S(1)}, u32[]{:S(2)}, u32[]{:S(2)}) collective-permute-start(f32[4,1,2,32]{3,0,2,1:T(4,128)S(1)} %pad_maximum_fusion.31), channel_id=1, source_target_pairs={{3,0},{4,1},{5,2},{6,3},{7,4},{8,5},{9,6},{10,7},{11,8},{12,9},{13... | collective-permute-start | bytes 3080 | tf_op jit(solution)/shard_map/ppermute | solution.py:18
  144.3 6.8 %collective-permute-start.25 = (f32[4,1,2,32]{3,0,2,1:T(4,128)S(1)}, f32[4,1,2,32]{3,0,2,1:T(4,128)S(1)}, u32[]{:S(2)}, u32[]{:S(2)}) collective-permute-start(f32[4,1,2,32]{3,0,2,1:T(4,128)S(1)} %pad_maximum_fusion.31), channel_id=1, source_target_pairs={{4,0},{5,1},{6,2},{7,3},{8,4},{9,5},{10,6},{11,7},{12,8},{13,9},{1... | collective-permute-start | bytes 3080 | tf_op jit(solution)/shard_map/ppermute | solution.py:18
  151.6 6.5 %collective-permute-start.26 = (f32[3,10,2,1]{3,0,2,1:T(4,128)S(1)}, f32[3,10,2,1]{3,0,2,1:T(4,128)S(1)}, u32[]{:S(2)}, u32[]{:S(2)}) collective-permute-start(f32[3,10,2,1]{3,0,2,1:T(4,128)S(1)} %broadcast.820), channel_id=1, source_target_pairs={{0,256},{1,257},{2,258},{3,259},{4,260},{5,261},{6,262},{7,263},{8... | collective-permute-start | bytes 728 | tf_op jit(solution)/shard_map/ppermute | solution.py:18
  158.4 2.9 collective-permute-start.27
  162.7 3.1 collective-permute-start.28
  166.0 2.9 collective-permute-start.29
  170.3 3.1 collective-permute-start.30
  173.6 2.9 collective-permute-start.31
  177.6 3.8 %copy-start = (f32[3,4,8,128]{3,0,2,1:T(4,128)S(1)}, f32[3,4,8,128]{3,0,2,1:T(4,128)}, u32[]{:S(2)}) copy-start(f32[3,4,8,128]{3,0,2,1:T(4,128)} %get-tuple-element.37) | copy-start | bytes 147460
  177.9 3.1 collective-permute-start.32
  181.5 6.6 %collective-permute-start.33 = (f32[3,1,8,128]{3,0,2,1:T(4,128)S(1)}, f32[3,1,8,128]{3,0,2,1:T(4,128)S(1)}, u32[]{:S(2)}, u32[]{:S(2)}) collective-permute-start(f32[3,1,8,128]{3,0,2,1:T(4,128)S(1)} %slice.1103), channel_id=1, source_target_pairs={{1,0},{2,1},{3,2},{4,3},{5,4},{6,5},{7,6},{8,7},{9,8},{10,9},{11,1... | collective-permute-start | bytes 36872 | tf_op jit(solution)/shard_map/ppermute | solution.py:18
  188.1 4.1 %collective-permute-start.34 = (f32[3,5,8,1]{3,0,2,1:T(4,128)S(1)}, f32[3,5,8,1]{3,0,2,1:T(4,128)S(1)}, u32[]{:S(2)}, u32[]{:S(2)}) collective-permute-start(f32[3,5,8,1]{3,0,2,1:T(4,128)S(1)} %slice_maximum_fusion.1), channel_id=1, source_target_pairs={{256,0},{257,1},{258,2},{259,3},{260,4},{261,5},{262,6},{263,7},{2... | collective-permute-start | bytes 1448 | tf_op jit(solution)/shard_map/ppermute | solution.py:18
  194.1 3.2 collective-permute-start.35
  197.4 4.9 %copy-start.2 = (f32[4,8,32,4]{2,1,3,0:T(8,128)S(1)}, f32[4,8,32,4]{2,1,3,0:T(8,128)}, u32[]{:S(2)}) copy-start(f32[4,8,32,4]{2,1,3,0:T(8,128)} %copy.184) | copy-start | bytes 49156
  197.5 4.9 %copy-start.3 = (f32[4,8,32,4]{2,1,3,0:T(8,128)S(1)}, f32[4,8,32,4]{2,1,3,0:T(8,128)}, u32[]{:S(2)}) copy-start(f32[4,8,32,4]{2,1,3,0:T(8,128)} %copy.192) | copy-start | bytes 49156
  197.5 4.9 %copy-start.4 = (f32[4,8,32,4]{2,1,3,0:T(8,128)S(1)}, f32[4,8,32,4]{2,1,3,0:T(8,128)}, u32[]{:S(2)}) copy-start(f32[4,8,32,4]{2,1,3,0:T(8,128)} %copy.186) | copy-start | bytes 49156
  197.6 4.5 %collective-permute-start.36 = (f32[3,1,8,128]{3,0,2,1:T(4,128)S(1)}, f32[3,1,8,128]{3,0,2,1:T(4,128)S(1)}, u32[]{:S(2)}, u32[]{:S(2)}) collective-permute-start(f32[3,1,8,128]{3,0,2,1:T(4,128)S(1)} %pad_maximum_fusion.25), channel_id=1, source_target_pairs={{0,1},{1,2},{2,3},{3,4},{4,5},{5,6},{6,7},{7,8},{8,9},{9,10},{10,1... | collective-permute-start | bytes 36872 | tf_op jit(solution)/shard_map/ppermute | solution.py:18
  320.6 6.6 %collective-permute-start.37 = (f32[3,1,8,128]{3,0,2,1:T(4,128)S(1)}, f32[3,1,8,128]{3,0,2,1:T(4,128)S(1)}, u32[]{:S(2)}, u32[]{:S(2)}) collective-permute-start(f32[3,1,8,128]{3,0,2,1:T(4,128)S(1)} %slice.1119), channel_id=1, source_target_pairs={{1,0},{2,1},{3,2},{4,3},{5,4},{6,5},{7,6},{8,7},{9,8},{10,9},{11,1... | collective-permute-start | bytes 36872 | tf_op jit(solution)/shard_map/ppermute | solution.py:18
  327.2 4.7 %collective-permute-start.38 = (f32[3,5,8,1]{3,0,2,1:T(4,128)S(1)}, f32[3,5,8,1]{3,0,2,1:T(4,128)S(1)}, u32[]{:S(2)}, u32[]{:S(2)}) collective-permute-start(f32[3,5,8,1]{3,0,2,1:T(4,128)S(1)} %slice_maximum_fusion), channel_id=1, source_target_pairs={{256,0},{257,1},{258,2},{259,3},{260,4},{261,5},{262,6},{263,7},{2... | collective-permute-start | bytes 1448 | tf_op jit(solution)/shard_map/ppermute | solution.py:18
  331.0 2.3 copy-start.8
  (3 other events, 3.7 us)
where the time goes:
time: 339 us; the launch traced here: 338 us
  blocking collectives  120 us (35%)
  starting transfers between devices  108 us (32%)
  waiting for transfers between devices  51.8 us (15%)
  local copies, waits for them, and re-layouts  34.9 us (10%)
  other arithmetic  11.4 us (3%)
  between operations  7.57 us (2%)
  matrix products  3.75 us (1%)
    psum x1, blocking collectives, on_device(): residual_dot = lax.psum(jnp.sum(right * precond), ('mirror', 'slab'))  116 us
    ppermute x39, starting transfers between devices, passed_along(): return lax.ppermute(array, axis, pairs)  108 us
    ppermute x39, waiting for transfers between devices, passed_along(): return lax.ppermute(array, axis, pairs)  51.8 us
    concatenate x30, local copies, waits for them, and re-layouts, gather_forces(): owned = jnp.concatenate([owned[:, :1] + arriving, owned[:, 1:]], axis=1)  13.2 us
  transfers between devices with their start and end apart: 39, of which 31 were waited for; matrix products, arithmetic and copies ran while one was open for 8% of the time, Pallas kernels for 0%

commit v1 on v0

v1 whole, which is shorter than its diff:
```python
import functools

import jax
import jax.numpy as jnp
import numpy as np
from jax import lax
from jax.experimental import pallas as pl
from jax.experimental.pallas import tpu as pltpu
from jax.sharding import Mesh
from jax.sharding import PartitionSpec as P

SWEEPS = 4
MODULUS_FLOOR = 0.001
EIG_LOWER = 0.05
EIG_UPPER = 1.0
CENTRE = 0.5 * (EIG_UPPER + EIG_LOWER)
HALF_WIDTH = 0.5 * (EIG_UPPER - EIG_LOWER)
DIRECTION = (0.4, -0.3, -1.0)
SLAB = ("y", "z", "x")
ROWS = 8
COLS = 256
OWN = 4


def element_matrix():
    poisson = 0.3
    lame_first = poisson / ((1.0 + poisson) * (1.0 - 2.0 * poisson))
    shear_modulus = 0.5 / (1.0 + poisson)
    elastic = np.zeros((6, 6))
    elastic[:3, :3] = lame_first
    for i in range(3):
        elastic[i, i] += 2.0 * shear_modulus
        elastic[i + 3, i + 3] = shear_modulus
    points = [0.5 - 0.5 / np.sqrt(3.0), 0.5 + 0.5 / np.sqrt(3.0)]
    stiffness = np.zeros((24, 24))
    for p in points:
        for q in points:
            for s in points:
                strain = np.zeros((6, 24))
                for corner in range(8):
                    z_bit, y_bit, x_bit = (corner // 4, corner // 2 % 2, corner % 2)
                    weight_z = p if z_bit else 1.0 - p
                    weight_y = q if y_bit else 1.0 - q
                    weight_x = s if x_bit else 1.0 - s
                    slope_z = 1.0 if z_bit else -1.0
                    slope_y = 1.0 if y_bit else -1.0
                    slope_x = 1.0 if x_bit else -1.0
                    grad_x = slope_x * weight_y * weight_z
                    grad_y = weight_x * slope_y * weight_z
                    grad_z = weight_x * weight_y * slope_z
                    c = 3 * corner
                    strain[0, c] = grad_x
                    strain[1, c + 1] = grad_y
                    strain[2, c + 2] = grad_z
                    strain[3, c] = grad_y
                    strain[3, c + 1] = grad_x
                    strain[4, c + 1] = grad_z
                    strain[4, c + 2] = grad_y
                    strain[5, c] = grad_z
                    strain[5, c + 2] = grad_x
                stiffness += strain.T @ elastic @ strain / 8.0
    return stiffness


@functools.lru_cache(None)
def mode_matrix():
    one = np.array([[1.0, 1.0], [-1.0, 1.0]])
    signs = np.kron(np.kron(one, one), one)
    spread = np.kron(signs, np.eye(3)) / 8.0
    matrix = spread @ element_matrix() @ spread.T
    table = {}
    for row in range(24):
        entries = [
            ((col // 3, col % 3), float(matrix[row, col]))
            for col in range(24)
            if abs(matrix[row, col]) > 1e-12
        ]
        if entries:
            table[(row // 3, row % 3)] = entries
    return table


@functools.lru_cache(None)
def row_total():
    totals = np.abs(element_matrix()).sum(axis=1)
    assert np.allclose(totals, totals[0], rtol=1e-12)
    return float(totals[0])


def chebyshev_factors():
    ratio = CENTRE / HALF_WIDTH
    rho = 1.0 / ratio
    factors = []
    for _ in range(1, SWEEPS):
        rho_next = 1.0 / (2.0 * ratio - rho)
        factors.append((rho_next * rho, 2.0 * rho_next / HALF_WIDTH))
        rho = rho_next
    return factors


class Plane:
    def __init__(self, step):
        lane = lax.broadcasted_iota(jnp.int32, (ROWS, COLS), 1)
        row = lax.broadcasted_iota(jnp.int32, (ROWS, COLS), 0)
        self.step = step
        self.lane_not_last = lane < COLS - step
        self.lane_not_first = lane >= step
        self.row_not_last = row < ROWS - step
        self.row_not_first = row >= step

    def next_x(self, v):
        return jnp.where(self.lane_not_last, pltpu.roll(v, COLS - self.step, 1), 0.0)

    def prev_x(self, v):
        return jnp.where(self.lane_not_first, pltpu.roll(v, self.step, 1), 0.0)

    def next_y(self, v):
        return jnp.where(self.row_not_last, pltpu.roll(v, ROWS - self.step, 0), 0.0)

    def prev_y(self, v):
        return jnp.where(self.row_not_first, pltpu.roll(v, self.step, 0), 0.0)

    def corner_sum(self, v):
        v = v + self.prev_x(v)
        return v + self.prev_y(v)

    def forward(self, comps):
        modes = [[None] * 3 for _ in range(4)]
        for c, v in enumerate(comps):
            ahead = self.next_x(v)
            for x_bit, w in enumerate((ahead + v, ahead - v)):
                above = self.next_y(w)
                modes[x_bit][c] = above + w
                modes[2 + x_bit][c] = above - w
        return modes

    def backward(self, modes):
        comps = []
        for c in range(3):
            along = []
            for x_bit in range(2):
                total, change = modes[x_bit][c], modes[2 + x_bit][c]
                along.append((total - change) + self.prev_y(total + change))
            comps.append((along[0] - along[1]) + self.prev_x(along[0] + along[1]))
        return comps

    def element(self, low, high, modulus, scale, with_energy=False):
        modes = {}
        for m in range(4):
            for c in range(3):
                if m > 0:
                    modes[(m, c)] = high[m][c] + low[m][c]
                modes[(4 + m, c)] = high[m][c] - low[m][c]
        forces = {}
        for row, entries in mode_matrix().items():
            total = None
            for col, entry in entries:
                term = modes[col] * np.float32(entry * scale)
                total = term if total is None else total + term
            forces[row] = total
        energy = None
        if with_energy:
            for row, force in forces.items():
                term = modes[row] * force
                energy = term if energy is None else energy + term
        on_low = [[None] * 3 for _ in range(4)]
        on_high = [[None] * 3 for _ in range(4)]
        for m in range(4):
            for c in range(3):
                change = modulus * forces[(4 + m, c)]
                if m > 0:
                    total = modulus * forces[(m, c)]
                    on_low[m][c] = total - change
                    on_high[m][c] = total + change
                else:
                    on_low[m][c] = -change
                    on_high[m][c] = change
        return on_low, on_high, energy


def apply_planes(plane, first, last, load, modulus_at, scale, consume, with_energy=False):
    def flat(modes):
        return tuple(v for mode in modes for v in mode)

    def nested(values):
        return [[values[3 * m + c] for c in range(3)] for m in range(4)]

    def body(p, carry):
        low, pending = nested(carry[:12]), nested(carry[12:])
        high = plane.forward(load(p + 1))
        on_low, on_high, energy = plane.element(low, high, modulus_at(p), scale, with_energy)
        total = [[pending[m][c] + on_low[m][c] for c in range(3)] for m in range(4)]
        consume(p, plane.backward(total), energy)
        return flat(high) + flat(on_high)

    start = flat(plane.forward(load(first - 1)))
    zeros = tuple(jnp.zeros((ROWS, COLS), jnp.float32) for _ in range(12))
    lax.fori_loop(first - 1, last + 1, body, start + zeros)


class Groups:
    def __init__(self):
        lane = lax.broadcasted_iota(jnp.int32, (ROWS, COLS), 1)
        row = lax.broadcasted_iota(jnp.int32, (ROWS, COLS), 0)
        self.lane_in, self.row_in = lane % 4, row % 4
        self.lane_bits = [lane % 2 == 1, lane // 2 % 2 == 1]
        self.row_bits = [row % 2 == 1, row // 2 % 2 == 1]

    def over_rows(self, v):
        for bit in range(2):
            by = 1 << bit
            v = v + jnp.where(self.row_bits[bit], pltpu.roll(v, by, 0), pltpu.roll(v, ROWS - by, 0))
        return v

    def over_lanes(self, v):
        for bit in range(2):
            by = 1 << bit
            v = v + jnp.where(self.lane_bits[bit], pltpu.roll(v, by, 1), pltpu.roll(v, COLS - by, 1))
        return v

    def both(self, v):
        return self.over_lanes(self.over_rows(v))


def modulus_of(density):
    return MODULUS_FLOOR + density * density * density * (1.0 - MODULUS_FLOOR)


def smooth_kernel(slabs, info, own, below, above, edge, smooth, coarse, mod, x, d, w, right, free, left):
    plane, groups = Plane(1), Groups()
    slab, sweep_count = info[0], info[2]
    has_below = (slab > 0).astype(jnp.float32)
    has_edge = (slab > 1).astype(jnp.float32)
    has_above = (slab < slabs - 1).astype(jnp.float32)

    mod[0] = modulus_of(edge[0]) * has_edge
    for source, at, inside in ((below, 0, has_below), (own, 4, None), (above, 8, has_above)):
        for k in range(OWN):
            value = modulus_of(source[0, k])
            mod[1 + at + k] = value if inside is None else value * inside
            open_node = 1.0 - source[2, k]
            free[at + k] = open_node if inside is None else open_node * inside

    def prepare(q, carry):
        summed = plane.corner_sum(mod[q + 1])
        scaling = np.float32(row_total()) * (carry + summed)
        f = free[q]
        scaling = jnp.where(f > 0.0, scaling, 1.0)
        inverse = 1.0 / scaling
        w[q] = inverse
        return summed

    lax.fori_loop(0, 12, prepare, plane.corner_sum(mod[0]))
    for source, at in ((below, 0), (own, 4), (above, 8)):
        for k in range(OWN):
            loaded = free[at + k] * source[1, k]
            start = loaded * (w[at + k] * np.float32(1.0 / CENTRE))
            right[at + k] = loaded
            for c in range(3):
                x[c, at + k] = start * np.float32(DIRECTION[c])
                d[c, at + k] = start * np.float32(DIRECTION[c])

    def load(q):
        f = free[q]
        return [f * x[c, q] for c in range(3)]

    def modulus_at(q):
        return mod[q + 1]

    for k, (keep, add) in enumerate(chebyshev_factors(), 1):

        @pl.when(k < sweep_count)
        def _(k=k, keep=keep, add=add):
            def consume(q, forces, _energy):
                f, weight = free[q], w[q] * np.float32(add)
                is_free = f > 0.0
                loaded = right[q]
                for c in range(3):
                    now = x[c, q]
                    image = jnp.where(is_free, forces[c], now)
                    defect = loaded * np.float32(DIRECTION[c]) - image
                    update = np.float32(keep) * d[c, q] + weight * defect
                    d[c, q] = update
                    x[c, q] = now + update

            apply_planes(plane, k, 11 - k, load, modulus_at, 1.0, consume)

    def consume_left(q, forces, _energy):
        is_free = free[q] > 0.0
        for c in range(3):
            image = jnp.where(is_free, forces[c], x[c, q])
            left[c, q - 3] = right[q] * np.float32(DIRECTION[c]) - image

    apply_planes(plane, 4, 7, load, modulus_at, 1.0, consume_left)

    for c in range(3):
        for k in range(6):
            smooth[c, k] = x[c, k + 3]
    fields = [groups.both((left[c, 1] + left[c, 2]) + (left[c, 3] + left[c, 4])) for c in range(3)]
    here = groups.both((mod[5] + mod[6]) + (mod[7] + mod[8])) * np.float32(1.0 / 64.0)
    under = groups.both((mod[1] + mod[2]) + (mod[3] + mod[4])) * np.float32(1.0 / 64.0)
    packed = jnp.where(groups.lane_in == 0, here, under)
    for c in range(3):
        packed = jnp.where(groups.row_in == c, fields[c], packed)
    coarse[...] = packed


def correct_kernel(
    slabs, info, own, below, above, smooth, gathered, moved, image, slope, sums, window, mod, x, d, w, target, p, free, img, energy
):
    coarse_plane, plane, groups = Plane(4), Plane(1), Groups()
    slab, mirror, sweep_count = info[0], info[1], info[3]
    offset = slab % 4
    for k in range(4):
        window[k] = gathered[k, ROWS : 2 * ROWS]
        window[4 + k] = gathered[k, :ROWS]
        window[8 + k] = gathered[4 + k, ROWS : 2 * ROWS]

    is_here = (groups.row_in == 3) & (groups.lane_in == 0)
    is_under = (groups.row_in == 3) & (groups.lane_in == 1)

    def unpack(q, carry):
        packed = window[offset + q]
        for c in range(3):
            target[c, q] = groups.over_rows(jnp.where(groups.row_in == c, packed, 0.0))
        mod[q + 1] = groups.both(jnp.where(is_here, packed, 0.0))
        return carry

    lax.fori_loop(0, 9, unpack, 0)
    mod[0] = groups.both(jnp.where(is_under, window[offset], 0.0))

    def prepare(q, carry):
        summed = coarse_plane.corner_sum(mod[q + 1])
        scaling = np.float32(4.0 * row_total()) * (carry + summed)
        at = slab - 4 + q
        inside = ((at >= 0) & (at < slabs)).astype(jnp.float32)
        inverse = inside / jnp.where(scaling > 0.0, scaling, 1.0)
        w[q] = inverse
        for c in range(3):
            start = target[c, q] * (inverse * np.float32(1.0 / CENTRE))
            x[c, q] = start
            d[c, q] = start
        return summed

    lax.fori_loop(0, 9, prepare, coarse_plane.corner_sum(mod[0]))

    for k, (keep, add) in enumerate(chebyshev_factors(), 1):

        @pl.when(k < sweep_count)
        def _(k=k, keep=keep, add=add):
            def consume(q, forces, _energy):
                weight = w[q] * np.float32(add)
                for c in range(3):
                    update = np.float32(keep) * d[c, q] + weight * (target[c, q] - forces[c])
                    d[c, q] = update
                    x[c, q] = x[c, q] + update

            apply_planes(
                coarse_plane,
                k,
                8 - k,
                lambda q: [x[c, q] for c in range(3)],
                lambda q: mod[q + 1],
                4.0,
                consume,
            )

    has_below = (slab > 0).astype(jnp.float32)
    has_above = (slab < slabs - 1).astype(jnp.float32)
    for k in range(6):
        source, at, inside, coarse = (
            (below, 3, has_below, 3) if k == 0 else (above, 0, has_above, 5) if k == 5 else (own, k - 1, None, 4)
        )
        open_node = 1.0 - source[2, at]
        if inside is not None:
            open_node = open_node * inside
        free[k] = open_node
        for c in range(3):
            p[c, k] = smooth[c, k] + open_node * x[c, coarse]
        if k < 5:
            value = modulus_of(source[0, at])
            mod[k] = value if inside is None else value * inside

    def consume_image(q, forces, strain):
        is_free = free[q] > 0.0
        for c in range(3):
            img[c, q] = jnp.where(is_free, forces[c], p[c, q])
        energy[q] = strain

    def load_p(q):
        f = free[q]
        return [f * p[c, q] for c in range(3)]

    apply_planes(plane, 1, 4, load_p, lambda q: mod[q], 1.0, consume_image, True)

    first = jnp.zeros((ROWS, COLS), jnp.float32)
    second = jnp.zeros((ROWS, COLS), jnp.float32)
    half = pl.ds(pl.multiple_of(mirror * 128, 128), 128)
    for k in range(OWN):
        loaded = free[k + 1] * own[1, k]
        for c in range(3):
            first = first + (loaded * np.float32(DIRECTION[c])) * p[c, k + 1]
            second = second + p[c, k + 1] * img[c, k + 1]
            moved[c, k] = p[c, k + 1, :, half]
            image[c, k] = img[c, k + 1, :, half]
        density = own[0, k]
        energy[k + 1] = np.float32(-3.0 * (1.0 - MODULUS_FLOOR)) * (density * density) * energy[k + 1]
    flip = (
        lax.broadcasted_iota(jnp.int32, (128, 128), 0) + lax.broadcasted_iota(jnp.int32, (128, 128), 1) == 127
    ).astype(jnp.float32)
    second_half = jnp.concatenate([energy[k + 1, :, 128:] for k in range(OWN)], axis=0)
    turned = jnp.dot(second_half, flip, precision=lax.Precision.HIGHEST, preferred_element_type=jnp.float32)
    for k in range(OWN):
        slope[k] = energy[k + 1, :, :128] + turned[ROWS * k : ROWS * (k + 1)]
    lane = lax.broadcasted_iota(jnp.int32, (1, 128), 1)
    dots = jnp.where(lane == 0, jnp.sum(first), jnp.where(lane == 1, jnp.sum(second), 0.0))
    for k in range(sums.shape[0]):
        sums[k] = dots


def scale_kernel(totals, load, fixed, moved, image, slope, displacement, residual, sensitivity):
    total = totals[0]
    for k in range(1, totals.shape[0]):
        total = total + totals[k]
    lane = lax.broadcasted_iota(jnp.int32, (1, 128), 1)
    residual_dot = jnp.sum(jnp.where(lane == 0, total, 0.0), axis=1, keepdims=True)
    curvature = jnp.sum(jnp.where(lane == 1, total, 0.0), axis=1, keepdims=True)
    alpha = jnp.broadcast_to(residual_dot / curvature, (ROWS, 128))
    for k in range(OWN):
        loaded = ((1 - fixed[0, k]) * load[0, k]).astype(jnp.float32)
        for c in range(3):
            displacement[c, k] = alpha * moved[c, k]
            residual[c, k] = loaded * np.float32(DIRECTION[c]) - alpha * image[c, k]
        sensitivity[k] = alpha * (alpha * slope[k])


def call(kernel, outs, ins, scratch=()):
    vmem = pl.BlockSpec(memory_space=pltpu.VMEM)
    smem = pl.BlockSpec(memory_space=pltpu.SMEM)
    return pl.pallas_call(
        kernel,
        out_shape=[jax.ShapeDtypeStruct(shape, jnp.float32) for shape in outs],
        in_specs=[smem if v.ndim == 1 else vmem for v in ins],
        out_specs=[vmem] * len(outs),
        scratch_shapes=[pltpu.VMEM(shape, jnp.float32) for shape in scratch],
        compiler_params=pltpu.CompilerParams(vmem_limit_bytes=16 * 1024 * 1024),
    )(*ins)


def shifted(array, axis, by):
    length = lax.axis_size(axis)
    pairs = [(i, i + by) for i in range(length) if 0 <= i + by < length]
    return lax.ppermute(array, axis, pairs)


def on_device(density, load_mask, fixed_mask, sweeps):
    slabs = lax.axis_size(SLAB)
    slab, mirror = lax.axis_index(SLAB), lax.axis_index("mirror")
    info = jnp.concatenate([jnp.stack([slab, mirror]).astype(jnp.int32), sweeps])
    plane = (ROWS, COLS)

    masks = lax.all_gather(jnp.concatenate([load_mask, fixed_mask], axis=0), "mirror")
    masks = jnp.concatenate([masks[0], masks[1]], axis=-1).astype(jnp.float32)
    wide = jnp.concatenate([density, density[..., ::-1]], axis=-1)
    own = jnp.concatenate([wide[None], masks], axis=0)
    below = shifted(own, SLAB, 1)
    above = shifted(own, SLAB, -1)
    edge = shifted(wide[OWN - 1 :], SLAB, 2)

    field = (3, 12) + plane
    smooth, coarse = call(
        functools.partial(smooth_kernel, slabs),
        [(3, 6) + plane, plane],
        [info, own, below, above, edge],
        [(13,) + plane, field, field, (12,) + plane, (12,) + plane, (12,) + plane, (3, 5) + plane],
    )

    reach = 4
    pairs = [(i, i + reach) for i in range(slabs - reach)]
    pairs += [(slabs + i + reach, slabs + i) for i in range(slabs - reach)]
    arrived = lax.ppermute(coarse, ("mirror",) + SLAB, pairs)
    sent = jnp.broadcast_to(jnp.concatenate([coarse, arrived], axis=0), (8, 2 * ROWS, COLS))
    gathered = lax.all_to_all(sent, ("mirror", "x"), 0, 0)

    coarse_field = (3, 9) + plane
    group = lax.axis_size(("y", "x"))
    part = (3, OWN, ROWS, 128)
    moved, image, slope, sums = call(
        functools.partial(correct_kernel, slabs),
        [part, part, part[1:], (group, 1, 128)],
        [info, own, below, above, smooth, gathered],
        [
            (12,) + plane,
            (10,) + plane,
            coarse_field,
            coarse_field,
            (9,) + plane,
            coarse_field,
            (3, 6) + plane,
            (6,) + plane,
            (3, 5) + plane,
            (5,) + plane,
        ],
    )
    sums = lax.all_to_all(sums, ("y", "x"), 0, 0)
    length = lax.axis_size("z")
    sums = jnp.broadcast_to(jnp.sum(sums, axis=0), (length, 1, 128))
    sums = lax.all_to_all(sums, "z", 0, 0)
    displacement, residual, sensitivity = call(
        scale_kernel, [part, part, part[1:]], [sums, load_mask, fixed_mask, moved, image, slope]
    )
    return displacement[None], residual[None], sensitivity


def solution(mesh):
    slabs = mesh.shape["slab"]
    ways = 4
    deep = min(16, slabs // ways)
    split = Mesh(mesh.devices.reshape(2, slabs // (ways * deep), deep, ways), ("mirror",) + SLAB)
    return jax.shard_map(
        on_device,
        mesh=split,
        in_specs=(
            P(SLAB, None, None),
            P("mirror", SLAB, None, None),
            P("mirror", SLAB, None, None),
            P(),
        ),
        out_specs=(
            P("mirror", None, SLAB, None, None),
            P("mirror", None, SLAB, None, None),
            P(SLAB, None, None),
        ),
        check_vma=False,
    )
```

time: 339 us -> 89.8 us (0.26)
  the two profiles are of different devices: /device:TPU:39 before, /device:TPU:2 now
where the time goes in v1:
time: 89.8 us; the launch traced here: 89.2 us
  blocking collectives  53.6 us (60%)
  starting transfers between devices  15.2 us (17%)
  Pallas kernels  14.2 us (16%)
  waiting for transfers between devices  3.01 us (3%)
  local copies, waits for them, and re-layouts  2.26 us (3%)
    all_to_all x1, blocking collectives, on_device(): sums = lax.all_to_all(sums, ('y', 'x'), 0, 0)  24.3 us
    all_to_all x1, blocking collectives, on_device(): sums = lax.all_to_all(sums, 'z', 0, 0)  17.4 us
    pallas_call x3, Pallas kernels, call(): pl.pallas_call(kernel, out_shape=[jax.ShapeDtypeStruct(shape, jnp.float32...  14.2 us
    ppermute x3, starting transfers between devices, shifted(): return lax.ppermute(array, axis, pairs)  12 us
    all_to_all x1, blocking collectives, on_device(): gathered = lax.all_to_all(sent, ('mirror', 'x'), 0, 0)  10.1 us
    ppermute x1, starting transfers between devices, on_device(): arrived = lax.ppermute(coarse, ('mirror',) + SLAB, pairs)  3.22 us
    all_gather x1, blocking collectives, on_device(): lax.all_gather(jnp.concatenate([load_mask, fixed_mask], axis=0), 'mirror')  1.84 us
  transfers between devices with their start and end apart: 4, of which 3 were waited for; matrix products, arithmetic and copies ran while one was open for 0% of the time, Pallas kernels for 0%

profile of v1, /device:TPU:2, one launch (start us, length us, event | category | flops | bytes accessed | tf_op | source)
XLA Modules:
  0.0 89.2 jit_solution(9704171272004694658)
XLA Ops:
  0.6 0.0 copy-start.2
  0.6 0.9 rev.3
  1.5 0.0 copy-done.2
  1.5 0.0 copy-start
  1.5 0.0 copy-start.1
  1.5 0.7 copy-done
  2.2 0.0 copy-done.1
  2.2 1.8 %all-gather = s32[4,4,8,128]{3,2,1,0:T(8,128)S(1)} all-gather(s32[2,4,8,128]{3,2,1,0:T(8,128)S(1)} %pad_add_fusion), channel_id=2, replica_groups=mesh['mirror'=2,'y'=4,'z'=16,'x'=4] {'mirror'}, dimensions={0}, use_global_device_ids=true | all-gather | bytes 98304 | tf_op jit(solution)/shard_map/all_gather | solution.py:462
  4.1 7.8 %collective-permute-start.1 = (f32[3,4,8,256]{3,2,1,0:T(8,128)S(1)}, f32[3,4,8,256]{3,2,1,0:T(8,128)S(1)}, u32[]{:S(2)}, u32[]{:S(2)}) collective-permute-start(f32[3,4,8,256]{3,2,1,0:T(8,128)S(1)} %pad_maximum_fusion.own), channel_id=1, source_target_pairs={{1,0},{2,1},{3,2},{4,3},{5,4},{6,5},{7,6},{8,7},{9,8},{10,9},{11,1... | collective-permute-start | bytes 294920 | tf_op jit(solution)/shard_map/ppermute | solution.py:453
  11.9 1.9 %collective-permute-start = (f32[3,4,8,256]{3,2,1,0:T(8,128)S(1)}, f32[3,4,8,256]{3,2,1,0:T(8,128)S(1)}, u32[]{:S(2)}, u32[]{:S(2)}) collective-permute-start(f32[3,4,8,256]{3,2,1,0:T(8,128)S(1)} %pad_maximum_fusion.own), channel_id=1, source_target_pairs={{0,1},{1,2},{2,3},{3,4},{4,5},{5,6},{6,7},{7,8},{8,9},{9,10},{10,1... | collective-permute-start | bytes 294920 | tf_op jit(solution)/shard_map/ppermute | solution.py:453
  13.9 2.2 %collective-permute-start.2 = (f32[1,8,256]{2,1,0:T(8,128)S(1)}, f32[1,8,256]{2,1,0:T(8,128)S(1)}, u32[]{:S(2)}, u32[]{:S(2)}) collective-permute-start(f32[1,8,256]{2,1,0:T(8,128)S(1)} %fusion.1), channel_id=1, source_target_pairs={{0,2},{1,3},{2,4},{3,5},{4,6},{5,7},{6,8},{7,9},{8,10},{9,11},{10,... | collective-permute-start | bytes 24584 | tf_op jit(solution)/shard_map/ppermute | solution.py:453
  16.1 0.0 copy-start.3
  16.1 0.6 copy-done.3
  16.8 0.1 pad_add_fusion.1.info
  16.9 0.6 collective-permute-done.2.edge
  17.5 0.0 collective-permute-done.1.above
  17.5 1.1 %collective-permute-done.below = f32[3,4,8,256]{3,2,1,0:T(8,128)S(1)} collective-permute-done((f32[3,4,8,256]{3,2,1,0:T(8,128)S(1)}, f32[3,4,8,256]{3,2,1,0:T(8,128)S(1)}, u32[]{:S(2)}, u32[]{:S(2)}) %collective-permute-start) | collective-permute-done | bytes 98336 | tf_op jit(solution)/shard_map/ppermute | solution.py:453
  18.5 5.3 %shard_map.67 = (f32[3,6,8,256]{3,2,1,0:T(8,128)S(1)}, f32[8,256]{1,0:T(8,128)S(1)}) custom-call(s32[4]{0:T(128)S(1)} %pad_add_fusion.1.info, f32[3,4,8,256]{3,2,1,0:T(8,128)S(1)} %pad_maximum_fusion.own, f32[3,4,8,256]{3,2,1,0:T(8,128)S(1)} %collective-permute-done.below, f32[3,4,8,256]{3,2,1,0:T(8,128)S(1)} %collective-permute-done.1.above, ...), custom_call_target="tpu_custom_call" | custom-call | tf_op jit(solution)/shard_map/pallas_call | solution.py:440
  23.8 3.2 %collective-permute-start.3 = (f32[8,256]{1,0:T(8,128)S(1)}, f32[8,256]{1,0:T(8,128)S(1)}, u32[]{:S(2)}, u32[]{:S(2)}) collective-permute-start(f32[8,256]{1,0:T(8,128)S(1)} %get-tuple-element.13), channel_id=1, source_target_pairs={{0,4},{1,5},{2,6},{3,7},{4,8},{5,9},{6,10},{7,11},{8,12},{9,13},{1... | collective-permute-start | bytes 24584 | tf_op jit(solution)/shard_map/ppermute | solution.py:481
  27.1 1.3 %collective-permute-done.3 = f32[8,256]{1,0:T(8,128)S(1)} collective-permute-done((f32[8,256]{1,0:T(8,128)S(1)}, f32[8,256]{1,0:T(8,128)S(1)}, u32[]{:S(2)}, u32[]{:S(2)}) %collective-permute-start.3) | collective-permute-done | bytes 8224 | tf_op jit(solution)/shard_map/ppermute | solution.py:481
  28.4 10.1 %all_to_all.15.gathered = f32[8,16,256]{2,1,0:T(8,128)S(1)} all-to-all(f32[8,16,256]{2,1,0:T(8,128)S(1)} %broadcast_in_dim.16), channel_id=1, replica_groups=mesh['mirror'=2,'y'=4,'z'=16,'x'=4] {'mirror','x'}, dimensions={0} | all-to-all | bytes 262144 | tf_op jit(solution)/shard_map/all_to_all | solution.py:483
  38.5 8.2 %shard_map.68 = (f32[3,4,8,128]{3,2,1,0:T(8,128)S(1)}, f32[3,4,8,128]{3,2,1,0:T(8,128)S(1)}, f32[4,8,128]{2,1,0:T(8,128)S(1)}, f32[16,1,128]{2,1,0:T(1,128)S(1)}) custom-call(s32[4]{0:T(128)S(1)} %pad_add_fusion.1.info, f32[3,4,8,256]{3,2,1,0:T(8,128)S(1)} %pad_maximum_fusion.own, f32[3,4,8,256]{3,2,1,0:T(8,128)S(1)} %collective-permute-done.below, ...), custom_call_target="tpu_custom_call" | custom-call | tf_op jit(solution)/shard_map/pallas_call | solution.py:440
  46.7 24.3 %all_to_all.16 = f32[16,1,128]{2,1,0:T(1,128)S(1)} all-to-all(f32[16,1,128]{2,1,0:T(1,128)S(1)} %get-tuple-element.14), channel_id=1, replica_groups=mesh['mirror'=2,'y'=4,'z'=16,'x'=4] {'y','x'}, dimensions={0} | all-to-all | bytes 16384 | tf_op jit(solution)/shard_map/all_to_all | solution.py:505
  71.1 17.4 %all_to_all.17.totals = f32[16,1,128]{2,1,0:T(1,128)S(1)} all-to-all(f32[16,1,128]{2,1,0:T(1,128)S(1)} %broadcast_in_dim.17), channel_id=1, replica_groups=mesh['mirror'=2,'y'=4,'z'=16,'x'=4] {'z'}, dimensions={0} | all-to-all | bytes 16384 | tf_op jit(solution)/shard_map/all_to_all | solution.py:508
  88.5 0.7 shard_map.69
  (10 shorter events, 0.1 us)
Async XLA Ops:
  0.6 0.9 copy-start.2
  1.5 0.7 copy-start
  1.5 0.7 copy-start.1
  4.1 13.4 %collective-permute-start.1 = (f32[3,4,8,256]{3,2,1,0:T(8,128)S(1)}, f32[3,4,8,256]{3,2,1,0:T(8,128)S(1)}, u32[]{:S(2)}, u32[]{:S(2)}) collective-permute-start(f32[3,4,8,256]{3,2,1,0:T(8,128)S(1)} %pad_maximum_fusion.own), channel_id=1, source_target_pairs={{1,0},{2,1},{3,2},{4,3},{5,4},{6,5},{7,6},{8,7},{9,8},{10,9},{11,1... | collective-permute-start | bytes 294920 | tf_op jit(solution)/shard_map/ppermute | solution.py:453
  11.9 6.6 %collective-permute-start = (f32[3,4,8,256]{3,2,1,0:T(8,128)S(1)}, f32[3,4,8,256]{3,2,1,0:T(8,128)S(1)}, u32[]{:S(2)}, u32[]{:S(2)}) collective-permute-start(f32[3,4,8,256]{3,2,1,0:T(8,128)S(1)} %pad_maximum_fusion.own), channel_id=1, source_target_pairs={{0,1},{1,2},{2,3},{3,4},{4,5},{5,6},{6,7},{7,8},{8,9},{9,10},{10,1... | collective-permute-start | bytes 294920 | tf_op jit(solution)/shard_map/ppermute | solution.py:453
  13.9 3.6 %collective-permute-start.2 = (f32[1,8,256]{2,1,0:T(8,128)S(1)}, f32[1,8,256]{2,1,0:T(8,128)S(1)}, u32[]{:S(2)}, u32[]{:S(2)}) collective-permute-start(f32[1,8,256]{2,1,0:T(8,128)S(1)} %fusion.1), channel_id=1, source_target_pairs={{0,2},{1,3},{2,4},{3,5},{4,6},{5,7},{6,8},{7,9},{8,10},{9,11},{10,... | collective-permute-start | bytes 24584 | tf_op jit(solution)/shard_map/ppermute | solution.py:453
  16.1 0.7 copy-start.3
  23.8 4.6 %collective-permute-start.3 = (f32[8,256]{1,0:T(8,128)S(1)}, f32[8,256]{1,0:T(8,128)S(1)}, u32[]{:S(2)}, u32[]{:S(2)}) collective-permute-start(f32[8,256]{1,0:T(8,128)S(1)} %get-tuple-element.13), channel_id=1, source_target_pairs={{0,4},{1,5},{2,6},{3,7},{4,8},{5,9},{6,10},{7,11},{8,12},{9,13},{1... | collective-permute-start | bytes 24584 | tf_op jit(solution)/shard_map/ppermute | solution.py:481

commit v2 on v1

--- a/solution.py
+++ b/solution.py
@@ -20,6 +20,7 @@
 ROWS = 8
 COLS = 256
 OWN = 4
+UNROLL = True
 
 
 def element_matrix():
@@ -195,7 +196,7 @@
 
     start = flat(plane.forward(load(first - 1)))
     zeros = tuple(jnp.zeros((ROWS, COLS), jnp.float32) for _ in range(12))
-    lax.fori_loop(first - 1, last + 1, body, start + zeros)
+    lax.fori_loop(first - 1, last + 1, body, start + zeros, unroll=UNROLL)
 
 
 class Groups:
@@ -226,19 +227,40 @@
     return MODULUS_FLOOR + density * density * density * (1.0 - MODULUS_FLOOR)
 
 
-def smooth_kernel(slabs, info, own, below, above, edge, smooth, coarse, mod, x, d, w, right, free, left):
+def flip_matrix():
+    row = lax.broadcasted_iota(jnp.int32, (128, 128), 0)
+    return (row + lax.broadcasted_iota(jnp.int32, (128, 128), 1) == 127).astype(jnp.float32)
+
+
+def flipped(stacked):
+    return jnp.dot(stacked, flip_matrix(), precision=lax.Precision.HIGHEST, preferred_element_type=jnp.float32)
+
+
+def smooth_kernel(
+    slabs, info, own, below, above, edge, smooth, coarse, dens_out, free_out, right_out, mod, x, d, w, right, free, left
+):
     plane, groups = Plane(1), Groups()
     slab, sweep_count = info[0], info[2]
     has_below = (slab > 0).astype(jnp.float32)
     has_edge = (slab > 1).astype(jnp.float32)
     has_above = (slab < slabs - 1).astype(jnp.float32)
 
-    mod[0] = modulus_of(edge[0]) * has_edge
+    halves = [edge[0]] + [source[0, k] for source in (below, own, above) for k in range(OWN)]
+    turned = flipped(jnp.concatenate(halves, axis=0))
+    insides = [has_edge] + [has_below] * OWN + [None] * OWN + [has_above] * OWN
+    for k in range(13):
+        density = jnp.concatenate([halves[k], turned[ROWS * k : ROWS * (k + 1)]], axis=1)
+        value = modulus_of(density)
+        mod[k] = value if insides[k] is None else value * insides[k]
+        if 4 <= k < 9:
+            dens_out[k - 4] = density
+
+    def both_halves(source, field, k):
+        return jnp.concatenate([source[1 + field, k], source[3 + field, k]], axis=1)
+
     for source, at, inside in ((below, 0, has_below), (own, 4, None), (above, 8, has_above)):
         for k in range(OWN):
-            value = modulus_of(source[0, k])
-            mod[1 + at + k] = value if inside is None else value * inside
-            open_node = 1.0 - source[2, k]
+            open_node = 1.0 - both_halves(source, 1, k)
             free[at + k] = open_node if inside is None else open_node * inside
 
     def prepare(q, carry):
@@ -250,10 +272,10 @@
         w[q] = inverse
         return summed
 
-    lax.fori_loop(0, 12, prepare, plane.corner_sum(mod[0]))
+    lax.fori_loop(0, 12, prepare, plane.corner_sum(mod[0]), unroll=UNROLL)
     for source, at in ((below, 0), (own, 4), (above, 8)):
         for k in range(OWN):
-            loaded = free[at + k] * source[1, k]
+            loaded = free[at + k] * both_halves(source, 0, k)
             start = loaded * (w[at + k] * np.float32(1.0 / CENTRE))
             right[at + k] = loaded
             for c in range(3):
@@ -299,35 +321,43 @@
     fields = [groups.both((left[c, 1] + left[c, 2]) + (left[c, 3] + left[c, 4])) for c in range(3)]
     here = groups.both((mod[5] + mod[6]) + (mod[7] + mod[8])) * np.float32(1.0 / 64.0)
     under = groups.both((mod[1] + mod[2]) + (mod[3] + mod[4])) * np.float32(1.0 / 64.0)
-    packed = jnp.where(groups.lane_in == 0, here, under)
+    packed = here
     for c in range(3):
-        packed = jnp.where(groups.row_in == c, fields[c], packed)
-    coarse[...] = packed
+        packed = jnp.where(groups.lane_in == c, fields[c], packed)
+    packed = jnp.where(groups.row_in == 0, packed, under)
+    coarse[0:2] = packed[0:2]
+    coarse[2:4] = packed[4:6]
+    for k in range(6):
+        free_out[k] = free[k + 3]
+    for k in range(OWN):
+        right_out[k] = right[k + 4]
 
 
 def correct_kernel(
-    slabs, info, own, below, above, smooth, gathered, moved, image, slope, sums, window, mod, x, d, w, target, p, free, img, energy
+    slabs, info, smooth, dens, free, right, gathered, moved, image, slope, sums, window, mod, x, d, w, target, p, fmod, img, energy
 ):
     coarse_plane, plane, groups = Plane(4), Plane(1), Groups()
     slab, mirror, sweep_count = info[0], info[1], info[3]
     offset = slab % 4
+    upper_rows = lax.broadcasted_iota(jnp.int32, (ROWS, COLS), 0) >= 4
+
+    def widened(first, second):
+        return jnp.where(upper_rows, jnp.broadcast_to(second, (ROWS, COLS)), jnp.broadcast_to(first, (ROWS, COLS)))
+
     for k in range(4):
-        window[k] = gathered[k, ROWS : 2 * ROWS]
-        window[4 + k] = gathered[k, :ROWS]
-        window[8 + k] = gathered[4 + k, ROWS : 2 * ROWS]
-
-    is_here = (groups.row_in == 3) & (groups.lane_in == 0)
-    is_under = (groups.row_in == 3) & (groups.lane_in == 1)
+        window[k] = widened(gathered[k, 4:5], gathered[k, 6:7])
+        window[4 + k] = widened(gathered[k, 0:1], gathered[k, 2:3])
+        window[8 + k] = widened(gathered[4 + k, 4:5], gathered[4 + k, 6:7])
 
     def unpack(q, carry):
         packed = window[offset + q]
         for c in range(3):
-            target[c, q] = groups.over_rows(jnp.where(groups.row_in == c, packed, 0.0))
-        mod[q + 1] = groups.both(jnp.where(is_here, packed, 0.0))
+            target[c, q] = groups.over_lanes(jnp.where(groups.lane_in == c, packed, 0.0))
+        mod[q + 1] = groups.over_lanes(jnp.where(groups.lane_in == 3, packed, 0.0))
         return carry
 
-    lax.fori_loop(0, 9, unpack, 0)
-    mod[0] = groups.both(jnp.where(is_under, window[offset], 0.0))
+    lax.fori_loop(0, 9, unpack, 0, unroll=UNROLL)
+    mod[0] = widened(gathered[offset, 5:6], gathered[offset, 7:8])
 
     def prepare(q, carry):
         summed = coarse_plane.corner_sum(mod[q + 1])
@@ -342,7 +372,7 @@
             d[c, q] = start
         return summed
 
-    lax.fori_loop(0, 9, prepare, coarse_plane.corner_sum(mod[0]))
+    lax.fori_loop(0, 9, prepare, coarse_plane.corner_sum(mod[0]), unroll=UNROLL)
 
     for k, (keep, add) in enumerate(chebyshev_factors(), 1):
 
@@ -366,20 +396,12 @@
             )
 
     has_below = (slab > 0).astype(jnp.float32)
-    has_above = (slab < slabs - 1).astype(jnp.float32)
     for k in range(6):
-        source, at, inside, coarse = (
-            (below, 3, has_below, 3) if k == 0 else (above, 0, has_above, 5) if k == 5 else (own, k - 1, None, 4)
-        )
-        open_node = 1.0 - source[2, at]
-        if inside is not None:
-            open_node = open_node * inside
-        free[k] = open_node
-        for c in range(3):
-            p[c, k] = smooth[c, k] + open_node * x[c, coarse]
+        for c in range(3):
+            p[c, k] = smooth[c, k] + free[k] * x[c, 3 if k == 0 else 5 if k == 5 else 4]
         if k < 5:
-            value = modulus_of(source[0, at])
-            mod[k] = value if inside is None else value * inside
+            value = modulus_of(dens[k])
+            fmod[k] = value * has_below if k == 0 else value
 
     def consume_image(q, forces, strain):
         is_free = free[q] > 0.0
@@ -391,25 +413,22 @@
         f = free[q]
         return [f * p[c, q] for c in range(3)]
 
-    apply_planes(plane, 1, 4, load_p, lambda q: mod[q], 1.0, consume_image, True)
+    apply_planes(plane, 1, 4, load_p, lambda q: fmod[q], 1.0, consume_image, True)
 
     first = jnp.zeros((ROWS, COLS), jnp.float32)
     second = jnp.zeros((ROWS, COLS), jnp.float32)
     half = pl.ds(pl.multiple_of(mirror * 128, 128), 128)
     for k in range(OWN):
-        loaded = free[k + 1] * own[1, k]
+        loaded = right[k]
         for c in range(3):
             first = first + (loaded * np.float32(DIRECTION[c])) * p[c, k + 1]
             second = second + p[c, k + 1] * img[c, k + 1]
             moved[c, k] = p[c, k + 1, :, half]
             image[c, k] = img[c, k + 1, :, half]
-        density = own[0, k]
+        density = dens[k + 1]
         energy[k + 1] = np.float32(-3.0 * (1.0 - MODULUS_FLOOR)) * (density * density) * energy[k + 1]
-    flip = (
-        lax.broadcasted_iota(jnp.int32, (128, 128), 0) + lax.broadcasted_iota(jnp.int32, (128, 128), 1) == 127
-    ).astype(jnp.float32)
     second_half = jnp.concatenate([energy[k + 1, :, 128:] for k in range(OWN)], axis=0)
-    turned = jnp.dot(second_half, flip, precision=lax.Precision.HIGHEST, preferred_element_type=jnp.float32)
+    turned = flipped(second_half)
     for k in range(OWN):
         slope[k] = energy[k + 1, :, :128] + turned[ROWS * k : ROWS * (k + 1)]
     lane = lax.broadcasted_iota(jnp.int32, (1, 128), 1)
@@ -453,42 +472,25 @@
     return lax.ppermute(array, axis, pairs)
 
 
-def on_device(density, load_mask, fixed_mask, sweeps):
-    slabs = lax.axis_size(SLAB)
-    slab, mirror = lax.axis_index(SLAB), lax.axis_index("mirror")
-    info = jnp.concatenate([jnp.stack([slab, mirror]).astype(jnp.int32), sweeps])
+def run_smooth(slabs, info, own, below, above, edge):
     plane = (ROWS, COLS)
-
-    masks = lax.all_gather(jnp.concatenate([load_mask, fixed_mask], axis=0), "mirror")
-    masks = jnp.concatenate([masks[0], masks[1]], axis=-1).astype(jnp.float32)
-    wide = jnp.concatenate([density, density[..., ::-1]], axis=-1)
-    own = jnp.concatenate([wide[None], masks], axis=0)
-    below = shifted(own, SLAB, 1)
-    above = shifted(own, SLAB, -1)
-    edge = shifted(wide[OWN - 1 :], SLAB, 2)
-
     field = (3, 12) + plane
-    smooth, coarse = call(
+    return call(
         functools.partial(smooth_kernel, slabs),
-        [(3, 6) + plane, plane],
+        [(3, 6) + plane, (4, COLS), (5,) + plane, (6,) + plane, (OWN,) + plane],
         [info, own, below, above, edge],
         [(13,) + plane, field, field, (12,) + plane, (12,) + plane, (12,) + plane, (3, 5) + plane],
     )
 
-    reach = 4
-    pairs = [(i, i + reach) for i in range(slabs - reach)]
-    pairs += [(slabs + i + reach, slabs + i) for i in range(slabs - reach)]
-    arrived = lax.ppermute(coarse, ("mirror",) + SLAB, pairs)
-    sent = jnp.broadcast_to(jnp.concatenate([coarse, arrived], axis=0), (8, 2 * ROWS, COLS))
-    gathered = lax.all_to_all(sent, ("mirror", "x"), 0, 0)
-
+
+def run_correct(slabs, group, info, smooth, dens, free, right, gathered):
+    plane = (ROWS, COLS)
     coarse_field = (3, 9) + plane
-    group = lax.axis_size(("y", "x"))
     part = (3, OWN, ROWS, 128)
-    moved, image, slope, sums = call(
+    return call(
         functools.partial(correct_kernel, slabs),
         [part, part, part[1:], (group, 1, 128)],
-        [info, own, below, above, smooth, gathered],
+        [info, smooth, dens, free, right, gathered],
         [
             (12,) + plane,
             (10,) + plane,
@@ -497,11 +499,36 @@
             (9,) + plane,
             coarse_field,
             (3, 6) + plane,
-            (6,) + plane,
+            (5,) + plane,
             (3, 5) + plane,
             (5,) + plane,
         ],
     )
+
+
+def on_device(density, load_mask, fixed_mask, sweeps):
+    slabs = lax.axis_size(SLAB)
+    slab, mirror = lax.axis_index(SLAB), lax.axis_index("mirror")
+    info = jnp.concatenate([jnp.stack([slab, mirror]).astype(jnp.int32), sweeps])
+
+    edge = shifted(density[OWN - 1 :], SLAB, 2)
+    masks = lax.all_gather(jnp.concatenate([load_mask, fixed_mask], axis=0), "mirror")
+    own = jnp.concatenate([density[None], masks.reshape((4,) + density.shape).astype(jnp.float32)], axis=0)
+    below = shifted(own, SLAB, 1)
+    above = shifted(own, SLAB, -1)
+
+    smooth, coarse, dens, free, right = run_smooth(slabs, info, own, below, above, edge)
+
+    reach = 4
+    pairs = [(i, i + reach) for i in range(slabs - reach)]
+    pairs += [(slabs + i + reach, slabs + i) for i in range(slabs - reach)]
+    arrived = lax.ppermute(coarse, ("mirror",) + SLAB, pairs)
+    sent = jnp.broadcast_to(jnp.concatenate([coarse, arrived], axis=0), (8, 8, COLS))
+    gathered = lax.all_to_all(sent, ("mirror", "x"), 0, 0)
+
+    part = (3, OWN, ROWS, 128)
+    group = lax.axis_size(("y", "x"))
+    moved, image, slope, sums = run_correct(slabs, group, info, smooth, dens, free, right, gathered)
     sums = lax.all_to_all(sums, ("y", "x"), 0, 0)
     length = lax.axis_size("z")
     sums = jnp.broadcast_to(jnp.sum(sums, axis=0), (length, 1, 128))

time: 89.8 us -> 82 us (0.913)
  Pallas kernels: 14.2 us -> 7.21 us
    pallas_call x3, Pallas kernels: 14.2 us -> 7.21 us  [call(): pl.pallas_call(kernel, out_shape=[jax.ShapeDtypeStruct(shape, jnp.float32...]
where the time goes in v2:
time: 82 us; the launch traced here: 81.4 us
  blocking collectives  53.1 us (65%)
  starting transfers between devices  15.4 us (19%)
  Pallas kernels  7.21 us (9%)
  waiting for transfers between devices  2.75 us (3%)
  local copies, waits for them, and re-layouts  1.38 us (2%)
  other arithmetic  0.87 us (1%)
    all_to_all x1, blocking collectives, on_device(): sums = lax.all_to_all(sums, ('y', 'x'), 0, 0)  24.2 us
    all_to_all x1, blocking collectives, on_device(): sums = lax.all_to_all(sums, 'z', 0, 0)  17.4 us
    ppermute x3, starting transfers between devices, shifted(): return lax.ppermute(array, axis, pairs)  12 us
    all_to_all x1, blocking collectives, on_device(): gathered = lax.all_to_all(sent, ('mirror', 'x'), 0, 0)  9.65 us
    pallas_call x3, Pallas kernels, call(): pl.pallas_call(kernel, out_shape=[jax.ShapeDtypeStruct(shape, jnp.float32...  7.21 us
    ppermute x1, starting transfers between devices, on_device(): arrived = lax.ppermute(coarse, ('mirror',) + SLAB, pairs)  3.39 us
    all_gather x1, blocking collectives, on_device(): lax.all_gather(jnp.concatenate([load_mask, fixed_mask], axis=0), 'mirror')  1.84 us
  transfers between devices with their start and end apart: 4, of which 3 were waited for; matrix products, arithmetic and copies ran while one was open for 0% of the time, Pallas kernels for 0%

profile of v2, /device:TPU:2, one launch (start us, length us, event | category | flops | bytes accessed | tf_op | source)
XLA Modules:
  0.0 81.4 jit_solution(17003129377969077489)
XLA Ops:
  0.6 0.7 pad_add_fusion
  1.4 1.8 %all-gather = s32[4,4,8,128]{3,2,1,0:T(8,128)S(1)} all-gather(s32[2,4,8,128]{3,2,1,0:T(8,128)S(1)} %pad_add_fusion), channel_id=2, replica_groups=mesh['mirror'=2,'y'=4,'z'=16,'x'=4] {'mirror'}, dimensions={0}, use_global_device_ids=true | all-gather | bytes 98304 | tf_op jit(solution)/shard_map/all_gather | solution.py:515
  3.2 0.0 copy-start.2
  3.2 0.7 copy-done.2
  3.9 7.8 %collective-permute-start.1 = (f32[5,4,8,128]{3,2,1,0:T(8,128)S(1)}, f32[5,4,8,128]{3,2,1,0:T(8,128)S(1)}, u32[]{:S(2)}, u32[]{:S(2)}) collective-permute-start(f32[5,4,8,128]{3,2,1,0:T(8,128)S(1)} %pad_maximum_fusion.own), channel_id=1, source_target_pairs={{1,0},{2,1},{3,2},{4,3},{5,4},{6,5},{7,6},{8,7},{9,8},{10,9},{11,1... | collective-permute-start | bytes 245768 | tf_op jit(solution)/shard_map/ppermute | solution.py:472
  11.7 1.9 %collective-permute-start = (f32[5,4,8,128]{3,2,1,0:T(8,128)S(1)}, f32[5,4,8,128]{3,2,1,0:T(8,128)S(1)}, u32[]{:S(2)}, u32[]{:S(2)}) collective-permute-start(f32[5,4,8,128]{3,2,1,0:T(8,128)S(1)} %pad_maximum_fusion.own), channel_id=1, source_target_pairs={{0,1},{1,2},{2,3},{3,4},{4,5},{5,6},{6,7},{7,8},{8,9},{9,10},{10,1... | collective-permute-start | bytes 245768 | tf_op jit(solution)/shard_map/ppermute | solution.py:472
  13.7 2.2 %collective-permute-start.2 = (f32[1,8,128]{2,1,0:T(8,128)S(1)}, f32[1,8,128]{2,1,0:T(8,128)S(1)}, u32[]{:S(2)}, u32[]{:S(2)}) collective-permute-start(f32[1,8,128]{2,1,0:T(8,128)S(1)} %slice.3), channel_id=1, source_target_pairs={{0,2},{1,3},{2,4},{3,5},{4,6},{5,7},{6,8},{7,9},{8,10},{9,11},{10,... | collective-permute-start | bytes 12296 | tf_op jit(solution)/shard_map/ppermute | solution.py:472
  15.9 0.0 copy-start.3
  16.0 0.6 copy-done.3
  16.6 0.1 pad_add_fusion.1.info
  16.7 0.6 collective-permute-done.2.edge
  17.2 0.0 collective-permute-done.1.above
  17.3 0.9 %collective-permute-done.below = f32[5,4,8,128]{3,2,1,0:T(8,128)S(1)} collective-permute-done((f32[5,4,8,128]{3,2,1,0:T(8,128)S(1)}, f32[5,4,8,128]{3,2,1,0:T(8,128)S(1)}, u32[]{:S(2)}, u32[]{:S(2)}) %collective-permute-start) | collective-permute-done | bytes 81952 | tf_op jit(solution)/shard_map/ppermute | solution.py:472
  18.1 2.3 %shard_map.67 = (f32[3,6,8,256]{3,2,1,0:T(8,128)S(1)}, f32[4,256]{1,0:T(4,128)S(1)}, f32[5,8,256]{2,1,0:T(8,128)S(1)}, f32[6,8,256]{2,1,0:T(8,128)S(1)}, f32[4,8,256]{2,1,0:T(8,128)S(1)}) custom-call(s32[4]{0:T(128)S(1)} %pad_add_fusion.1.info, f32[5,4,8,128]{3,2,1,0:T(8,128)S(1)} %pad_maximum_fusion.own, f32[5,4,8,128]{3,2,1,0:T(8,128)S(1)} %collective-permute-done.below, ...), custom_call_target="tpu_custom_call" | custom-call | tf_op jit(solution)/shard_map/pallas_call | solution.py:459
  20.4 3.4 %collective-permute-start.3 = (f32[4,256]{1,0:T(4,128)S(1)}, f32[4,256]{1,0:T(4,128)S(1)}, u32[]{:S(2)}, u32[]{:S(2)}) collective-permute-start(f32[4,256]{1,0:T(4,128)S(1)} %get-tuple-element.19), channel_id=1, source_target_pairs={{0,4},{1,5},{2,6},{3,7},{4,8},{5,9},{6,10},{7,11},{8,12},{9,13},{1... | collective-permute-start | bytes 12296 | tf_op jit(solution)/shard_map/ppermute | solution.py:525
  23.8 1.3 %collective-permute-done.3 = f32[4,256]{1,0:T(4,128)S(1)} collective-permute-done((f32[4,256]{1,0:T(4,128)S(1)}, f32[4,256]{1,0:T(4,128)S(1)}, u32[]{:S(2)}, u32[]{:S(2)}) %collective-permute-start.3) | collective-permute-done | bytes 4128 | tf_op jit(solution)/shard_map/ppermute | solution.py:525
  25.2 9.6 %all_to_all.15.gathered = f32[8,8,256]{2,1,0:T(8,128)S(1)} all-to-all(f32[8,8,256]{2,1,0:T(8,128)S(1)} %broadcast_in_dim.16), channel_id=1, replica_groups=mesh['mirror'=2,'y'=4,'z'=16,'x'=4] {'mirror','x'}, dimensions={0} | all-to-all | bytes 131072 | tf_op jit(solution)/shard_map/all_to_all | solution.py:527
  34.8 4.2 %shard_map.68 = (f32[3,4,8,128]{3,2,1,0:T(8,128)S(1)}, f32[3,4,8,128]{3,2,1,0:T(8,128)S(1)}, f32[4,8,128]{2,1,0:T(8,128)S(1)}, f32[16,1,128]{2,1,0:T(1,128)S(1)}) custom-call(s32[4]{0:T(128)S(1)} %pad_add_fusion.1.info, f32[3,6,8,256]{3,2,1,0:T(8,128)S(1)} %get-tuple-element.15.smooth, f32[5,8,256]{2,1,0:T(8,128)S(1)} %get-tuple-element.16.dens, ...), custom_call_target="tpu_custom_call" | custom-call | tf_op jit(solution)/shard_map/pallas_call | solution.py:459
  39.0 24.2 %all_to_all.16 = f32[16,1,128]{2,1,0:T(1,128)S(1)} all-to-all(f32[16,1,128]{2,1,0:T(1,128)S(1)} %get-tuple-element.20), channel_id=1, replica_groups=mesh['mirror'=2,'y'=4,'z'=16,'x'=4] {'y','x'}, dimensions={0} | all-to-all | bytes 16384 | tf_op jit(solution)/shard_map/all_to_all | solution.py:532
  63.2 0.0 copy-start.1
  63.2 0.0 copy-start
  63.2 17.4 %all_to_all.17.totals = f32[16,1,128]{2,1,0:T(1,128)S(1)} all-to-all(f32[16,1,128]{2,1,0:T(1,128)S(1)} %broadcast_in_dim.17), channel_id=1, replica_groups=mesh['mirror'=2,'y'=4,'z'=16,'x'=4] {'z'}, dimensions={0} | all-to-all | bytes 16384 | tf_op jit(solution)/shard_map/all_to_all | solution.py:535
  80.7 0.0 copy-done.1
  80.7 0.0 copy-done
  80.7 0.7 shard_map.69
  (7 shorter events, 0.1 us)
Async XLA Ops:
  3.2 0.7 copy-start.2
  3.9 13.3 %collective-permute-start.1 = (f32[5,4,8,128]{3,2,1,0:T(8,128)S(1)}, f32[5,4,8,128]{3,2,1,0:T(8,128)S(1)}, u32[]{:S(2)}, u32[]{:S(2)}) collective-permute-start(f32[5,4,8,128]{3,2,1,0:T(8,128)S(1)} %pad_maximum_fusion.own), channel_id=1, source_target_pairs={{1,0},{2,1},{3,2},{4,3},{5,4},{6,5},{7,6},{8,7},{9,8},{10,9},{11,1... | collective-permute-start | bytes 245768 | tf_op jit(solution)/shard_map/ppermute | solution.py:472
  11.7 6.4 %collective-permute-start = (f32[5,4,8,128]{3,2,1,0:T(8,128)S(1)}, f32[5,4,8,128]{3,2,1,0:T(8,128)S(1)}, u32[]{:S(2)}, u32[]{:S(2)}) collective-permute-start(f32[5,4,8,128]{3,2,1,0:T(8,128)S(1)} %pad_maximum_fusion.own), channel_id=1, source_target_pairs={{0,1},{1,2},{2,3},{3,4},{4,5},{5,6},{6,7},{7,8},{8,9},{9,10},{10,1... | collective-permute-start | bytes 245768 | tf_op jit(solution)/shard_map/ppermute | solution.py:472
  13.7 3.6 %collective-permute-start.2 = (f32[1,8,128]{2,1,0:T(8,128)S(1)}, f32[1,8,128]{2,1,0:T(8,128)S(1)}, u32[]{:S(2)}, u32[]{:S(2)}) collective-permute-start(f32[1,8,128]{2,1,0:T(8,128)S(1)} %slice.3), channel_id=1, source_target_pairs={{0,2},{1,3},{2,4},{3,5},{4,6},{5,7},{6,8},{7,9},{8,10},{9,11},{10,... | collective-permute-start | bytes 12296 | tf_op jit(solution)/shard_map/ppermute | solution.py:472
  15.9 0.7 copy-start.3
  20.4 4.7 %collective-permute-start.3 = (f32[4,256]{1,0:T(4,128)S(1)}, f32[4,256]{1,0:T(4,128)S(1)}, u32[]{:S(2)}, u32[]{:S(2)}) collective-permute-start(f32[4,256]{1,0:T(4,128)S(1)} %get-tuple-element.19), channel_id=1, source_target_pairs={{0,4},{1,5},{2,6},{3,7},{4,8},{5,9},{6,10},{7,11},{8,12},{9,13},{1... | collective-permute-start | bytes 12296 | tf_op jit(solution)/shard_map/ppermute | solution.py:525
  63.2 17.5 %copy-start.1 = (s32[1,4,8,128]{3,2,1,0:T(8,128)S(1)}, s32[1,4,8,128]{3,2,1,0:T(8,128)}, u32[]{:S(2)}) copy-start(s32[1,4,8,128]{3,2,1,0:T(8,128)} %load.1) | copy-start | bytes 49156
  63.2 17.5 %copy-start = (s32[1,4,8,128]{3,2,1,0:T(8,128)S(1)}, s32[1,4,8,128]{3,2,1,0:T(8,128)}, u32[]{:S(2)}) copy-start(s32[1,4,8,128]{3,2,1,0:T(8,128)} %fixed.1) | copy-start | bytes 49156

commit v3 on v2

--- a/solution.py
+++ b/solution.py
@@ -20,7 +20,7 @@
 ROWS = 8
 COLS = 256
 OWN = 4
-UNROLL = True
+DENSITY, LOAD, FIXED, FIELDS = 0, 1, 2, 3
 
 
 def element_matrix():
@@ -186,17 +186,18 @@
     def nested(values):
         return [[values[3 * m + c] for c in range(3)] for m in range(4)]
 
-    def body(p, carry):
+    def body(q, carry):
         low, pending = nested(carry[:12]), nested(carry[12:])
-        high = plane.forward(load(p + 1))
-        on_low, on_high, energy = plane.element(low, high, modulus_at(p), scale, with_energy)
+        high = plane.forward(load(q + 1))
+        on_low, on_high, energy = plane.element(low, high, modulus_at(q), scale, with_energy)
         total = [[pending[m][c] + on_low[m][c] for c in range(3)] for m in range(4)]
-        consume(p, plane.backward(total), energy)
+        consume(q, plane.backward(total), energy)
         return flat(high) + flat(on_high)
 
-    start = flat(plane.forward(load(first - 1)))
+    start = flat(plane.forward(load(first)))
     zeros = tuple(jnp.zeros((ROWS, COLS), jnp.float32) for _ in range(12))
-    lax.fori_loop(first - 1, last + 1, body, start + zeros, unroll=UNROLL)
+    carry = lax.fori_loop(first, last + 1, body, start + zeros, unroll=True)
+    return lambda: plane.backward(nested(carry[12:]))
 
 
 class Groups:
@@ -236,51 +237,44 @@
     return jnp.dot(stacked, flip_matrix(), precision=lax.Precision.HIGHEST, preferred_element_type=jnp.float32)
 
 
+def both_halves(source, field, k):
+    return jnp.concatenate([source[field, k], source[FIELDS + field, k]], axis=1)
+
+
 def smooth_kernel(
-    slabs, info, own, below, above, edge, smooth, coarse, dens_out, free_out, right_out, mod, x, d, w, right, free, left
+    slabs, info, own, below, above, smooth, coarse, dens_out, free_out, right_out, mod, x, d, w, right, free, left
 ):
     plane, groups = Plane(1), Groups()
     slab, sweep_count = info[0], info[2]
     has_below = (slab > 0).astype(jnp.float32)
-    has_edge = (slab > 1).astype(jnp.float32)
     has_above = (slab < slabs - 1).astype(jnp.float32)
 
-    halves = [edge[0]] + [source[0, k] for source in (below, own, above) for k in range(OWN)]
-    turned = flipped(jnp.concatenate(halves, axis=0))
-    insides = [has_edge] + [has_below] * OWN + [None] * OWN + [has_above] * OWN
-    for k in range(13):
-        density = jnp.concatenate([halves[k], turned[ROWS * k : ROWS * (k + 1)]], axis=1)
+    places = [(below, k, has_below) for k in range(OWN)]
+    places += [(own, k, None) for k in range(OWN)]
+    places += [(above, k, has_above) for k in range(OWN)]
+    turned = flipped(jnp.concatenate([source[DENSITY, k] for source, k, _ in places], axis=0))
+    for e, (source, k, inside) in enumerate(places):
+        density = jnp.concatenate([source[DENSITY, k], turned[ROWS * e : ROWS * (e + 1)]], axis=1)
         value = modulus_of(density)
-        mod[k] = value if insides[k] is None else value * insides[k]
-        if 4 <= k < 9:
-            dens_out[k - 4] = density
-
-    def both_halves(source, field, k):
-        return jnp.concatenate([source[1 + field, k], source[3 + field, k]], axis=1)
-
-    for source, at, inside in ((below, 0, has_below), (own, 4, None), (above, 8, has_above)):
-        for k in range(OWN):
-            open_node = 1.0 - both_halves(source, 1, k)
-            free[at + k] = open_node if inside is None else open_node * inside
-
-    def prepare(q, carry):
-        summed = plane.corner_sum(mod[q + 1])
-        scaling = np.float32(row_total()) * (carry + summed)
-        f = free[q]
-        scaling = jnp.where(f > 0.0, scaling, 1.0)
-        inverse = 1.0 / scaling
+        mod[e] = value if inside is None else value * inside
+        if source is own:
+            dens_out[k] = density
+        if e > 0:
+            open_node = 1.0 - both_halves(source, FIXED, k)
+            free[e - 1] = open_node if inside is None else open_node * inside
+
+    summed = plane.corner_sum(mod[0])
+    for q, (source, k, _) in enumerate(places[1:]):
+        lower, summed = summed, plane.corner_sum(mod[q + 1])
+        scaling = np.float32(row_total()) * (lower + summed)
+        inverse = 1.0 / jnp.where(free[q] > 0.0, scaling, 1.0)
         w[q] = inverse
-        return summed
-
-    lax.fori_loop(0, 12, prepare, plane.corner_sum(mod[0]), unroll=UNROLL)
-    for source, at in ((below, 0), (own, 4), (above, 8)):
-        for k in range(OWN):
-            loaded = free[at + k] * both_halves(source, 0, k)
-            start = loaded * (w[at + k] * np.float32(1.0 / CENTRE))
-            right[at + k] = loaded
-            for c in range(3):
-                x[c, at + k] = start * np.float32(DIRECTION[c])
-                d[c, at + k] = start * np.float32(DIRECTION[c])
+        loaded = free[q] * both_halves(source, LOAD, k)
+        right[q] = loaded
+        start = loaded * (inverse * np.float32(1.0 / CENTRE))
+        for c in range(3):
+            x[c, q] = start * np.float32(DIRECTION[c])
+            d[c, q] = start * np.float32(DIRECTION[c])
 
     def load(q):
         f = free[q]
@@ -305,7 +299,7 @@
                     d[c, q] = update
                     x[c, q] = now + update
 
-            apply_planes(plane, k, 11 - k, load, modulus_at, 1.0, consume)
+            apply_planes(plane, k - 1, 10 - k, load, modulus_at, 1.0, consume)
 
     def consume_left(q, forces, _energy):
         is_free = free[q] > 0.0
@@ -313,56 +307,59 @@
             image = jnp.where(is_free, forces[c], x[c, q])
             left[c, q - 3] = right[q] * np.float32(DIRECTION[c]) - image
 
-    apply_planes(plane, 4, 7, load, modulus_at, 1.0, consume_left)
-
+    rest = apply_planes(plane, 3, 6, load, modulus_at, 1.0, consume_left)()
+
+    odd = groups.lane_bits[0]
+    packed = groups.both((mod[4] + mod[5]) + (mod[6] + mod[7])) * np.float32(1.0 / 64.0)
     for c in range(3):
-        for k in range(6):
+        for k in range(5):
             smooth[c, k] = x[c, k + 3]
-    fields = [groups.both((left[c, 1] + left[c, 2]) + (left[c, 3] + left[c, 4])) for c in range(3)]
-    here = groups.both((mod[5] + mod[6]) + (mod[7] + mod[8])) * np.float32(1.0 / 64.0)
-    under = groups.both((mod[1] + mod[2]) + (mod[3] + mod[4])) * np.float32(1.0 / 64.0)
-    packed = here
-    for c in range(3):
-        packed = jnp.where(groups.lane_in == c, fields[c], packed)
-    packed = jnp.where(groups.row_in == 0, packed, under)
-    coarse[0:2] = packed[0:2]
-    coarse[2:4] = packed[4:6]
-    for k in range(6):
+        mine = groups.both((left[c, 0] + left[c, 1]) + (left[c, 2] + left[c, 3]))
+        passed = groups.both(free[7] * -rest[c])
+        packed = jnp.where(groups.row_in == c, jnp.where(odd, passed, mine), packed)
+    coarse[...] = packed
+    for k in range(5):
         free_out[k] = free[k + 3]
     for k in range(OWN):
-        right_out[k] = right[k + 4]
+        right_out[k] = right[k + 3]
 
 
 def correct_kernel(
-    slabs, info, smooth, dens, free, right, gathered, moved, image, slope, sums, window, mod, x, d, w, target, p, fmod, img, energy
+    slabs, info, smooth, dens, free, right, gathered, moved, image, passed, slope, sums, mod, x, d, w, target, p, own_mod, energy
 ):
     coarse_plane, plane, groups = Plane(4), Plane(1), Groups()
     slab, mirror, sweep_count = info[0], info[1], info[3]
     offset = slab % 4
     upper_rows = lax.broadcasted_iota(jnp.int32, (ROWS, COLS), 0) >= 4
-
-    def widened(first, second):
+    odd = groups.lane_bits[0]
+    groups_of = [(k, ROWS) for k in range(4)] + [(k, 0) for k in range(4)] + [(4 + k, ROWS) for k in range(4)]
+
+    def unpack(field, j):
+        block, row = groups_of[j]
+        first = gathered[block, row + field : row + field + 1]
+        second = gathered[block, row + 4 + field : row + 5 + field]
         return jnp.where(upper_rows, jnp.broadcast_to(second, (ROWS, COLS)), jnp.broadcast_to(first, (ROWS, COLS)))
 
-    for k in range(4):
-        window[k] = widened(gathered[k, 4:5], gathered[k, 6:7])
-        window[4 + k] = widened(gathered[k, 0:1], gathered[k, 2:3])
-        window[8 + k] = widened(gathered[4 + k, 4:5], gathered[4 + k, 6:7])
-
-    def unpack(q, carry):
-        packed = window[offset + q]
-        for c in range(3):
-            target[c, q] = groups.over_lanes(jnp.where(groups.lane_in == c, packed, 0.0))
-        mod[q + 1] = groups.over_lanes(jnp.where(groups.lane_in == 3, packed, 0.0))
-        return carry
-
-    lax.fori_loop(0, 9, unpack, 0, unroll=UNROLL)
-    mod[0] = widened(gathered[offset, 5:6], gathered[offset, 7:8])
-
-    def prepare(q, carry):
-        summed = coarse_plane.corner_sum(mod[q + 1])
-        scaling = np.float32(4.0 * row_total()) * (carry + summed)
-        at = slab - 4 + q
+    for lead in range(4):
+
+        @pl.when(offset == lead)
+        def _(lead=lead):
+            for q in range(9):
+                mod[q] = unpack(3, lead + q)
+            for c in range(3):
+                lower = None
+                for q in range(9):
+                    value = unpack(c, lead + q)
+                    if q > 0:
+                        part = jnp.where(odd, pltpu.roll(value, 1, 1), value)
+                        target[c, q - 1] = part + jnp.where(odd, lower, pltpu.roll(lower, COLS - 1, 1))
+                    lower = value
+
+    summed = coarse_plane.corner_sum(mod[0])
+    for q in range(8):
+        lower, summed = summed, coarse_plane.corner_sum(mod[q + 1])
+        scaling = np.float32(4.0 * row_total()) * (lower + summed)
+        at = slab - 3 + q
         inside = ((at >= 0) & (at < slabs)).astype(jnp.float32)
         inverse = inside / jnp.where(scaling > 0.0, scaling, 1.0)
         w[q] = inverse
@@ -370,9 +367,6 @@
             start = target[c, q] * (inverse * np.float32(1.0 / CENTRE))
             x[c, q] = start
             d[c, q] = start
-        return summed
-
-    lax.fori_loop(0, 9, prepare, coarse_plane.corner_sum(mod[0]), unroll=UNROLL)
 
     for k, (keep, add) in enumerate(chebyshev_factors(), 1):
 
@@ -387,57 +381,57 @@
 
             apply_planes(
                 coarse_plane,
-                k,
-                8 - k,
+                k - 1,
+                7 - k,
                 lambda q: [x[c, q] for c in range(3)],
                 lambda q: mod[q + 1],
                 4.0,
                 consume,
             )
 
-    has_below = (slab > 0).astype(jnp.float32)
-    for k in range(6):
-        for c in range(3):
-            p[c, k] = smooth[c, k] + free[k] * x[c, 3 if k == 0 else 5 if k == 5 else 4]
-        if k < 5:
-            value = modulus_of(dens[k])
-            fmod[k] = value * has_below if k == 0 else value
+    half = pl.ds(pl.multiple_of(mirror * 128, 128), 128)
+    for k in range(5):
+        for c in range(3):
+            p[c, k] = smooth[c, k] + free[k] * x[c, 4 if k == 4 else 3]
+    for k in range(OWN):
+        own_mod[k] = modulus_of(dens[k])
 
     def consume_image(q, forces, strain):
-        is_free = free[q] > 0.0
-        for c in range(3):
-            img[c, q] = jnp.where(is_free, forces[c], p[c, q])
+        for c in range(3):
+            x[c, q] = forces[c]
         energy[q] = strain
 
     def load_p(q):
         f = free[q]
         return [f * p[c, q] for c in range(3)]
 
-    apply_planes(plane, 1, 4, load_p, lambda q: fmod[q], 1.0, consume_image, True)
+    rest = apply_planes(plane, 0, 3, load_p, lambda q: own_mod[q], 1.0, consume_image, True)()
 
     first = jnp.zeros((ROWS, COLS), jnp.float32)
     second = jnp.zeros((ROWS, COLS), jnp.float32)
-    half = pl.ds(pl.multiple_of(mirror * 128, 128), 128)
+    for c in range(3):
+        x[c, 4] = rest[c]
+        passed[c] = x[c, 4, :, half]
     for k in range(OWN):
-        loaded = right[k]
-        for c in range(3):
-            first = first + (loaded * np.float32(DIRECTION[c])) * p[c, k + 1]
-            second = second + p[c, k + 1] * img[c, k + 1]
-            moved[c, k] = p[c, k + 1, :, half]
-            image[c, k] = img[c, k + 1, :, half]
-        density = dens[k + 1]
-        energy[k + 1] = np.float32(-3.0 * (1.0 - MODULUS_FLOOR)) * (density * density) * energy[k + 1]
-    second_half = jnp.concatenate([energy[k + 1, :, 128:] for k in range(OWN)], axis=0)
-    turned = flipped(second_half)
+        second = second + own_mod[k] * energy[k]
+        for c in range(3):
+            value = p[c, k]
+            first = first + (right[k] * np.float32(DIRECTION[c])) * value
+            second = second + (1.0 - free[k]) * (value * value)
+            moved[c, k] = p[c, k, :, half]
+            image[c, k] = x[c, k, :, half]
+        density = dens[k]
+        energy[k] = np.float32(-3.0 * (1.0 - MODULUS_FLOOR)) * (density * density) * energy[k]
+    turned = flipped(jnp.concatenate([energy[k, :, 128:] for k in range(OWN)], axis=0))
     for k in range(OWN):
-        slope[k] = energy[k + 1, :, :128] + turned[ROWS * k : ROWS * (k + 1)]
+        slope[k] = energy[k, :, :128] + turned[ROWS * k : ROWS * (k + 1)]
     lane = lax.broadcasted_iota(jnp.int32, (1, 128), 1)
     dots = jnp.where(lane == 0, jnp.sum(first), jnp.where(lane == 1, jnp.sum(second), 0.0))
     for k in range(sums.shape[0]):
         sums[k] = dots
 
 
-def scale_kernel(totals, load, fixed, moved, image, slope, displacement, residual, sensitivity):
+def scale_kernel(totals, load, fixed, moved, image, arrived, slope, displacement, residual, sensitivity):
     total = totals[0]
     for k in range(1, totals.shape[0]):
         total = total + totals[k]
@@ -449,7 +443,9 @@
         loaded = ((1 - fixed[0, k]) * load[0, k]).astype(jnp.float32)
         for c in range(3):
             displacement[c, k] = alpha * moved[c, k]
-            residual[c, k] = loaded * np.float32(DIRECTION[c]) - alpha * image[c, k]
+            forces = image[c, k] + arrived[c] if k == 0 else image[c, k]
+            forces = jnp.where(fixed[0, k] == 0, forces, moved[c, k])
+            residual[c, k] = loaded * np.float32(DIRECTION[c]) - alpha * forces
         sensitivity[k] = alpha * (alpha * slope[k])
 
 
@@ -472,37 +468,26 @@
     return lax.ppermute(array, axis, pairs)
 
 
-def run_smooth(slabs, info, own, below, above, edge):
+def run_smooth(slabs, info, own, below, above):
     plane = (ROWS, COLS)
-    field = (3, 12) + plane
+    field = (3, 11) + plane
     return call(
         functools.partial(smooth_kernel, slabs),
-        [(3, 6) + plane, (4, COLS), (5,) + plane, (6,) + plane, (OWN,) + plane],
-        [info, own, below, above, edge],
-        [(13,) + plane, field, field, (12,) + plane, (12,) + plane, (12,) + plane, (3, 5) + plane],
+        [(3, 5) + plane, plane, (OWN,) + plane, (5,) + plane, (OWN,) + plane],
+        [info, own, below, above],
+        [(12,) + plane, field, field, (11,) + plane, (11,) + plane, (11,) + plane, (3, 4) + plane],
     )
 
 
 def run_correct(slabs, group, info, smooth, dens, free, right, gathered):
     plane = (ROWS, COLS)
-    coarse_field = (3, 9) + plane
+    field = (3, 8) + plane
     part = (3, OWN, ROWS, 128)
     return call(
         functools.partial(correct_kernel, slabs),
-        [part, part, part[1:], (group, 1, 128)],
+        [part, part, (3, ROWS, 128), part[1:], (group, 1, 128)],
         [info, smooth, dens, free, right, gathered],
-        [
-            (12,) + plane,
-            (10,) + plane,
-            coarse_field,
-            coarse_field,
-            (9,) + plane,
-            coarse_field,
-            (3, 6) + plane,
-            (5,) + plane,
-            (3, 5) + plane,
-            (5,) + plane,
-        ],
+        [(9,) + plane, field, field, (8,) + plane, field, (3, 5) + plane, (OWN,) + plane, (OWN,) + plane],
     )
 
 
@@ -511,30 +496,29 @@
     slab, mirror = lax.axis_index(SLAB), lax.axis_index("mirror")
     info = jnp.concatenate([jnp.stack([slab, mirror]).astype(jnp.int32), sweeps])
 
-    edge = shifted(density[OWN - 1 :], SLAB, 2)
-    masks = lax.all_gather(jnp.concatenate([load_mask, fixed_mask], axis=0), "mirror")
-    own = jnp.concatenate([density[None], masks.reshape((4,) + density.shape).astype(jnp.float32)], axis=0)
+    here = jnp.concatenate([density[None], load_mask.astype(jnp.float32), fixed_mask.astype(jnp.float32)], axis=0)
+    own = lax.all_gather(here, "mirror").reshape((2 * FIELDS,) + density.shape)
     below = shifted(own, SLAB, 1)
     above = shifted(own, SLAB, -1)
-
-    smooth, coarse, dens, free, right = run_smooth(slabs, info, own, below, above, edge)
+    smooth, coarse, dens, free, right = run_smooth(slabs, info, own, below, above)
 
     reach = 4
     pairs = [(i, i + reach) for i in range(slabs - reach)]
     pairs += [(slabs + i + reach, slabs + i) for i in range(slabs - reach)]
     arrived = lax.ppermute(coarse, ("mirror",) + SLAB, pairs)
-    sent = jnp.broadcast_to(jnp.concatenate([coarse, arrived], axis=0), (8, 8, COLS))
+    sent = jnp.broadcast_to(jnp.concatenate([coarse, arrived], axis=0), (8, 2 * ROWS, COLS))
     gathered = lax.all_to_all(sent, ("mirror", "x"), 0, 0)
 
     part = (3, OWN, ROWS, 128)
     group = lax.axis_size(("y", "x"))
-    moved, image, slope, sums = run_correct(slabs, group, info, smooth, dens, free, right, gathered)
+    moved, image, passed, slope, sums = run_correct(slabs, group, info, smooth, dens, free, right, gathered)
+    added = shifted(passed, SLAB, 1)
     sums = lax.all_to_all(sums, ("y", "x"), 0, 0)
     length = lax.axis_size("z")
     sums = jnp.broadcast_to(jnp.sum(sums, axis=0), (length, 1, 128))
     sums = lax.all_to_all(sums, "z", 0, 0)
     displacement, residual, sensitivity = call(
-        scale_kernel, [part, part, part[1:]], [sums, load_mask, fixed_mask, moved, image, slope]
+        scale_kernel, [part, part, part[1:]], [sums, load_mask, fixed_mask, moved, image, added, slope]
     )
     return displacement[None], residual[None], sensitivity
 

time: 82 us -> 79.6 us (0.971)
  blocking collectives: 53.1 us -> 37 us
  waiting for transfers between devices: 2.75 us -> 15 us
  starting transfers between devices: 15.4 us -> 17.5 us
  Pallas kernels: 7.21 us -> 5.91 us
    all_to_all x1 -> x0, blocking collectives: 17.4 us -> none  [on_device(): sums = lax.all_to_all(sums, 'z', 0, 0)]
    all_to_all x0 -> x1, waiting for transfers between devices: none -> 6.78 us  [on_device(): sums = lax.all_to_all(sums, 'z', 0, 0)]
    ppermute x3, waiting for transfers between devices: 1.44 us -> 6.92 us  [shifted(): return lax.ppermute(array, axis, pairs)]
    all_to_all x0 -> x1, starting transfers between devices: none -> 4.01 us  [on_device(): sums = lax.all_to_all(sums, 'z', 0, 0)]
    all_to_all x1, blocking collectives: 24.2 us -> 26.6 us  [on_device(): sums = lax.all_to_all(sums, ('y', 'x'), 0, 0)]
    ppermute x1, starting transfers between devices: 3.39 us -> 1.29 us  [on_device(): arrived = lax.ppermute(coarse, ('mirror',) + SLAB, pairs)]
    pallas_call x3, Pallas kernels: 7.21 us -> 5.91 us  [call(): pl.pallas_call(kernel, out_shape=[jax.ShapeDtypeStruct(shape, jnp.float32...]
    all_to_all x1, blocking collectives: 9.65 us -> 8.58 us  [on_device(): gathered = lax.all_to_all(sent, ('mirror', 'x'), 0, 0)]
  transfers between devices with their start and end apart: 4 -> 5, of which waited for: 3 -> 4; matrix products, arithmetic and copies ran while one was open for 0% -> 0% of each run, Pallas kernels for 0% -> 0%
where the time goes in v3:
time: 79.6 us; the launch traced here: 79 us
  blocking collectives  37 us (46%)
  starting transfers between devices  17.5 us (22%)
  waiting for transfers between devices  15 us (19%)
  Pallas kernels  5.91 us (7%)
  local copies, waits for them, and re-layouts  1.99 us (2%)
  other arithmetic  0.85 us (1%)
    all_to_all x1, blocking collectives, on_device(): sums = lax.all_to_all(sums, ('y', 'x'), 0, 0)  26.6 us
    ppermute x3, starting transfers between devices, shifted(): return lax.ppermute(array, axis, pairs)  12.2 us
    all_to_all x1, blocking collectives, on_device(): gathered = lax.all_to_all(sent, ('mirror', 'x'), 0, 0)  8.58 us
    ppermute x3, waiting for transfers between devices, shifted(): return lax.ppermute(array, axis, pairs)  6.92 us
    all_to_all x1, waiting for transfers between devices, on_device(): sums = lax.all_to_all(sums, 'z', 0, 0)  6.78 us
    pallas_call x3, Pallas kernels, call(): pl.pallas_call(kernel, out_shape=[jax.ShapeDtypeStruct(shape, jnp.float32...  5.91 us
    all_to_all x1, starting transfers between devices, on_device(): sums = lax.all_to_all(sums, 'z', 0, 0)  4.01 us
    all_gather x1, blocking collectives, on_device(): own = lax.all_gather(here, 'mirror').reshape((2 * FIELDS,) + density.shape)  1.86 us
  transfers between devices with their start and end apart: 5, of which 4 were waited for; matrix products, arithmetic and copies ran while one was open for 0% of the time, Pallas kernels for 0%

profile of v3, /device:TPU:2, one launch (start us, length us, event | category | flops | bytes accessed | tf_op | source)
XLA Modules:
  0.0 79.0 jit_solution(4653657619524676460)
XLA Ops:
  0.6 0.0 copy-start
  0.6 0.7 convert_element_type.6
  1.4 0.0 copy-done
  1.4 0.0 copy-start.2
  1.4 0.7 copy-done.2
  2.1 1.9 %all-gather.own = f32[6,4,8,128]{3,2,1,0:T(8,128)S(1)} all-gather(f32[3,4,8,128]{3,2,1,0:T(8,128)S(1)} %pad_maximum_fusion), channel_id=2, replica_groups=mesh['mirror'=2,'y'=4,'z'=16,'x'=4] {'mirror'}, dimensions={0}, use_global_device_ids=true | all-gather | bytes 147456 | tf_op jit(solution)/shard_map/all_gather | solution.py:500
  4.0 7.8 %collective-permute-start.1 = (f32[6,4,8,128]{3,2,1,0:T(8,128)S(1)}, f32[6,4,8,128]{3,2,1,0:T(8,128)S(1)}, u32[]{:S(2)}, u32[]{:S(2)}) collective-permute-start(f32[6,4,8,128]{3,2,1,0:T(8,128)S(1)} %all-gather.own), channel_id=1, source_target_pairs={{1,0},{2,1},{3,2},{4,3},{5,4},{6,5},{7,6},{8,7},{9,8},{10,9},{11,1... | collective-permute-start | bytes 294920 | tf_op jit(solution)/shard_map/ppermute | solution.py:468
  11.8 1.9 %collective-permute-start = (f32[6,4,8,128]{3,2,1,0:T(8,128)S(1)}, f32[6,4,8,128]{3,2,1,0:T(8,128)S(1)}, u32[]{:S(2)}, u32[]{:S(2)}) collective-permute-start(f32[6,4,8,128]{3,2,1,0:T(8,128)S(1)} %all-gather.own), channel_id=1, source_target_pairs={{0,1},{1,2},{2,3},{3,4},{4,5},{5,6},{6,7},{7,8},{8,9},{9,10},{10,1... | collective-permute-start | bytes 294920 | tf_op jit(solution)/shard_map/ppermute | solution.py:468
  13.7 0.0 copy-start.3
  13.7 0.6 copy-done.3
  14.4 0.1 pad_add_fusion.info
  14.4 0.0 collective-permute-done.1.above
  14.4 3.8 %collective-permute-done.below = f32[6,4,8,128]{3,2,1,0:T(8,128)S(1)} collective-permute-done((f32[6,4,8,128]{3,2,1,0:T(8,128)S(1)}, f32[6,4,8,128]{3,2,1,0:T(8,128)S(1)}, u32[]{:S(2)}, u32[]{:S(2)}) %collective-permute-start) | collective-permute-done | bytes 98336 | tf_op jit(solution)/shard_map/ppermute | solution.py:468
  18.3 3.2 %shard_map.67 = (f32[3,5,8,256]{3,2,1,0:T(8,128)S(1)}, f32[8,256]{1,0:T(8,128)S(1)}, f32[4,8,256]{2,1,0:T(8,128)S(1)}, f32[5,8,256]{2,1,0:T(8,128)S(1)}, f32[4,8,256]{2,1,0:T(8,128)S(1)}) custom-call(s32[4]{0:T(128)S(1)} %pad_add_fusion.info, f32[6,4,8,128]{3,2,1,0:T(8,128)S(1)} %all-gather.own, f32[6,4,8,128]{3,2,1,0:T(8,128)S(1)} %collective-permute-done.below, ...), custom_call_target="tpu_custom_call" | custom-call | tf_op jit(solution)/shard_map/pallas_call | solution.py:455
  21.5 1.3 %collective-permute-start.2 = (f32[8,256]{1,0:T(8,128)S(1)}, f32[8,256]{1,0:T(8,128)S(1)}, u32[]{:S(2)}, u32[]{:S(2)}) collective-permute-start(f32[8,256]{1,0:T(8,128)S(1)} %get-tuple-element.20), channel_id=1, source_target_pairs={{0,4},{1,5},{2,6},{3,7},{4,8},{5,9},{6,10},{7,11},{8,12},{9,13},{1... | collective-permute-start | bytes 24584 | tf_op jit(solution)/shard_map/ppermute | solution.py:508
  22.8 1.3 %collective-permute-done.2 = f32[8,256]{1,0:T(8,128)S(1)} collective-permute-done((f32[8,256]{1,0:T(8,128)S(1)}, f32[8,256]{1,0:T(8,128)S(1)}, u32[]{:S(2)}, u32[]{:S(2)}) %collective-permute-start.2) | collective-permute-done | bytes 8224 | tf_op jit(solution)/shard_map/ppermute | solution.py:508
  24.2 8.6 %all_to_all.15.gathered = f32[8,16,256]{2,1,0:T(8,128)S(1)} all-to-all(f32[8,16,256]{2,1,0:T(8,128)S(1)} %broadcast_in_dim.16), channel_id=1, replica_groups=mesh['mirror'=2,'y'=4,'z'=16,'x'=4] {'mirror','x'}, dimensions={0} | all-to-all | bytes 262144 | tf_op jit(solution)/shard_map/all_to_all | solution.py:510
  32.8 1.9 %shard_map.68 = (f32[3,4,8,128]{3,2,1,0:T(8,128)S(1)}, f32[3,4,8,128]{3,2,1,0:T(8,128)S(1)}, f32[3,8,128]{2,1,0:T(8,128)S(1)}, f32[4,8,128]{2,1,0:T(8,128)S(1)}, f32[16,1,128]{2,1,0:T(1,128)S(1)}) custom-call(s32[4]{0:T(128)S(1)} %pad_add_fusion.info, f32[3,5,8,256]{3,2,1,0:T(8,128)S(1)} %get-tuple-element.16.smooth, ...), custom_call_target="tpu_custom_call" | custom-call | tf_op jit(solution)/shard_map/pallas_call | solution.py:455
  34.7 26.6 %all_to_all.16 = f32[16,1,128]{2,1,0:T(1,128)S(1)} all-to-all(f32[16,1,128]{2,1,0:T(1,128)S(1)} %get-tuple-element.21), channel_id=1, replica_groups=mesh['mirror'=2,'y'=4,'z'=16,'x'=4] {'y','x'}, dimensions={0} | all-to-all | bytes 16384 | tf_op jit(solution)/shard_map/all_to_all | solution.py:516
  61.3 0.0 copy-start.1
  61.3 0.6 broadcast_in_dim.17
  61.9 4.0 %all-to-all-start.2 = ((f32[16,1,128]{2,1,0:T(1,128)}), f32[16,1,128]{2,1,0:T(1,128)S(1)}, u32[]{:S(2)}, u32[]{:S(2)}) async-start(f32[16,1,128]{2,1,0:T(1,128)} %broadcast_in_dim.17), calls=%async_computation.2 | async-start | bytes 16384 | tf_op jit(solution)/shard_map/all_to_all | solution.py:519
  65.9 2.5 %collective-permute-start.3 = (f32[3,8,128]{2,1,0:T(8,128)S(1)}, f32[3,8,128]{2,1,0:T(8,128)S(1)}, u32[]{:S(2)}, u32[]{:S(2)}) collective-permute-start(f32[3,8,128]{2,1,0:T(8,128)S(1)} %get-tuple-element.24), channel_id=1, source_target_pairs={{0,1},{1,2},{2,3},{3,4},{4,5},{5,6},{6,7},{7,8},{8,9},{9,10},{10,1... | collective-permute-start | bytes 36872 | tf_op jit(solution)/shard_map/ppermute | solution.py:468
  68.4 3.1 %collective-permute-done.3.arrived = f32[3,8,128]{2,1,0:T(8,128)S(1)} collective-permute-done((f32[3,8,128]{2,1,0:T(8,128)S(1)}, f32[3,8,128]{2,1,0:T(8,128)S(1)}, u32[]{:S(2)}, u32[]{:S(2)}) %collective-permute-start.3) | collective-permute-done | bytes 12320 | tf_op jit(solution)/shard_map/ppermute | solution.py:468
  71.5 6.8 %all-to-all-done.2.totals = f32[16,1,128]{2,1,0:T(1,128)S(1)} async-done(((f32[16,1,128]{2,1,0:T(1,128)}), f32[16,1,128]{2,1,0:T(1,128)S(1)}, u32[]{:S(2)}, u32[]{:S(2)}) %all-to-all-start.2) | async-done | bytes 8224 | tf_op jit(solution)/shard_map/all_to_all | solution.py:519
  78.3 0.0 copy-done.1
  78.3 0.7 shard_map.69
  (5 shorter events, 0.1 us)
Async XLA Ops:
  0.6 0.7 copy-start
  1.4 0.7 copy-start.2
  4.0 10.5 %collective-permute-start.1 = (f32[6,4,8,128]{3,2,1,0:T(8,128)S(1)}, f32[6,4,8,128]{3,2,1,0:T(8,128)S(1)}, u32[]{:S(2)}, u32[]{:S(2)}) collective-permute-start(f32[6,4,8,128]{3,2,1,0:T(8,128)S(1)} %all-gather.own), channel_id=1, source_target_pairs={{1,0},{2,1},{3,2},{4,3},{5,4},{6,5},{7,6},{8,7},{9,8},{10,9},{11,1... | collective-permute-start | bytes 294920 | tf_op jit(solution)/shard_map/ppermute | solution.py:468
  11.8 6.5 %collective-permute-start = (f32[6,4,8,128]{3,2,1,0:T(8,128)S(1)}, f32[6,4,8,128]{3,2,1,0:T(8,128)S(1)}, u32[]{:S(2)}, u32[]{:S(2)}) collective-permute-start(f32[6,4,8,128]{3,2,1,0:T(8,128)S(1)} %all-gather.own), channel_id=1, source_target_pairs={{0,1},{1,2},{2,3},{3,4},{4,5},{5,6},{6,7},{7,8},{8,9},{9,10},{10,1... | collective-permute-start | bytes 294920 | tf_op jit(solution)/shard_map/ppermute | solution.py:468
  13.7 0.7 copy-start.3
  21.5 2.6 %collective-permute-start.2 = (f32[8,256]{1,0:T(8,128)S(1)}, f32[8,256]{1,0:T(8,128)S(1)}, u32[]{:S(2)}, u32[]{:S(2)}) collective-permute-start(f32[8,256]{1,0:T(8,128)S(1)} %get-tuple-element.20), channel_id=1, source_target_pairs={{0,4},{1,5},{2,6},{3,7},{4,8},{5,9},{6,10},{7,11},{8,12},{9,13},{1... | collective-permute-start | bytes 24584 | tf_op jit(solution)/shard_map/ppermute | solution.py:508
  61.3 17.0 %copy-start.1 = (s32[1,4,8,128]{3,2,1,0:T(8,128)S(1)}, s32[1,4,8,128]{3,2,1,0:T(8,128)}, u32[]{:S(2)}) copy-start(s32[1,4,8,128]{3,2,1,0:T(8,128)} %load.1) | copy-start | bytes 49156
  61.9 16.4 %all-to-all-start.2 = ((f32[16,1,128]{2,1,0:T(1,128)}), f32[16,1,128]{2,1,0:T(1,128)S(1)}, u32[]{:S(2)}, u32[]{:S(2)}) async-start(f32[16,1,128]{2,1,0:T(1,128)} %broadcast_in_dim.17), calls=%async_computation.2 | async-start | bytes 16384 | tf_op jit(solution)/shard_map/all_to_all | solution.py:519
  65.9 5.6 %collective-permute-start.3 = (f32[3,8,128]{2,1,0:T(8,128)S(1)}, f32[3,8,128]{2,1,0:T(8,128)S(1)}, u32[]{:S(2)}, u32[]{:S(2)}) collective-permute-start(f32[3,8,128]{2,1,0:T(8,128)S(1)} %get-tuple-element.24), channel_id=1, source_target_pairs={{0,1},{1,2},{2,3},{3,4},{4,5},{5,6},{6,7},{7,8},{8,9},{9,10},{10,1... | collective-permute-start | bytes 36872 | tf_op jit(solution)/shard_map/ppermute | solution.py:468

commit v4 on v3

--- a/solution.py
+++ b/solution.py
@@ -20,7 +20,7 @@
 ROWS = 8
 COLS = 256
 OWN = 4
-DENSITY, LOAD, FIXED, FIELDS = 0, 1, 2, 3
+LOAD, FIXED = 0, 1
 
 
 def element_matrix():
@@ -237,24 +237,30 @@
     return jnp.dot(stacked, flip_matrix(), precision=lax.Precision.HIGHEST, preferred_element_type=jnp.float32)
 
 
-def both_halves(source, field, k):
-    return jnp.concatenate([source[field, k], source[FIELDS + field, k]], axis=1)
+def pack_kernel(density, load, fixed, packed):
+    packed[0] = density[...]
+    packed[1 + LOAD] = load[0].astype(jnp.float32)
+    packed[1 + FIXED] = fixed[0].astype(jnp.float32)
 
 
 def smooth_kernel(
-    slabs, info, own, below, above, smooth, coarse, dens_out, free_out, right_out, mod, x, d, w, right, free, left
+    slabs, info, own, below, above, masks, smooth, coarse, dens_out, free_out, right_out, mod, x, d, w, right, free, left
 ):
     plane, groups = Plane(1), Groups()
     slab, sweep_count = info[0], info[2]
     has_below = (slab > 0).astype(jnp.float32)
     has_above = (slab < slabs - 1).astype(jnp.float32)
 
+    def both_halves(source, field, k):
+        at = 2 * (0 if source is below else 1 if source is own else 2) + field
+        return jnp.concatenate([masks[at, k], masks[6 + at, k]], axis=1)
+
     places = [(below, k, has_below) for k in range(OWN)]
     places += [(own, k, None) for k in range(OWN)]
     places += [(above, k, has_above) for k in range(OWN)]
-    turned = flipped(jnp.concatenate([source[DENSITY, k] for source, k, _ in places], axis=0))
+    turned = flipped(jnp.concatenate([source[0, k] for source, k, _ in places], axis=0))
     for e, (source, k, inside) in enumerate(places):
-        density = jnp.concatenate([source[DENSITY, k], turned[ROWS * e : ROWS * (e + 1)]], axis=1)
+        density = jnp.concatenate([source[0, k], turned[ROWS * e : ROWS * (e + 1)]], axis=1)
         value = modulus_of(density)
         mod[e] = value if inside is None else value * inside
         if source is own:
@@ -468,13 +474,13 @@
     return lax.ppermute(array, axis, pairs)
 
 
-def run_smooth(slabs, info, own, below, above):
+def run_smooth(slabs, info, own, below, above, masks):
     plane = (ROWS, COLS)
     field = (3, 11) + plane
     return call(
         functools.partial(smooth_kernel, slabs),
         [(3, 5) + plane, plane, (OWN,) + plane, (5,) + plane, (OWN,) + plane],
-        [info, own, below, above],
+        [info, own, below, above, masks],
         [(12,) + plane, field, field, (11,) + plane, (11,) + plane, (11,) + plane, (3, 4) + plane],
     )
 
@@ -496,11 +502,12 @@
     slab, mirror = lax.axis_index(SLAB), lax.axis_index("mirror")
     info = jnp.concatenate([jnp.stack([slab, mirror]).astype(jnp.int32), sweeps])
 
-    here = jnp.concatenate([density[None], load_mask.astype(jnp.float32), fixed_mask.astype(jnp.float32)], axis=0)
-    own = lax.all_gather(here, "mirror").reshape((2 * FIELDS,) + density.shape)
+    (own,) = call(pack_kernel, [(3,) + density.shape], [density, load_mask, fixed_mask])
     below = shifted(own, SLAB, 1)
     above = shifted(own, SLAB, -1)
-    smooth, coarse, dens, free, right = run_smooth(slabs, info, own, below, above)
+    masks = lax.all_gather(jnp.concatenate([below[1:], own[1:], above[1:]], axis=0), "mirror")
+    masks = masks.reshape((12,) + density.shape)
+    smooth, coarse, dens, free, right = run_smooth(slabs, info, own, below, above, masks)
 
     reach = 4
     pairs = [(i, i + reach) for i in range(slabs - reach)]

time: 79.6 us -> 80.4 us (1.010)
  local copies, waits for them, and re-layouts: 1.99 us -> 3.43 us
    unnamed x8 -> x12, local copies, waits for them, and re-layouts: 1.37 us -> 2.81 us
    pallas_call x3 -> x4, Pallas kernels: 5.91 us -> 6.34 us  [call(): pl.pallas_call(kernel, out_shape=[jax.ShapeDtypeStruct(shape, jnp.float32...]
where the time goes in v4:
time: 80.4 us; the launch traced here: 79.7 us
  blocking collectives  37.1 us (46%)
  starting transfers between devices  17.5 us (22%)
  waiting for transfers between devices  14.5 us (18%)
  Pallas kernels  6.34 us (8%)
  local copies, waits for them, and re-layouts  3.43 us (4%)
    all_to_all x1, blocking collectives, on_device(): sums = lax.all_to_all(sums, ('y', 'x'), 0, 0)  26 us
    ppermute x3, starting transfers between devices, shifted(): return lax.ppermute(array, axis, pairs)  12.2 us
    all_to_all x1, blocking collectives, on_device(): gathered = lax.all_to_all(sent, ('mirror', 'x'), 0, 0)  9.15 us
    all_to_all x1, waiting for transfers between devices, on_device(): sums = lax.all_to_all(sums, 'z', 0, 0)  6.78 us
    ppermute x3, waiting for transfers between devices, shifted(): return lax.ppermute(array, axis, pairs)  6.39 us
    pallas_call x4, Pallas kernels, call(): pl.pallas_call(kernel, out_shape=[jax.ShapeDtypeStruct(shape, jnp.float32...  6.34 us
    all_to_all x1, starting transfers between devices, on_device(): sums = lax.all_to_all(sums, 'z', 0, 0)  4.01 us
    unnamed x12, local copies, waits for them, and re-layouts  2.81 us
  transfers between devices with their start and end apart: 5, of which 4 were waited for; matrix products, arithmetic and copies ran while one was open for 0% of the time, Pallas kernels for 0%

profile of v4, /device:TPU:2, one launch (start us, length us, event | category | flops | bytes accessed | tf_op | source)
XLA Modules:
  0.0 79.7 jit_solution(18400269713932009320)
XLA Ops:
  0.6 0.0 copy-start
  0.6 0.7 copy-done
  1.4 0.0 copy-start.2
  1.4 0.7 copy-done.2
  2.1 0.0 copy-start.4
  2.1 0.7 copy-done.4
  2.8 7.8 %collective-permute-start.1 = (f32[3,4,8,128]{3,2,1,0:T(8,128)S(1)}, f32[3,4,8,128]{3,2,1,0:T(8,128)S(1)}, u32[]{:S(2)}, u32[]{:S(2)}) collective-permute-start(f32[3,4,8,128]{3,2,1,0:T(8,128)S(1)} %shard_map.67.own), channel_id=1, source_target_pairs={{1,0},{2,1},{3,2},{4,3},{5,4},{6,5},{7,6},{8,7},{9,8},{10,9},{11,1... | collective-permute-start | bytes 147464 | tf_op jit(solution)/shard_map/ppermute | solution.py:474
  10.6 1.9 %collective-permute-start = (f32[3,4,8,128]{3,2,1,0:T(8,128)S(1)}, f32[3,4,8,128]{3,2,1,0:T(8,128)S(1)}, u32[]{:S(2)}, u32[]{:S(2)}) collective-permute-start(f32[3,4,8,128]{3,2,1,0:T(8,128)S(1)} %shard_map.67.own), channel_id=1, source_target_pairs={{0,1},{1,2},{2,3},{3,4},{4,5},{5,6},{6,7},{7,8},{8,9},{9,10},{10,1... | collective-permute-start | bytes 147464 | tf_op jit(solution)/shard_map/ppermute | solution.py:474
  12.5 0.0 copy-start.5
  12.6 0.6 copy-done.5
  13.2 0.1 pad_add_fusion.info
  13.3 0.0 collective-permute-done.1.above
  13.3 3.3 %collective-permute-done.below = f32[3,4,8,128]{3,2,1,0:T(8,128)S(1)} collective-permute-done((f32[3,4,8,128]{3,2,1,0:T(8,128)S(1)}, f32[3,4,8,128]{3,2,1,0:T(8,128)S(1)}, u32[]{:S(2)}, u32[]{:S(2)}) %collective-permute-start) | collective-permute-done | bytes 49184 | tf_op jit(solution)/shard_map/ppermute | solution.py:474
  16.6 1.9 %all-gather.masks = f32[12,4,8,128]{3,2,1,0:T(8,128)S(1)} all-gather(f32[6,4,8,128]{3,2,1,0:T(8,128)S(1)} %pad_maximum_fusion), channel_id=2, replica_groups=mesh['mirror'=2,'y'=4,'z'=16,'x'=4] {'mirror'}, dimensions={0}, use_global_device_ids=true | all-gather | bytes 294912 | tf_op jit(solution)/shard_map/all_gather | solution.py:508
  18.6 3.2 %shard_map.68 = (f32[3,5,8,256]{3,2,1,0:T(8,128)S(1)}, f32[8,256]{1,0:T(8,128)S(1)}, f32[4,8,256]{2,1,0:T(8,128)S(1)}, f32[5,8,256]{2,1,0:T(8,128)S(1)}, f32[4,8,256]{2,1,0:T(8,128)S(1)}) custom-call(s32[4]{0:T(128)S(1)} %pad_add_fusion.info, f32[3,4,8,128]{3,2,1,0:T(8,128)S(1)} %shard_map.67.own, f32[3,4,8,128]{3,2,1,0:T(8,128)S(1)} %collective-permute-done.below, ...), custom_call_target="tpu_custom_call" | custom-call | tf_op jit(solution)/shard_map/pallas_call | solution.py:461
  21.8 1.3 %collective-permute-start.2 = (f32[8,256]{1,0:T(8,128)S(1)}, f32[8,256]{1,0:T(8,128)S(1)}, u32[]{:S(2)}, u32[]{:S(2)}) collective-permute-start(f32[8,256]{1,0:T(8,128)S(1)} %get-tuple-element.20), channel_id=1, source_target_pairs={{0,4},{1,5},{2,6},{3,7},{4,8},{5,9},{6,10},{7,11},{8,12},{9,13},{1... | collective-permute-start | bytes 24584 | tf_op jit(solution)/shard_map/ppermute | solution.py:515
  23.1 1.3 %collective-permute-done.2 = f32[8,256]{1,0:T(8,128)S(1)} collective-permute-done((f32[8,256]{1,0:T(8,128)S(1)}, f32[8,256]{1,0:T(8,128)S(1)}, u32[]{:S(2)}, u32[]{:S(2)}) %collective-permute-start.2) | collective-permute-done | bytes 8224 | tf_op jit(solution)/shard_map/ppermute | solution.py:515
  24.5 9.2 %all_to_all.15.gathered = f32[8,16,256]{2,1,0:T(8,128)S(1)} all-to-all(f32[8,16,256]{2,1,0:T(8,128)S(1)} %broadcast_in_dim.12), channel_id=1, replica_groups=mesh['mirror'=2,'y'=4,'z'=16,'x'=4] {'mirror','x'}, dimensions={0} | all-to-all | bytes 262144 | tf_op jit(solution)/shard_map/all_to_all | solution.py:517
  33.6 2.3 %shard_map.69 = (f32[3,4,8,128]{3,2,1,0:T(8,128)S(1)}, f32[3,4,8,128]{3,2,1,0:T(8,128)S(1)}, f32[3,8,128]{2,1,0:T(8,128)S(1)}, f32[4,8,128]{2,1,0:T(8,128)S(1)}, f32[16,1,128]{2,1,0:T(1,128)S(1)}) custom-call(s32[4]{0:T(128)S(1)} %pad_add_fusion.info, f32[3,5,8,256]{3,2,1,0:T(8,128)S(1)} %get-tuple-element.16.smooth, ...), custom_call_target="tpu_custom_call" | custom-call | tf_op jit(solution)/shard_map/pallas_call | solution.py:461
  36.0 26.0 %all_to_all.16 = f32[16,1,128]{2,1,0:T(1,128)S(1)} all-to-all(f32[16,1,128]{2,1,0:T(1,128)S(1)} %get-tuple-element.21), channel_id=1, replica_groups=mesh['mirror'=2,'y'=4,'z'=16,'x'=4] {'y','x'}, dimensions={0} | all-to-all | bytes 16384 | tf_op jit(solution)/shard_map/all_to_all | solution.py:523
  62.0 0.0 copy-start.1
  62.0 0.0 copy-start.3
  62.0 0.6 broadcast_in_dim.13
  62.6 4.0 %all-to-all-start.2 = ((f32[16,1,128]{2,1,0:T(1,128)}), f32[16,1,128]{2,1,0:T(1,128)S(1)}, u32[]{:S(2)}, u32[]{:S(2)}) async-start(f32[16,1,128]{2,1,0:T(1,128)} %broadcast_in_dim.13), calls=%async_computation.2 | async-start | bytes 16384 | tf_op jit(solution)/shard_map/all_to_all | solution.py:526
  66.6 2.5 %collective-permute-start.3 = (f32[3,8,128]{2,1,0:T(8,128)S(1)}, f32[3,8,128]{2,1,0:T(8,128)S(1)}, u32[]{:S(2)}, u32[]{:S(2)}) collective-permute-start(f32[3,8,128]{2,1,0:T(8,128)S(1)} %get-tuple-element.24), channel_id=1, source_target_pairs={{0,1},{1,2},{2,3},{3,4},{4,5},{5,6},{6,7},{7,8},{8,9},{9,10},{10,1... | collective-permute-start | bytes 36872 | tf_op jit(solution)/shard_map/ppermute | solution.py:474
  69.1 3.1 %collective-permute-done.3.arrived = f32[3,8,128]{2,1,0:T(8,128)S(1)} collective-permute-done((f32[3,8,128]{2,1,0:T(8,128)S(1)}, f32[3,8,128]{2,1,0:T(8,128)S(1)}, u32[]{:S(2)}, u32[]{:S(2)}) %collective-permute-start.3) | collective-permute-done | bytes 12320 | tf_op jit(solution)/shard_map/ppermute | solution.py:474
  72.2 6.8 %all-to-all-done.2.totals = f32[16,1,128]{2,1,0:T(1,128)S(1)} async-done(((f32[16,1,128]{2,1,0:T(1,128)}), f32[16,1,128]{2,1,0:T(1,128)S(1)}, u32[]{:S(2)}, u32[]{:S(2)}) %all-to-all-start.2) | async-done | bytes 8224 | tf_op jit(solution)/shard_map/all_to_all | solution.py:526
  79.0 0.0 copy-done.1
  79.0 0.0 copy-done.3
  79.0 0.7 shard_map.70
  (8 shorter events, 0.1 us)
Async XLA Ops:
  0.6 0.7 copy-start
  1.4 0.7 copy-start.2
  2.1 0.7 copy-start.4
  2.8 10.5 %collective-permute-start.1 = (f32[3,4,8,128]{3,2,1,0:T(8,128)S(1)}, f32[3,4,8,128]{3,2,1,0:T(8,128)S(1)}, u32[]{:S(2)}, u32[]{:S(2)}) collective-permute-start(f32[3,4,8,128]{3,2,1,0:T(8,128)S(1)} %shard_map.67.own), channel_id=1, source_target_pairs={{1,0},{2,1},{3,2},{4,3},{5,4},{6,5},{7,6},{8,7},{9,8},{10,9},{11,1... | collective-permute-start | bytes 147464 | tf_op jit(solution)/shard_map/ppermute | solution.py:474
  10.6 6.0 %collective-permute-start = (f32[3,4,8,128]{3,2,1,0:T(8,128)S(1)}, f32[3,4,8,128]{3,2,1,0:T(8,128)S(1)}, u32[]{:S(2)}, u32[]{:S(2)}) collective-permute-start(f32[3,4,8,128]{3,2,1,0:T(8,128)S(1)} %shard_map.67.own), channel_id=1, source_target_pairs={{0,1},{1,2},{2,3},{3,4},{4,5},{5,6},{6,7},{7,8},{8,9},{9,10},{10,1... | collective-permute-start | bytes 147464 | tf_op jit(solution)/shard_map/ppermute | solution.py:474
  12.5 0.7 copy-start.5
  21.8 2.6 %collective-permute-start.2 = (f32[8,256]{1,0:T(8,128)S(1)}, f32[8,256]{1,0:T(8,128)S(1)}, u32[]{:S(2)}, u32[]{:S(2)}) collective-permute-start(f32[8,256]{1,0:T(8,128)S(1)} %get-tuple-element.20), channel_id=1, source_target_pairs={{0,4},{1,5},{2,6},{3,7},{4,8},{5,9},{6,10},{7,11},{8,12},{9,13},{1... | collective-permute-start | bytes 24584 | tf_op jit(solution)/shard_map/ppermute | solution.py:515
  62.0 17.0 %copy-start.1 = (s32[1,4,8,128]{3,2,1,0:T(8,128)S(1)}, s32[1,4,8,128]{3,2,1,0:T(8,128)}, u32[]{:S(2)}) copy-start(s32[1,4,8,128]{3,2,1,0:T(8,128)} %load.3) | copy-start | bytes 49156
  62.0 17.0 %copy-start.3 = (s32[1,4,8,128]{3,2,1,0:T(8,128)S(1)}, s32[1,4,8,128]{3,2,1,0:T(8,128)}, u32[]{:S(2)}) copy-start(s32[1,4,8,128]{3,2,1,0:T(8,128)} %fixed.3) | copy-start | bytes 49156
  62.6 16.4 %all-to-all-start.2 = ((f32[16,1,128]{2,1,0:T(1,128)}), f32[16,1,128]{2,1,0:T(1,128)S(1)}, u32[]{:S(2)}, u32[]{:S(2)}) async-start(f32[16,1,128]{2,1,0:T(1,128)} %broadcast_in_dim.13), calls=%async_computation.2 | async-start | bytes 16384 | tf_op jit(solution)/shard_map/all_to_all | solution.py:526
  66.6 5.6 %collective-permute-start.3 = (f32[3,8,128]{2,1,0:T(8,128)S(1)}, f32[3,8,128]{2,1,0:T(8,128)S(1)}, u32[]{:S(2)}, u32[]{:S(2)}) collective-permute-start(f32[3,8,128]{2,1,0:T(8,128)S(1)} %get-tuple-element.24), channel_id=1, source_target_pairs={{0,1},{1,2},{2,3},{3,4},{4,5},{5,6},{6,7},{7,8},{8,9},{9,10},{10,1... | collective-permute-start | bytes 36872 | tf_op jit(solution)/shard_map/ppermute | solution.py:474

commit v5 on v3

--- a/solution.py
+++ b/solution.py
@@ -498,8 +498,10 @@
 
     here = jnp.concatenate([density[None], load_mask.astype(jnp.float32), fixed_mask.astype(jnp.float32)], axis=0)
     own = lax.all_gather(here, "mirror").reshape((2 * FIELDS,) + density.shape)
-    below = shifted(own, SLAB, 1)
-    above = shifted(own, SLAB, -1)
+    near = [(i, i + 1) for i in range(slabs - 1)]
+    near += [(slabs + i + 1, slabs + i) for i in range(slabs - 1)]
+    both = lax.all_gather(lax.ppermute(own, ("mirror",) + SLAB, near), "mirror")
+    below, above = both[0], both[1]
     smooth, coarse, dens, free, right = run_smooth(slabs, info, own, below, above)
 
     reach = 4

time: 79.6 us -> 77.3 us (0.971)
  starting transfers between devices: 17.5 us -> 15.1 us
  waiting for transfers between devices: 15 us -> 16.8 us
  blocking collectives: 37 us -> 35.4 us
    ppermute x3 -> x1, starting transfers between devices: 12.2 us -> 2.49 us  [shifted(): return lax.ppermute(array, axis, pairs)]
    ppermute x0 -> x1, waiting for transfers between devices: none -> 5.63 us  [on_device(): both = lax.all_gather(lax.ppermute(own, ('mirror',) + SLAB, near), 'mirror')]
    all_to_all x1, blocking collectives: 26.6 us -> 22.5 us  [on_device(): sums = lax.all_to_all(sums, ('y', 'x'), 0, 0)]
    all_to_all x1, starting transfers between devices: 4.01 us -> 7.92 us  [on_device(): sums = lax.all_to_all(sums, 'z', 0, 0)]
    ppermute x3 -> x1, waiting for transfers between devices: 6.92 us -> 3.09 us  [shifted(): return lax.ppermute(array, axis, pairs)]
    ppermute x0 -> x1, starting transfers between devices: none -> 3.39 us  [on_device(): both = lax.all_gather(lax.ppermute(own, ('mirror',) + SLAB, near), 'mirror')]
    all_gather x0 -> x1, blocking collectives: none -> 1.93 us  [on_device(): both = lax.all_gather(lax.ppermute(own, ('mirror',) + SLAB, near), 'mirror')]
  transfers between devices with their start and end apart: 5 -> 4, of which waited for: 4 -> 4; matrix products, arithmetic and copies ran while one was open for 0% -> 0% of each run, Pallas kernels for 0% -> 0%
where the time goes in v5:
time: 77.3 us; the launch traced here: 76.8 us
  blocking collectives  35.4 us (46%)
  waiting for transfers between devices  16.8 us (22%)
  starting transfers between devices  15.1 us (20%)
  Pallas kernels  5.91 us (8%)
  local copies, waits for them, and re-layouts  2 us (3%)
  other arithmetic  0.85 us (1%)
    all_to_all x1, blocking collectives, on_device(): sums = lax.all_to_all(sums, ('y', 'x'), 0, 0)  22.5 us
    all_to_all x1, blocking collectives, on_device(): gathered = lax.all_to_all(sent, ('mirror', 'x'), 0, 0)  9.1 us
    all_to_all x1, starting transfers between devices, on_device(): sums = lax.all_to_all(sums, 'z', 0, 0)  7.92 us
    all_to_all x1, waiting for transfers between devices, on_device(): sums = lax.all_to_all(sums, 'z', 0, 0)  6.78 us
    pallas_call x3, Pallas kernels, call(): pl.pallas_call(kernel, out_shape=[jax.ShapeDtypeStruct(shape, jnp.float32...  5.91 us
    ppermute x1, waiting for transfers between devices, on_device(): both = lax.all_gather(lax.ppermute(own, ('mirror',) + SLAB, near), 'mirror')  5.63 us
    ppermute x1, starting transfers between devices, on_device(): both = lax.all_gather(lax.ppermute(own, ('mirror',) + SLAB, near), 'mirror')  3.39 us
    ppermute x1, waiting for transfers between devices, shifted(): return lax.ppermute(array, axis, pairs)  3.09 us
  transfers between devices with their start and end apart: 4, of which 4 were waited for; matrix products, arithmetic and copies ran while one was open for 0% of the time, Pallas kernels for 0%

profile of v5, /device:TPU:2, one launch (start us, length us, event | category | flops | bytes accessed | tf_op | source)
XLA Modules:
  0.0 76.8 jit_solution(9109027267555255992)
XLA Ops:
  0.6 0.0 copy-start
  0.6 0.7 convert_element_type.6
  1.4 0.0 copy-done
  1.4 0.0 copy-start.2
  1.4 0.7 copy-done.2
  2.1 1.9 %all-gather.own = f32[6,4,8,128]{3,2,1,0:T(8,128)S(1)} all-gather(f32[3,4,8,128]{3,2,1,0:T(8,128)S(1)} %pad_maximum_fusion), channel_id=2, replica_groups=mesh['mirror'=2,'y'=4,'z'=16,'x'=4] {'mirror'}, dimensions={0}, use_global_device_ids=true | all-gather | bytes 147456 | tf_op jit(solution)/shard_map/all_gather | solution.py:500
  4.0 3.4 %collective-permute-start = (f32[6,4,8,128]{3,2,1,0:T(8,128)S(1)}, f32[6,4,8,128]{3,2,1,0:T(8,128)S(1)}, u32[]{:S(2)}, u32[]{:S(2)}) collective-permute-start(f32[6,4,8,128]{3,2,1,0:T(8,128)S(1)} %all-gather.own), channel_id=1, source_target_pairs={{0,1},{1,2},{2,3},{3,4},{4,5},{5,6},{6,7},{7,8},{8,9},{9,10},{10,1... | collective-permute-start | bytes 294920 | tf_op jit(solution)/shard_map/ppermute | solution.py:503
  7.4 0.0 copy-start.3
  7.4 0.6 copy-done.3
  8.0 0.1 pad_add_fusion.info
  8.1 5.6 %collective-permute-done = f32[6,4,8,128]{3,2,1,0:T(8,128)S(1)} collective-permute-done((f32[6,4,8,128]{3,2,1,0:T(8,128)S(1)}, f32[6,4,8,128]{3,2,1,0:T(8,128)S(1)}, u32[]{:S(2)}, u32[]{:S(2)}) %collective-permute-start) | collective-permute-done | bytes 98336 | tf_op jit(solution)/shard_map/ppermute | solution.py:503
  13.7 1.9 %all-gather.1 = f32[12,4,8,128]{3,2,1,0:T(8,128)S(1)} all-gather(f32[6,4,8,128]{3,2,1,0:T(8,128)S(1)} %collective-permute-done), channel_id=3, replica_groups=mesh['mirror'=2,'y'=4,'z'=16,'x'=4] {'mirror'}, dimensions={0}, use_global_device_ids=true | all-gather | bytes 294912 | tf_op jit(solution)/shard_map/all_gather | solution.py:503
  15.7 3.2 %shard_map.67 = (f32[3,5,8,256]{3,2,1,0:T(8,128)S(1)}, f32[8,256]{1,0:T(8,128)S(1)}, f32[4,8,256]{2,1,0:T(8,128)S(1)}, f32[5,8,256]{2,1,0:T(8,128)S(1)}, f32[4,8,256]{2,1,0:T(8,128)S(1)}) custom-call(s32[4]{0:T(128)S(1)} %pad_add_fusion.info, f32[6,4,8,128]{3,2,1,0:T(8,128)S(1)} %all-gather.own, f32[6,4,8,128]{3,2,1,0:T(8,128)S(1)} %get-tuple-element.30.below, ...), custom_call_target="tpu_custom_call" | custom-call | tf_op jit(solution)/shard_map/pallas_call | solution.py:455
  18.9 1.3 %collective-permute-start.1 = (f32[8,256]{1,0:T(8,128)S(1)}, f32[8,256]{1,0:T(8,128)S(1)}, u32[]{:S(2)}, u32[]{:S(2)}) collective-permute-start(f32[8,256]{1,0:T(8,128)S(1)} %get-tuple-element.20), channel_id=1, source_target_pairs={{0,4},{1,5},{2,6},{3,7},{4,8},{5,9},{6,10},{7,11},{8,12},{9,13},{1... | collective-permute-start | bytes 24584 | tf_op jit(solution)/shard_map/ppermute | solution.py:510
  20.2 1.3 %collective-permute-done.1 = f32[8,256]{1,0:T(8,128)S(1)} collective-permute-done((f32[8,256]{1,0:T(8,128)S(1)}, f32[8,256]{1,0:T(8,128)S(1)}, u32[]{:S(2)}, u32[]{:S(2)}) %collective-permute-start.1) | collective-permute-done | bytes 8224 | tf_op jit(solution)/shard_map/ppermute | solution.py:510
  21.6 9.1 %all_to_all.15.gathered = f32[8,16,256]{2,1,0:T(8,128)S(1)} all-to-all(f32[8,16,256]{2,1,0:T(8,128)S(1)} %broadcast_in_dim.16), channel_id=1, replica_groups=mesh['mirror'=2,'y'=4,'z'=16,'x'=4] {'mirror','x'}, dimensions={0} | all-to-all | bytes 262144 | tf_op jit(solution)/shard_map/all_to_all | solution.py:512
  30.7 1.9 %shard_map.68 = (f32[3,4,8,128]{3,2,1,0:T(8,128)S(1)}, f32[3,4,8,128]{3,2,1,0:T(8,128)S(1)}, f32[3,8,128]{2,1,0:T(8,128)S(1)}, f32[4,8,128]{2,1,0:T(8,128)S(1)}, f32[16,1,128]{2,1,0:T(1,128)S(1)}) custom-call(s32[4]{0:T(128)S(1)} %pad_add_fusion.info, f32[3,5,8,256]{3,2,1,0:T(8,128)S(1)} %get-tuple-element.16.smooth, ...), custom_call_target="tpu_custom_call" | custom-call | tf_op jit(solution)/shard_map/pallas_call | solution.py:455
  32.6 22.5 %all_to_all.16 = f32[16,1,128]{2,1,0:T(1,128)S(1)} all-to-all(f32[16,1,128]{2,1,0:T(1,128)S(1)} %get-tuple-element.21), channel_id=1, replica_groups=mesh['mirror'=2,'y'=4,'z'=16,'x'=4] {'y','x'}, dimensions={0} | all-to-all | bytes 16384 | tf_op jit(solution)/shard_map/all_to_all | solution.py:518
  55.1 0.0 copy-start.1
  55.1 0.6 broadcast_in_dim.17
  55.7 7.9 %all-to-all-start.2 = ((f32[16,1,128]{2,1,0:T(1,128)}), f32[16,1,128]{2,1,0:T(1,128)S(1)}, u32[]{:S(2)}, u32[]{:S(2)}) async-start(f32[16,1,128]{2,1,0:T(1,128)} %broadcast_in_dim.17), calls=%async_computation.2 | async-start | bytes 16384 | tf_op jit(solution)/shard_map/all_to_all | solution.py:521
  63.7 2.5 %collective-permute-start.2 = (f32[3,8,128]{2,1,0:T(8,128)S(1)}, f32[3,8,128]{2,1,0:T(8,128)S(1)}, u32[]{:S(2)}, u32[]{:S(2)}) collective-permute-start(f32[3,8,128]{2,1,0:T(8,128)S(1)} %get-tuple-element.24), channel_id=1, source_target_pairs={{0,1},{1,2},{2,3},{3,4},{4,5},{5,6},{6,7},{7,8},{8,9},{9,10},{10,1... | collective-permute-start | bytes 36872 | tf_op jit(solution)/shard_map/ppermute | solution.py:468
  66.2 3.1 %collective-permute-done.2.arrived = f32[3,8,128]{2,1,0:T(8,128)S(1)} collective-permute-done((f32[3,8,128]{2,1,0:T(8,128)S(1)}, f32[3,8,128]{2,1,0:T(8,128)S(1)}, u32[]{:S(2)}, u32[]{:S(2)}) %collective-permute-start.2) | collective-permute-done | bytes 12320 | tf_op jit(solution)/shard_map/ppermute | solution.py:468
  69.2 6.8 %all-to-all-done.2.totals = f32[16,1,128]{2,1,0:T(1,128)S(1)} async-done(((f32[16,1,128]{2,1,0:T(1,128)}), f32[16,1,128]{2,1,0:T(1,128)S(1)}, u32[]{:S(2)}, u32[]{:S(2)}) %all-to-all-start.2) | async-done | bytes 8224 | tf_op jit(solution)/shard_map/all_to_all | solution.py:521
  76.0 0.0 copy-done.1
  76.0 0.7 shard_map.69
  (6 shorter events, 0.1 us)
Async XLA Ops:
  0.6 0.7 copy-start
  1.4 0.7 copy-start.2
  4.0 9.8 %collective-permute-start = (f32[6,4,8,128]{3,2,1,0:T(8,128)S(1)}, f32[6,4,8,128]{3,2,1,0:T(8,128)S(1)}, u32[]{:S(2)}, u32[]{:S(2)}) collective-permute-start(f32[6,4,8,128]{3,2,1,0:T(8,128)S(1)} %all-gather.own), channel_id=1, source_target_pairs={{0,1},{1,2},{2,3},{3,4},{4,5},{5,6},{6,7},{7,8},{8,9},{9,10},{10,1... | collective-permute-start | bytes 294920 | tf_op jit(solution)/shard_map/ppermute | solution.py:503
  7.4 0.7 copy-start.3
  18.9 2.6 %collective-permute-start.1 = (f32[8,256]{1,0:T(8,128)S(1)}, f32[8,256]{1,0:T(8,128)S(1)}, u32[]{:S(2)}, u32[]{:S(2)}) collective-permute-start(f32[8,256]{1,0:T(8,128)S(1)} %get-tuple-element.20), channel_id=1, source_target_pairs={{0,4},{1,5},{2,6},{3,7},{4,8},{5,9},{6,10},{7,11},{8,12},{9,13},{1... | collective-permute-start | bytes 24584 | tf_op jit(solution)/shard_map/ppermute | solution.py:510
  55.1 20.9 %copy-start.1 = (s32[1,4,8,128]{3,2,1,0:T(8,128)S(1)}, s32[1,4,8,128]{3,2,1,0:T(8,128)}, u32[]{:S(2)}) copy-start(s32[1,4,8,128]{3,2,1,0:T(8,128)} %load.1) | copy-start | bytes 49156
  55.7 20.3 %all-to-all-start.2 = ((f32[16,1,128]{2,1,0:T(1,128)}), f32[16,1,128]{2,1,0:T(1,128)S(1)}, u32[]{:S(2)}, u32[]{:S(2)}) async-start(f32[16,1,128]{2,1,0:T(1,128)} %broadcast_in_dim.17), calls=%async_computation.2 | async-start | bytes 16384 | tf_op jit(solution)/shard_map/all_to_all | solution.py:521
  63.7 5.6 %collective-permute-start.2 = (f32[3,8,128]{2,1,0:T(8,128)S(1)}, f32[3,8,128]{2,1,0:T(8,128)S(1)}, u32[]{:S(2)}, u32[]{:S(2)}) collective-permute-start(f32[3,8,128]{2,1,0:T(8,128)S(1)} %get-tuple-element.24), channel_id=1, source_target_pairs={{0,1},{1,2},{2,3},{3,4},{4,5},{5,6},{6,7},{7,8},{8,9},{9,10},{10,1... | collective-permute-start | bytes 36872 | tf_op jit(solution)/shard_map/ppermute | solution.py:468

commit v6 on v5

--- a/solution.py
+++ b/solution.py
@@ -63,22 +63,68 @@
     return stiffness
 
 
+STRETCH = ((1, 0), (2, 1), (4, 2))
+SHEAR = (((2, 0), (1, 1)), ((4, 0), (1, 2)), ((4, 1), (2, 2)))
+BEND = (((5, 0), (6, 1)), ((3, 0), (6, 2)), ((3, 1), (5, 2)))
+TWIST = ((6, 0), (5, 1), (3, 2))
+WARP = ((7, 0), (7, 1), (7, 2))
+
+
 @functools.lru_cache(None)
-def mode_matrix():
+def mode_entries():
     one = np.array([[1.0, 1.0], [-1.0, 1.0]])
     signs = np.kron(np.kron(one, one), one)
     spread = np.kron(signs, np.eye(3)) / 8.0
     matrix = spread @ element_matrix() @ spread.T
-    table = {}
-    for row in range(24):
-        entries = [
-            ((col // 3, col % 3), float(matrix[row, col]))
-            for col in range(24)
-            if abs(matrix[row, col]) > 1e-12
-        ]
-        if entries:
-            table[(row // 3, row % 3)] = entries
-    return table
+
+    def at(row, col):
+        return matrix[3 * row[0] + row[1], 3 * col[0] + col[1]]
+
+    names = {
+        "stretch": (at(STRETCH[0], STRETCH[0]), at(STRETCH[0], STRETCH[1])),
+        "shear": at(SHEAR[0][0], SHEAR[0][1]),
+        "bend": (at(BEND[0][0], BEND[0][0]), at(BEND[0][0], BEND[0][1])),
+        "twist": at(TWIST[0], TWIST[1]),
+        "warp": at(WARP[0], WARP[0]),
+    }
+    again = np.zeros((24, 24))
+
+    def put(modes, diagonal, other):
+        for row in modes:
+            for col in modes:
+                again[3 * row[0] + row[1], 3 * col[0] + col[1]] = diagonal if row == col else other
+
+    put(STRETCH, *names["stretch"])
+    put(TWIST, 2.0 * names["twist"], names["twist"])
+    for pair in SHEAR:
+        put(pair, names["shear"], names["shear"])
+    for pair in BEND:
+        put(pair, *names["bend"])
+    for mode in WARP:
+        put((mode,), names["warp"], 0.0)
+    assert np.allclose(matrix, again, rtol=0.0, atol=1e-13)
+    return names
+
+
+def mode_forces(modes, scale):
+    entries = mode_entries()
+    forces = {}
+    diagonal, other = entries["stretch"]
+    shared = (modes[STRETCH[0]] + modes[STRETCH[1]] + modes[STRETCH[2]]) * np.float32(other * scale)
+    for mode in STRETCH:
+        forces[mode] = shared + modes[mode] * np.float32((diagonal - other) * scale)
+    for first, second in SHEAR:
+        forces[first] = forces[second] = (modes[first] + modes[second]) * np.float32(entries["shear"] * scale)
+    diagonal, other = np.float32(entries["bend"][0] * scale), np.float32(entries["bend"][1] * scale)
+    for first, second in BEND:
+        forces[first] = modes[first] * diagonal + modes[second] * other
+        forces[second] = modes[second] * diagonal + modes[first] * other
+    shared = modes[TWIST[0]] + modes[TWIST[1]] + modes[TWIST[2]]
+    for mode in TWIST:
+        forces[mode] = (shared + modes[mode]) * np.float32(entries["twist"] * scale)
+    for mode in WARP:
+        forces[mode] = modes[mode] * np.float32(entries["warp"] * scale)
+    return forces
 
 
 @functools.lru_cache(None)
@@ -152,25 +198,25 @@
                 if m > 0:
                     modes[(m, c)] = high[m][c] + low[m][c]
                 modes[(4 + m, c)] = high[m][c] - low[m][c]
-        forces = {}
-        for row, entries in mode_matrix().items():
-            total = None
-            for col, entry in entries:
-                term = modes[col] * np.float32(entry * scale)
-                total = term if total is None else total + term
-            forces[row] = total
+        forces = mode_forces(modes, scale)
         energy = None
         if with_energy:
-            for row, force in forces.items():
-                term = modes[row] * force
+            terms = [forces[first] * (modes[first] + modes[second]) for first, second in SHEAR]
+            paired = [mode for pair in SHEAR for mode in pair]
+            terms += [forces[mode] * modes[mode] for mode in forces if mode not in paired]
+            for term in terms:
                 energy = term if energy is None else energy + term
+        for first, second in SHEAR:
+            forces[first] = forces[second] = modulus * forces[first]
+        for mode in STRETCH + TWIST + WARP + BEND[0] + BEND[1] + BEND[2]:
+            forces[mode] = modulus * forces[mode]
         on_low = [[None] * 3 for _ in range(4)]
         on_high = [[None] * 3 for _ in range(4)]
         for m in range(4):
             for c in range(3):
-                change = modulus * forces[(4 + m, c)]
+                change = forces[(4 + m, c)]
                 if m > 0:
-                    total = modulus * forces[(m, c)]
+                    total = forces[(m, c)]
                     on_low[m][c] = total - change
                     on_high[m][c] = total + change
                 else:

time: 77.3 us -> 77.6 us (level)
  no operation moved by 1% of the time
where the time goes in v6:
time: 77.6 us; the launch traced here: 77 us
  blocking collectives  35.4 us (46%)
  waiting for transfers between devices  16.8 us (22%)
  starting transfers between devices  15.1 us (19%)
  Pallas kernels  6.18 us (8%)
  local copies, waits for them, and re-layouts  2 us (3%)
  other arithmetic  0.85 us (1%)
    all_to_all x1, blocking collectives, on_device(): sums = lax.all_to_all(sums, ('y', 'x'), 0, 0)  22.5 us
    all_to_all x1, blocking collectives, on_device(): gathered = lax.all_to_all(sent, ('mirror', 'x'), 0, 0)  9.1 us
    all_to_all x1, starting transfers between devices, on_device(): sums = lax.all_to_all(sums, 'z', 0, 0)  7.92 us
    all_to_all x1, waiting for transfers between devices, on_device(): sums = lax.all_to_all(sums, 'z', 0, 0)  6.78 us
    pallas_call x3, Pallas kernels, call(): pl.pallas_call(kernel, out_shape=[jax.ShapeDtypeStruct(shape, jnp.float32...  6.18 us
    ppermute x1, waiting for transfers between devices, on_device(): both = lax.all_gather(lax.ppermute(own, ('mirror',) + SLAB, near), 'mirror')  5.63 us
    ppermute x1, starting transfers between devices, on_device(): both = lax.all_gather(lax.ppermute(own, ('mirror',) + SLAB, near), 'mirror')  3.39 us
    ppermute x1, waiting for transfers between devices, shifted(): return lax.ppermute(array, axis, pairs)  3.09 us
  transfers between devices with their start and end apart: 4, of which 4 were waited for; matrix products, arithmetic and copies ran while one was open for 0% of the time, Pallas kernels for 0%

profile of v6, /device:TPU:2, one launch (start us, length us, event | category | flops | bytes accessed | tf_op | source)
XLA Modules:
  0.0 77.0 jit_solution(14397064429679464867)
XLA Ops:
  0.6 0.0 copy-start
  0.6 0.7 convert_element_type.6
  1.4 0.0 copy-done
  1.4 0.0 copy-start.2
  1.4 0.7 copy-done.2
  2.1 1.9 %all-gather.own = f32[6,4,8,128]{3,2,1,0:T(8,128)S(1)} all-gather(f32[3,4,8,128]{3,2,1,0:T(8,128)S(1)} %pad_maximum_fusion), channel_id=2, replica_groups=mesh['mirror'=2,'y'=4,'z'=16,'x'=4] {'mirror'}, dimensions={0}, use_global_device_ids=true | all-gather | bytes 147456 | tf_op jit(solution)/shard_map/all_gather | solution.py:546
  4.0 3.4 %collective-permute-start = (f32[6,4,8,128]{3,2,1,0:T(8,128)S(1)}, f32[6,4,8,128]{3,2,1,0:T(8,128)S(1)}, u32[]{:S(2)}, u32[]{:S(2)}) collective-permute-start(f32[6,4,8,128]{3,2,1,0:T(8,128)S(1)} %all-gather.own), channel_id=1, source_target_pairs={{0,1},{1,2},{2,3},{3,4},{4,5},{5,6},{6,7},{7,8},{8,9},{9,10},{10,1... | collective-permute-start | bytes 294920 | tf_op jit(solution)/shard_map/ppermute | solution.py:549
  7.4 0.0 copy-start.3
  7.4 0.6 copy-done.3
  8.0 0.1 pad_add_fusion.info
  8.1 5.6 %collective-permute-done = f32[6,4,8,128]{3,2,1,0:T(8,128)S(1)} collective-permute-done((f32[6,4,8,128]{3,2,1,0:T(8,128)S(1)}, f32[6,4,8,128]{3,2,1,0:T(8,128)S(1)}, u32[]{:S(2)}, u32[]{:S(2)}) %collective-permute-start) | collective-permute-done | bytes 98336 | tf_op jit(solution)/shard_map/ppermute | solution.py:549
  13.7 1.9 %all-gather.1 = f32[12,4,8,128]{3,2,1,0:T(8,128)S(1)} all-gather(f32[6,4,8,128]{3,2,1,0:T(8,128)S(1)} %collective-permute-done), channel_id=3, replica_groups=mesh['mirror'=2,'y'=4,'z'=16,'x'=4] {'mirror'}, dimensions={0}, use_global_device_ids=true | all-gather | bytes 294912 | tf_op jit(solution)/shard_map/all_gather | solution.py:549
  15.7 3.2 %shard_map.67 = (f32[3,5,8,256]{3,2,1,0:T(8,128)S(1)}, f32[8,256]{1,0:T(8,128)S(1)}, f32[4,8,256]{2,1,0:T(8,128)S(1)}, f32[5,8,256]{2,1,0:T(8,128)S(1)}, f32[4,8,256]{2,1,0:T(8,128)S(1)}) custom-call(s32[4]{0:T(128)S(1)} %pad_add_fusion.info, f32[6,4,8,128]{3,2,1,0:T(8,128)S(1)} %all-gather.own, f32[6,4,8,128]{3,2,1,0:T(8,128)S(1)} %get-tuple-element.30.below, ...), custom_call_target="tpu_custom_call" | custom-call | tf_op jit(solution)/shard_map/pallas_call | solution.py:501
  18.8 1.3 %collective-permute-start.1 = (f32[8,256]{1,0:T(8,128)S(1)}, f32[8,256]{1,0:T(8,128)S(1)}, u32[]{:S(2)}, u32[]{:S(2)}) collective-permute-start(f32[8,256]{1,0:T(8,128)S(1)} %get-tuple-element.20), channel_id=1, source_target_pairs={{0,4},{1,5},{2,6},{3,7},{4,8},{5,9},{6,10},{7,11},{8,12},{9,13},{1... | collective-permute-start | bytes 24584 | tf_op jit(solution)/shard_map/ppermute | solution.py:556
  20.1 1.3 %collective-permute-done.1 = f32[8,256]{1,0:T(8,128)S(1)} collective-permute-done((f32[8,256]{1,0:T(8,128)S(1)}, f32[8,256]{1,0:T(8,128)S(1)}, u32[]{:S(2)}, u32[]{:S(2)}) %collective-permute-start.1) | collective-permute-done | bytes 8224 | tf_op jit(solution)/shard_map/ppermute | solution.py:556
  21.5 9.1 %all_to_all.15.gathered = f32[8,16,256]{2,1,0:T(8,128)S(1)} all-to-all(f32[8,16,256]{2,1,0:T(8,128)S(1)} %broadcast_in_dim.16), channel_id=1, replica_groups=mesh['mirror'=2,'y'=4,'z'=16,'x'=4] {'mirror','x'}, dimensions={0} | all-to-all | bytes 262144 | tf_op jit(solution)/shard_map/all_to_all | solution.py:558
  30.6 2.3 %shard_map.68 = (f32[3,4,8,128]{3,2,1,0:T(8,128)S(1)}, f32[3,4,8,128]{3,2,1,0:T(8,128)S(1)}, f32[3,8,128]{2,1,0:T(8,128)S(1)}, f32[4,8,128]{2,1,0:T(8,128)S(1)}, f32[16,1,128]{2,1,0:T(1,128)S(1)}) custom-call(s32[4]{0:T(128)S(1)} %pad_add_fusion.info, f32[3,5,8,256]{3,2,1,0:T(8,128)S(1)} %get-tuple-element.16.smooth, ...), custom_call_target="tpu_custom_call" | custom-call | tf_op jit(solution)/shard_map/pallas_call | solution.py:501
  32.9 22.5 %all_to_all.16 = f32[16,1,128]{2,1,0:T(1,128)S(1)} all-to-all(f32[16,1,128]{2,1,0:T(1,128)S(1)} %get-tuple-element.21), channel_id=1, replica_groups=mesh['mirror'=2,'y'=4,'z'=16,'x'=4] {'y','x'}, dimensions={0} | all-to-all | bytes 16384 | tf_op jit(solution)/shard_map/all_to_all | solution.py:564
  55.4 0.0 copy-start.1
  55.4 0.6 broadcast_in_dim.17
  56.0 7.9 %all-to-all-start.2 = ((f32[16,1,128]{2,1,0:T(1,128)}), f32[16,1,128]{2,1,0:T(1,128)S(1)}, u32[]{:S(2)}, u32[]{:S(2)}) async-start(f32[16,1,128]{2,1,0:T(1,128)} %broadcast_in_dim.17), calls=%async_computation.2 | async-start | bytes 16384 | tf_op jit(solution)/shard_map/all_to_all | solution.py:567
  63.9 2.5 %collective-permute-start.2 = (f32[3,8,128]{2,1,0:T(8,128)S(1)}, f32[3,8,128]{2,1,0:T(8,128)S(1)}, u32[]{:S(2)}, u32[]{:S(2)}) collective-permute-start(f32[3,8,128]{2,1,0:T(8,128)S(1)} %get-tuple-element.24), channel_id=1, source_target_pairs={{0,1},{1,2},{2,3},{3,4},{4,5},{5,6},{6,7},{7,8},{8,9},{9,10},{10,1... | collective-permute-start | bytes 36872 | tf_op jit(solution)/shard_map/ppermute | solution.py:514
  66.4 3.1 %collective-permute-done.2.arrived = f32[3,8,128]{2,1,0:T(8,128)S(1)} collective-permute-done((f32[3,8,128]{2,1,0:T(8,128)S(1)}, f32[3,8,128]{2,1,0:T(8,128)S(1)}, u32[]{:S(2)}, u32[]{:S(2)}) %collective-permute-start.2) | collective-permute-done | bytes 12320 | tf_op jit(solution)/shard_map/ppermute | solution.py:514
  69.5 6.8 %all-to-all-done.2.totals = f32[16,1,128]{2,1,0:T(1,128)S(1)} async-done(((f32[16,1,128]{2,1,0:T(1,128)}), f32[16,1,128]{2,1,0:T(1,128)S(1)}, u32[]{:S(2)}, u32[]{:S(2)}) %all-to-all-start.2) | async-done | bytes 8224 | tf_op jit(solution)/shard_map/all_to_all | solution.py:567
  76.3 0.0 copy-done.1
  76.3 0.7 shard_map.69
  (6 shorter events, 0.1 us)
Async XLA Ops:
  0.6 0.7 copy-start
  1.4 0.7 copy-start.2
  4.0 9.8 %collective-permute-start = (f32[6,4,8,128]{3,2,1,0:T(8,128)S(1)}, f32[6,4,8,128]{3,2,1,0:T(8,128)S(1)}, u32[]{:S(2)}, u32[]{:S(2)}) collective-permute-start(f32[6,4,8,128]{3,2,1,0:T(8,128)S(1)} %all-gather.own), channel_id=1, source_target_pairs={{0,1},{1,2},{2,3},{3,4},{4,5},{5,6},{6,7},{7,8},{8,9},{9,10},{10,1... | collective-permute-start | bytes 294920 | tf_op jit(solution)/shard_map/ppermute | solution.py:549
  7.4 0.7 copy-start.3
  18.8 2.6 %collective-permute-start.1 = (f32[8,256]{1,0:T(8,128)S(1)}, f32[8,256]{1,0:T(8,128)S(1)}, u32[]{:S(2)}, u32[]{:S(2)}) collective-permute-start(f32[8,256]{1,0:T(8,128)S(1)} %get-tuple-element.20), channel_id=1, source_target_pairs={{0,4},{1,5},{2,6},{3,7},{4,8},{5,9},{6,10},{7,11},{8,12},{9,13},{1... | collective-permute-start | bytes 24584 | tf_op jit(solution)/shard_map/ppermute | solution.py:556
  55.4 20.9 %copy-start.1 = (s32[1,4,8,128]{3,2,1,0:T(8,128)S(1)}, s32[1,4,8,128]{3,2,1,0:T(8,128)}, u32[]{:S(2)}) copy-start(s32[1,4,8,128]{3,2,1,0:T(8,128)} %load.1) | copy-start | bytes 49156
  56.0 20.3 %all-to-all-start.2 = ((f32[16,1,128]{2,1,0:T(1,128)}), f32[16,1,128]{2,1,0:T(1,128)S(1)}, u32[]{:S(2)}, u32[]{:S(2)}) async-start(f32[16,1,128]{2,1,0:T(1,128)} %broadcast_in_dim.17), calls=%async_computation.2 | async-start | bytes 16384 | tf_op jit(solution)/shard_map/all_to_all | solution.py:567
  63.9 5.6 %collective-permute-start.2 = (f32[3,8,128]{2,1,0:T(8,128)S(1)}, f32[3,8,128]{2,1,0:T(8,128)S(1)}, u32[]{:S(2)}, u32[]{:S(2)}) collective-permute-start(f32[3,8,128]{2,1,0:T(8,128)S(1)} %get-tuple-element.24), channel_id=1, source_target_pairs={{0,1},{1,2},{2,3},{3,4},{4,5},{5,6},{6,7},{7,8},{8,9},{9,10},{10,1... | collective-permute-start | bytes 36872 | tf_op jit(solution)/shard_map/ppermute | solution.py:514

commit v7 on v6

--- a/solution.py
+++ b/solution.py
@@ -127,6 +127,22 @@
     return forces
 
 
+def weighted_forces(modes, modulus, scale, with_energy):
+    forces = mode_forces(modes, scale)
+    energy = None
+    if with_energy:
+        terms = [forces[first] * (modes[first] + modes[second]) for first, second in SHEAR]
+        paired = [mode for pair in SHEAR for mode in pair]
+        terms += [forces[mode] * modes[mode] for mode in forces if mode not in paired]
+        for term in terms:
+            energy = term if energy is None else energy + term
+    for first, second in SHEAR:
+        forces[first] = forces[second] = modulus * forces[first]
+    for mode in STRETCH + TWIST + WARP + BEND[0] + BEND[1] + BEND[2]:
+        forces[mode] = modulus * forces[mode]
+    return forces, energy
+
+
 @functools.lru_cache(None)
 def row_total():
     totals = np.abs(element_matrix()).sum(axis=1)
@@ -198,18 +214,7 @@
                 if m > 0:
                     modes[(m, c)] = high[m][c] + low[m][c]
                 modes[(4 + m, c)] = high[m][c] - low[m][c]
-        forces = mode_forces(modes, scale)
-        energy = None
-        if with_energy:
-            terms = [forces[first] * (modes[first] + modes[second]) for first, second in SHEAR]
-            paired = [mode for pair in SHEAR for mode in pair]
-            terms += [forces[mode] * modes[mode] for mode in forces if mode not in paired]
-            for term in terms:
-                energy = term if energy is None else energy + term
-        for first, second in SHEAR:
-            forces[first] = forces[second] = modulus * forces[first]
-        for mode in STRETCH + TWIST + WARP + BEND[0] + BEND[1] + BEND[2]:
-            forces[mode] = modulus * forces[mode]
+        forces, energy = weighted_forces(modes, modulus, scale, with_energy)
         on_low = [[None] * 3 for _ in range(4)]
         on_high = [[None] * 3 for _ in range(4)]
         for m in range(4):
@@ -246,6 +251,60 @@
     return lambda: plane.backward(nested(carry[12:]))
 
 
+class CoarseBlock:
+    def __init__(self, planes):
+        self.rows = 2 * planes
+        shape = (self.rows, COLS)
+        lane = lax.broadcasted_iota(jnp.int32, shape, 1)
+        self.row = lax.broadcasted_iota(jnp.int32, shape, 0)
+        self.odd_lane = lane % 2 == 1
+        ahead = {0: (1, self.row % 2 == 0), 1: (2, self.row < self.rows - 2)}
+        behind = {0: (1, self.row % 2 == 1), 1: (2, self.row >= 2)}
+        self.ahead = {"y": (0,) + ahead[0], "z": (0,) + ahead[1], "x": (1, 4, lane < COLS - 4)}
+        self.behind = {"y": (0,) + behind[0], "z": (0,) + behind[1], "x": (1, 4, lane >= 4)}
+
+    def next(self, v, along):
+        axis, by, mask = self.ahead[along]
+        return jnp.where(mask, pltpu.roll(v, v.shape[axis] - by, axis), 0.0)
+
+    def prev(self, v, along):
+        axis, by, mask = self.behind[along]
+        return jnp.where(mask, pltpu.roll(v, by, axis), 0.0)
+
+    def corner_sum(self, v):
+        v = v + self.prev(v, "x")
+        return v + self.prev(v, "y")
+
+    def apply(self, comps, modulus, scale):
+        modes = {}
+        for c, v in enumerate(comps):
+            parts = {0: v}
+            for bit, along in enumerate("xyz"):
+                split = {}
+                for number, w in parts.items():
+                    ahead = self.next(w, along)
+                    split[number] = ahead + w
+                    split[number + (1 << bit)] = ahead - w
+                parts = split
+            for number, w in parts.items():
+                modes[(number, c)] = w
+        forces, _ = weighted_forces(modes, modulus, scale, False)
+        result = []
+        for c in range(3):
+            parts = {number: forces.get((number, c)) for number in range(8)}
+            for bit, along in reversed(list(enumerate("xyz"))):
+                joined = {}
+                for number in range(1 << bit):
+                    total, change = parts[number], parts[number + (1 << bit)]
+                    if total is None:
+                        joined[number] = self.prev(change, along) - change
+                    else:
+                        joined[number] = (total - change) + self.prev(total + change, along)
+                parts = joined
+            result.append(parts[0])
+        return result
+
+
 class Groups:
     def __init__(self):
         lane = lax.broadcasted_iota(jnp.int32, (ROWS, COLS), 1)
@@ -356,14 +415,17 @@
     rest = apply_planes(plane, 3, 6, load, modulus_at, 1.0, consume_left)()
 
     odd = groups.lane_bits[0]
-    packed = groups.both((mod[4] + mod[5]) + (mod[6] + mod[7])) * np.float32(1.0 / 64.0)
+    fields = []
     for c in range(3):
         for k in range(5):
             smooth[c, k] = x[c, k + 3]
         mine = groups.both((left[c, 0] + left[c, 1]) + (left[c, 2] + left[c, 3]))
         passed = groups.both(free[7] * -rest[c])
-        packed = jnp.where(groups.row_in == c, jnp.where(odd, passed, mine), packed)
-    coarse[...] = packed
+        fields.append(jnp.where(odd, passed, mine))
+    fields.append(groups.both((mod[4] + mod[5]) + (mod[6] + mod[7])) * np.float32(1.0 / 64.0))
+    for f, field in enumerate(fields):
+        coarse[2 * f : 2 * f + 1] = field[0:1]
+        coarse[2 * f + 1 : 2 * f + 2] = field[4:5]
     for k in range(5):
         free_out[k] = free[k + 3]
     for k in range(OWN):
@@ -371,74 +433,60 @@
 
 
 def correct_kernel(
-    slabs, info, smooth, dens, free, right, gathered, moved, image, passed, slope, sums, mod, x, d, w, target, p, own_mod, energy
+    slabs, info, smooth, dens, free, right, gathered, moved, image, passed, slope, sums, window, d, xc, x, p, own_mod, energy
 ):
-    coarse_plane, plane, groups = Plane(4), Plane(1), Groups()
+    plane, block = Plane(1), CoarseBlock(8)
     slab, mirror, sweep_count = info[0], info[1], info[3]
     offset = slab % 4
     upper_rows = lax.broadcasted_iota(jnp.int32, (ROWS, COLS), 0) >= 4
-    odd = groups.lane_bits[0]
-    groups_of = [(k, ROWS) for k in range(4)] + [(k, 0) for k in range(4)] + [(4 + k, ROWS) for k in range(4)]
-
-    def unpack(field, j):
-        block, row = groups_of[j]
-        first = gathered[block, row + field : row + field + 1]
-        second = gathered[block, row + 4 + field : row + 5 + field]
-        return jnp.where(upper_rows, jnp.broadcast_to(second, (ROWS, COLS)), jnp.broadcast_to(first, (ROWS, COLS)))
+    sources = [(k, ROWS) for k in range(4)] + [(k, 0) for k in range(4)] + [(4 + k, ROWS) for k in range(4)]
 
     for lead in range(4):
 
         @pl.when(offset == lead)
         def _(lead=lead):
             for q in range(9):
-                mod[q] = unpack(3, lead + q)
-            for c in range(3):
-                lower = None
-                for q in range(9):
-                    value = unpack(c, lead + q)
-                    if q > 0:
-                        part = jnp.where(odd, pltpu.roll(value, 1, 1), value)
-                        target[c, q - 1] = part + jnp.where(odd, lower, pltpu.roll(lower, COLS - 1, 1))
-                    lower = value
-
-    summed = coarse_plane.corner_sum(mod[0])
-    for q in range(8):
-        lower, summed = summed, coarse_plane.corner_sum(mod[q + 1])
-        scaling = np.float32(4.0 * row_total()) * (lower + summed)
-        at = slab - 3 + q
-        inside = ((at >= 0) & (at < slabs)).astype(jnp.float32)
-        inverse = inside / jnp.where(scaling > 0.0, scaling, 1.0)
-        w[q] = inverse
-        for c in range(3):
-            start = target[c, q] * (inverse * np.float32(1.0 / CENTRE))
-            x[c, q] = start
-            d[c, q] = start
+                source, row = sources[lead + q]
+                for f in range(4):
+                    window[f, 2 * q : 2 * q + 2] = gathered[source, row + 2 * f : row + 2 * f + 2]
+
+    modulus = window[3, 2:18]
+    scaling = block.corner_sum(window[3, 0:16]) + block.corner_sum(modulus)
+    scaling = np.float32(4.0 * row_total()) * scaling
+    at = slab - 3 + block.row // 2
+    inside = ((at >= 0) & (at < slabs)).astype(jnp.float32)
+    inverse = inside / jnp.where(scaling > 0.0, scaling, 1.0)
+    targets = []
+    for c in range(3):
+        lower, value = window[c, 0:16], window[c, 2:18]
+        part = jnp.where(block.odd_lane, pltpu.roll(value, 1, 1), value)
+        target = part + jnp.where(block.odd_lane, lower, pltpu.roll(lower, COLS - 1, 1))
+        targets.append(target)
+        start = target * (inverse * np.float32(1.0 / CENTRE))
+        xc[c] = start
+        d[c] = start
 
     for k, (keep, add) in enumerate(chebyshev_factors(), 1):
 
         @pl.when(k < sweep_count)
         def _(k=k, keep=keep, add=add):
-            def consume(q, forces, _energy):
-                weight = w[q] * np.float32(add)
-                for c in range(3):
-                    update = np.float32(keep) * d[c, q] + weight * (target[c, q] - forces[c])
-                    d[c, q] = update
-                    x[c, q] = x[c, q] + update
-
-            apply_planes(
-                coarse_plane,
-                k - 1,
-                7 - k,
-                lambda q: [x[c, q] for c in range(3)],
-                lambda q: mod[q + 1],
-                4.0,
-                consume,
-            )
-
+            now = [xc[c] for c in range(3)]
+            forces = block.apply(now, modulus, 4.0)
+            weight = inverse * np.float32(add)
+            for c in range(3):
+                update = np.float32(keep) * d[c] + weight * (targets[c] - forces[c])
+                d[c] = update
+                xc[c] = now[c] + update
+
+    def prolonged(c, q):
+        first = jnp.broadcast_to(xc[c, 2 * q : 2 * q + 1], (ROWS, COLS))
+        return jnp.where(upper_rows, jnp.broadcast_to(xc[c, 2 * q + 1 : 2 * q + 2], (ROWS, COLS)), first)
+
+    spread = [[prolonged(c, q) for q in (3, 4)] for c in range(3)]
     half = pl.ds(pl.multiple_of(mirror * 128, 128), 128)
     for k in range(5):
         for c in range(3):
-            p[c, k] = smooth[c, k] + free[k] * x[c, 4 if k == 4 else 3]
+            p[c, k] = smooth[c, k] + free[k] * spread[c][1 if k == 4 else 0]
     for k in range(OWN):
         own_mod[k] = modulus_of(dens[k])
 
@@ -527,13 +575,13 @@
 
 def run_correct(slabs, group, info, smooth, dens, free, right, gathered):
     plane = (ROWS, COLS)
-    field = (3, 8) + plane
+    block = (3, 16, COLS)
     part = (3, OWN, ROWS, 128)
     return call(
         functools.partial(correct_kernel, slabs),
         [part, part, (3, ROWS, 128), part[1:], (group, 1, 128)],
         [info, smooth, dens, free, right, gathered],
-        [(9,) + plane, field, field, (8,) + plane, field, (3, 5) + plane, (OWN,) + plane, (OWN,) + plane],
+        [(4, 24, COLS), block, block, (3, 5) + plane, (3, 5) + plane, (OWN,) + plane, (OWN,) + plane],
     )
 
 

time: 77.6 us -> 76.5 us (0.986)
  Pallas kernels: 6.18 us -> 5.11 us
    pallas_call x3, Pallas kernels: 6.18 us -> 5.11 us  [call(): pl.pallas_call(kernel, out_shape=[jax.ShapeDtypeStruct(shape, jnp.float32...]
where the time goes in v7:
time: 76.5 us; the launch traced here: 76 us
  blocking collectives  35.4 us (46%)
  waiting for transfers between devices  16.8 us (22%)
  starting transfers between devices  15.1 us (20%)
  Pallas kernels  5.11 us (7%)
  local copies, waits for them, and re-layouts  2 us (3%)
  other arithmetic  0.85 us (1%)
    all_to_all x1, blocking collectives, on_device(): sums = lax.all_to_all(sums, ('y', 'x'), 0, 0)  22.5 us
    all_to_all x1, blocking collectives, on_device(): gathered = lax.all_to_all(sent, ('mirror', 'x'), 0, 0)  9.1 us
    all_to_all x1, starting transfers between devices, on_device(): sums = lax.all_to_all(sums, 'z', 0, 0)  7.92 us
    all_to_all x1, waiting for transfers between devices, on_device(): sums = lax.all_to_all(sums, 'z', 0, 0)  6.78 us
    ppermute x1, waiting for transfers between devices, on_device(): both = lax.all_gather(lax.ppermute(own, ('mirror',) + SLAB, near), 'mirror')  5.63 us
    pallas_call x3, Pallas kernels, call(): pl.pallas_call(kernel, out_shape=[jax.ShapeDtypeStruct(shape, jnp.float32...  5.11 us
    ppermute x1, starting transfers between devices, on_device(): both = lax.all_gather(lax.ppermute(own, ('mirror',) + SLAB, near), 'mirror')  3.39 us
    ppermute x1, waiting for transfers between devices, shifted(): return lax.ppermute(array, axis, pairs)  3.09 us
  transfers between devices with their start and end apart: 4, of which 4 were waited for; matrix products, arithmetic and copies ran while one was open for 0% of the time, Pallas kernels for 0%

profile of v7, /device:TPU:2, one launch (start us, length us, event | category | flops | bytes accessed | tf_op | source)
XLA Modules:
  0.0 76.0 jit_solution(2748500517789638557)
XLA Ops:
  0.6 0.0 copy-start
  0.6 0.7 convert_element_type.6
  1.4 0.0 copy-done
  1.4 0.0 copy-start.2
  1.4 0.7 copy-done.2
  2.1 1.9 %all-gather.own = f32[6,4,8,128]{3,2,1,0:T(8,128)S(1)} all-gather(f32[3,4,8,128]{3,2,1,0:T(8,128)S(1)} %pad_maximum_fusion), channel_id=2, replica_groups=mesh['mirror'=2,'y'=4,'z'=16,'x'=4] {'mirror'}, dimensions={0}, use_global_device_ids=true | all-gather | bytes 147456 | tf_op jit(solution)/shard_map/all_gather | solution.py:594
  4.0 3.4 %collective-permute-start = (f32[6,4,8,128]{3,2,1,0:T(8,128)S(1)}, f32[6,4,8,128]{3,2,1,0:T(8,128)S(1)}, u32[]{:S(2)}, u32[]{:S(2)}) collective-permute-start(f32[6,4,8,128]{3,2,1,0:T(8,128)S(1)} %all-gather.own), channel_id=1, source_target_pairs={{0,1},{1,2},{2,3},{3,4},{4,5},{5,6},{6,7},{7,8},{8,9},{9,10},{10,1... | collective-permute-start | bytes 294920 | tf_op jit(solution)/shard_map/ppermute | solution.py:597
  7.4 0.0 copy-start.3
  7.4 0.6 copy-done.3
  8.0 0.1 pad_add_fusion.info
  8.1 5.6 %collective-permute-done = f32[6,4,8,128]{3,2,1,0:T(8,128)S(1)} collective-permute-done((f32[6,4,8,128]{3,2,1,0:T(8,128)S(1)}, f32[6,4,8,128]{3,2,1,0:T(8,128)S(1)}, u32[]{:S(2)}, u32[]{:S(2)}) %collective-permute-start) | collective-permute-done | bytes 98336 | tf_op jit(solution)/shard_map/ppermute | solution.py:597
  13.7 1.9 %all-gather.1 = f32[12,4,8,128]{3,2,1,0:T(8,128)S(1)} all-gather(f32[6,4,8,128]{3,2,1,0:T(8,128)S(1)} %collective-permute-done), channel_id=3, replica_groups=mesh['mirror'=2,'y'=4,'z'=16,'x'=4] {'mirror'}, dimensions={0}, use_global_device_ids=true | all-gather | bytes 294912 | tf_op jit(solution)/shard_map/all_gather | solution.py:597
  15.7 3.2 %shard_map.67 = (f32[3,5,8,256]{3,2,1,0:T(8,128)S(1)}, f32[8,256]{1,0:T(8,128)S(1)}, f32[4,8,256]{2,1,0:T(8,128)S(1)}, f32[5,8,256]{2,1,0:T(8,128)S(1)}, f32[4,8,256]{2,1,0:T(8,128)S(1)}) custom-call(s32[4]{0:T(128)S(1)} %pad_add_fusion.info, f32[6,4,8,128]{3,2,1,0:T(8,128)S(1)} %all-gather.own, f32[6,4,8,128]{3,2,1,0:T(8,128)S(1)} %get-tuple-element.30.below, ...), custom_call_target="tpu_custom_call" | custom-call | tf_op jit(solution)/shard_map/pallas_call | solution.py:549
  18.8 1.3 %collective-permute-start.1 = (f32[8,256]{1,0:T(8,128)S(1)}, f32[8,256]{1,0:T(8,128)S(1)}, u32[]{:S(2)}, u32[]{:S(2)}) collective-permute-start(f32[8,256]{1,0:T(8,128)S(1)} %get-tuple-element.20), channel_id=1, source_target_pairs={{0,4},{1,5},{2,6},{3,7},{4,8},{5,9},{6,10},{7,11},{8,12},{9,13},{1... | collective-permute-start | bytes 24584 | tf_op jit(solution)/shard_map/ppermute | solution.py:604
  20.1 1.3 %collective-permute-done.1 = f32[8,256]{1,0:T(8,128)S(1)} collective-permute-done((f32[8,256]{1,0:T(8,128)S(1)}, f32[8,256]{1,0:T(8,128)S(1)}, u32[]{:S(2)}, u32[]{:S(2)}) %collective-permute-start.1) | collective-permute-done | bytes 8224 | tf_op jit(solution)/shard_map/ppermute | solution.py:604
  21.5 9.1 %all_to_all.15.gathered = f32[8,16,256]{2,1,0:T(8,128)S(1)} all-to-all(f32[8,16,256]{2,1,0:T(8,128)S(1)} %broadcast_in_dim.16), channel_id=1, replica_groups=mesh['mirror'=2,'y'=4,'z'=16,'x'=4] {'mirror','x'}, dimensions={0} | all-to-all | bytes 262144 | tf_op jit(solution)/shard_map/all_to_all | solution.py:606
  30.6 1.2 %shard_map.68 = (f32[3,4,8,128]{3,2,1,0:T(8,128)S(1)}, f32[3,4,8,128]{3,2,1,0:T(8,128)S(1)}, f32[3,8,128]{2,1,0:T(8,128)S(1)}, f32[4,8,128]{2,1,0:T(8,128)S(1)}, f32[16,1,128]{2,1,0:T(1,128)S(1)}) custom-call(s32[4]{0:T(128)S(1)} %pad_add_fusion.info, f32[3,5,8,256]{3,2,1,0:T(8,128)S(1)} %get-tuple-element.16.smooth, ...), custom_call_target="tpu_custom_call" | custom-call | tf_op jit(solution)/shard_map/pallas_call | solution.py:549
  31.8 22.5 %all_to_all.16 = f32[16,1,128]{2,1,0:T(1,128)S(1)} all-to-all(f32[16,1,128]{2,1,0:T(1,128)S(1)} %get-tuple-element.21), channel_id=1, replica_groups=mesh['mirror'=2,'y'=4,'z'=16,'x'=4] {'y','x'}, dimensions={0} | all-to-all | bytes 16384 | tf_op jit(solution)/shard_map/all_to_all | solution.py:612
  54.3 0.0 copy-start.1
  54.3 0.6 broadcast_in_dim.17
  54.9 7.9 %all-to-all-start.2 = ((f32[16,1,128]{2,1,0:T(1,128)}), f32[16,1,128]{2,1,0:T(1,128)S(1)}, u32[]{:S(2)}, u32[]{:S(2)}) async-start(f32[16,1,128]{2,1,0:T(1,128)} %broadcast_in_dim.17), calls=%async_computation.2 | async-start | bytes 16384 | tf_op jit(solution)/shard_map/all_to_all | solution.py:615
  62.8 2.5 %collective-permute-start.2 = (f32[3,8,128]{2,1,0:T(8,128)S(1)}, f32[3,8,128]{2,1,0:T(8,128)S(1)}, u32[]{:S(2)}, u32[]{:S(2)}) collective-permute-start(f32[3,8,128]{2,1,0:T(8,128)S(1)} %get-tuple-element.24), channel_id=1, source_target_pairs={{0,1},{1,2},{2,3},{3,4},{4,5},{5,6},{6,7},{7,8},{8,9},{9,10},{10,1... | collective-permute-start | bytes 36872 | tf_op jit(solution)/shard_map/ppermute | solution.py:562
  65.3 3.1 %collective-permute-done.2.arrived = f32[3,8,128]{2,1,0:T(8,128)S(1)} collective-permute-done((f32[3,8,128]{2,1,0:T(8,128)S(1)}, f32[3,8,128]{2,1,0:T(8,128)S(1)}, u32[]{:S(2)}, u32[]{:S(2)}) %collective-permute-start.2) | collective-permute-done | bytes 12320 | tf_op jit(solution)/shard_map/ppermute | solution.py:562
  68.4 6.8 %all-to-all-done.2.totals = f32[16,1,128]{2,1,0:T(1,128)S(1)} async-done(((f32[16,1,128]{2,1,0:T(1,128)}), f32[16,1,128]{2,1,0:T(1,128)S(1)}, u32[]{:S(2)}, u32[]{:S(2)}) %all-to-all-start.2) | async-done | bytes 8224 | tf_op jit(solution)/shard_map/all_to_all | solution.py:615
  75.2 0.0 copy-done.1
  75.2 0.7 shard_map.69
  (6 shorter events, 0.1 us)
Async XLA Ops:
  0.6 0.7 copy-start
  1.4 0.7 copy-start.2
  4.0 9.8 %collective-permute-start = (f32[6,4,8,128]{3,2,1,0:T(8,128)S(1)}, f32[6,4,8,128]{3,2,1,0:T(8,128)S(1)}, u32[]{:S(2)}, u32[]{:S(2)}) collective-permute-start(f32[6,4,8,128]{3,2,1,0:T(8,128)S(1)} %all-gather.own), channel_id=1, source_target_pairs={{0,1},{1,2},{2,3},{3,4},{4,5},{5,6},{6,7},{7,8},{8,9},{9,10},{10,1... | collective-permute-start | bytes 294920 | tf_op jit(solution)/shard_map/ppermute | solution.py:597
  7.4 0.7 copy-start.3
  18.8 2.6 %collective-permute-start.1 = (f32[8,256]{1,0:T(8,128)S(1)}, f32[8,256]{1,0:T(8,128)S(1)}, u32[]{:S(2)}, u32[]{:S(2)}) collective-permute-start(f32[8,256]{1,0:T(8,128)S(1)} %get-tuple-element.20), channel_id=1, source_target_pairs={{0,4},{1,5},{2,6},{3,7},{4,8},{5,9},{6,10},{7,11},{8,12},{9,13},{1... | collective-permute-start | bytes 24584 | tf_op jit(solution)/shard_map/ppermute | solution.py:604
  54.3 20.9 %copy-start.1 = (s32[1,4,8,128]{3,2,1,0:T(8,128)S(1)}, s32[1,4,8,128]{3,2,1,0:T(8,128)}, u32[]{:S(2)}) copy-start(s32[1,4,8,128]{3,2,1,0:T(8,128)} %load.1) | copy-start | bytes 49156
  54.9 20.3 %all-to-all-start.2 = ((f32[16,1,128]{2,1,0:T(1,128)}), f32[16,1,128]{2,1,0:T(1,128)S(1)}, u32[]{:S(2)}, u32[]{:S(2)}) async-start(f32[16,1,128]{2,1,0:T(1,128)} %broadcast_in_dim.17), calls=%async_computation.2 | async-start | bytes 16384 | tf_op jit(solution)/shard_map/all_to_all | solution.py:615
  62.8 5.6 %collective-permute-start.2 = (f32[3,8,128]{2,1,0:T(8,128)S(1)}, f32[3,8,128]{2,1,0:T(8,128)S(1)}, u32[]{:S(2)}, u32[]{:S(2)}) collective-permute-start(f32[3,8,128]{2,1,0:T(8,128)S(1)} %get-tuple-element.24), channel_id=1, source_target_pairs={{0,1},{1,2},{2,3},{3,4},{4,5},{5,6},{6,7},{7,8},{8,9},{9,10},{10,1... | collective-permute-start | bytes 36872 | tf_op jit(solution)/shard_map/ppermute | solution.py:562

commit v8 on v7

--- a/solution.py
+++ b/solution.py
@@ -161,6 +161,18 @@
     return factors
 
 
+def run_sweeps(sweeps, count):
+    @pl.when(count >= SWEEPS)
+    def _():
+        for sweep in sweeps:
+            sweep()
+
+    @pl.when(count < SWEEPS)
+    def _():
+        for k, sweep in enumerate(sweeps, 1):
+            pl.when(k < count)(sweep)
+
+
 class Plane:
     def __init__(self, step):
         lane = lax.broadcasted_iota(jnp.int32, (ROWS, COLS), 1)
@@ -388,10 +400,10 @@
     def modulus_at(q):
         return mod[q + 1]
 
+    sweeps = []
     for k, (keep, add) in enumerate(chebyshev_factors(), 1):
 
-        @pl.when(k < sweep_count)
-        def _(k=k, keep=keep, add=add):
+        def sweep(k=k, keep=keep, add=add):
             def consume(q, forces, _energy):
                 f, weight = free[q], w[q] * np.float32(add)
                 is_free = f > 0.0
@@ -405,6 +417,10 @@
                     x[c, q] = now + update
 
             apply_planes(plane, k - 1, 10 - k, load, modulus_at, 1.0, consume)
+
+        sweeps.append(sweep)
+
+    run_sweeps(sweeps, sweep_count)
 
     def consume_left(q, forces, _energy):
         is_free = free[q] > 0.0
@@ -466,10 +482,10 @@
         xc[c] = start
         d[c] = start
 
+    sweeps = []
     for k, (keep, add) in enumerate(chebyshev_factors(), 1):
 
-        @pl.when(k < sweep_count)
-        def _(k=k, keep=keep, add=add):
+        def sweep(k=k, keep=keep, add=add):
             now = [xc[c] for c in range(3)]
             forces = block.apply(now, modulus, 4.0)
             weight = inverse * np.float32(add)
@@ -477,6 +493,10 @@
                 update = np.float32(keep) * d[c] + weight * (targets[c] - forces[c])
                 d[c] = update
                 xc[c] = now[c] + update
+
+        sweeps.append(sweep)
+
+    run_sweeps(sweeps, sweep_count)
 
     def prolonged(c, q):
         first = jnp.broadcast_to(xc[c, 2 * q : 2 * q + 1], (ROWS, COLS))

time: 76.5 us -> 77.1 us (level)
  no operation moved by 1% of the time
where the time goes in v8:
time: 77.1 us; the launch traced here: 76.1 us
  blocking collectives  35.4 us (46%)
  waiting for transfers between devices  16.8 us (22%)
  starting transfers between devices  15.1 us (20%)
  Pallas kernels  5.3 us (7%)
  local copies, waits for them, and re-layouts  2 us (3%)
  other arithmetic  0.85 us (1%)
    all_to_all x1, blocking collectives, on_device(): sums = lax.all_to_all(sums, ('y', 'x'), 0, 0)  22.5 us
    all_to_all x1, blocking collectives, on_device(): gathered = lax.all_to_all(sent, ('mirror', 'x'), 0, 0)  9.1 us
    all_to_all x1, starting transfers between devices, on_device(): sums = lax.all_to_all(sums, 'z', 0, 0)  7.92 us
    all_to_all x1, waiting for transfers between devices, on_device(): sums = lax.all_to_all(sums, 'z', 0, 0)  6.78 us
    ppermute x1, waiting for transfers between devices, on_device(): both = lax.all_gather(lax.ppermute(own, ('mirror',) + SLAB, near), 'mirror')  5.63 us
    pallas_call x3, Pallas kernels, call(): pl.pallas_call(kernel, out_shape=[jax.ShapeDtypeStruct(shape, jnp.float32...  5.3 us
    ppermute x1, starting transfers between devices, on_device(): both = lax.all_gather(lax.ppermute(own, ('mirror',) + SLAB, near), 'mirror')  3.39 us
    ppermute x1, waiting for transfers between devices, shifted(): return lax.ppermute(array, axis, pairs)  3.09 us
  transfers between devices with their start and end apart: 4, of which 4 were waited for; matrix products, arithmetic and copies ran while one was open for 0% of the time, Pallas kernels for 0%

profile of v8, /device:TPU:2, one launch (start us, length us, event | category | flops | bytes accessed | tf_op | source)
XLA Modules:
  0.0 76.1 jit_solution(9548056045601691325)
XLA Ops:
  0.6 0.0 copy-start
  0.6 0.7 convert_element_type.6
  1.4 0.0 copy-done
  1.4 0.0 copy-start.2
  1.4 0.7 copy-done.2
  2.1 1.9 %all-gather.own = f32[6,4,8,128]{3,2,1,0:T(8,128)S(1)} all-gather(f32[3,4,8,128]{3,2,1,0:T(8,128)S(1)} %pad_maximum_fusion), channel_id=2, replica_groups=mesh['mirror'=2,'y'=4,'z'=16,'x'=4] {'mirror'}, dimensions={0}, use_global_device_ids=true | all-gather | bytes 147456 | tf_op jit(solution)/shard_map/all_gather | solution.py:614
  4.0 3.4 %collective-permute-start = (f32[6,4,8,128]{3,2,1,0:T(8,128)S(1)}, f32[6,4,8,128]{3,2,1,0:T(8,128)S(1)}, u32[]{:S(2)}, u32[]{:S(2)}) collective-permute-start(f32[6,4,8,128]{3,2,1,0:T(8,128)S(1)} %all-gather.own), channel_id=1, source_target_pairs={{0,1},{1,2},{2,3},{3,4},{4,5},{5,6},{6,7},{7,8},{8,9},{9,10},{10,1... | collective-permute-start | bytes 294920 | tf_op jit(solution)/shard_map/ppermute | solution.py:617
  7.4 0.0 copy-start.3
  7.4 0.6 copy-done.3
  8.0 0.1 pad_add_fusion.info
  8.1 5.6 %collective-permute-done = f32[6,4,8,128]{3,2,1,0:T(8,128)S(1)} collective-permute-done((f32[6,4,8,128]{3,2,1,0:T(8,128)S(1)}, f32[6,4,8,128]{3,2,1,0:T(8,128)S(1)}, u32[]{:S(2)}, u32[]{:S(2)}) %collective-permute-start) | collective-permute-done | bytes 98336 | tf_op jit(solution)/shard_map/ppermute | solution.py:617
  13.7 1.9 %all-gather.1 = f32[12,4,8,128]{3,2,1,0:T(8,128)S(1)} all-gather(f32[6,4,8,128]{3,2,1,0:T(8,128)S(1)} %collective-permute-done), channel_id=3, replica_groups=mesh['mirror'=2,'y'=4,'z'=16,'x'=4] {'mirror'}, dimensions={0}, use_global_device_ids=true | all-gather | bytes 294912 | tf_op jit(solution)/shard_map/all_gather | solution.py:617
  15.7 3.0 %shard_map.67 = (f32[3,5,8,256]{3,2,1,0:T(8,128)S(1)}, f32[8,256]{1,0:T(8,128)S(1)}, f32[4,8,256]{2,1,0:T(8,128)S(1)}, f32[5,8,256]{2,1,0:T(8,128)S(1)}, f32[4,8,256]{2,1,0:T(8,128)S(1)}) custom-call(s32[4]{0:T(128)S(1)} %pad_add_fusion.info, f32[6,4,8,128]{3,2,1,0:T(8,128)S(1)} %all-gather.own, f32[6,4,8,128]{3,2,1,0:T(8,128)S(1)} %get-tuple-element.30.below, ...), custom_call_target="tpu_custom_call" | custom-call | tf_op jit(solution)/shard_map/pallas_call | solution.py:569
  18.7 1.3 %collective-permute-start.1 = (f32[8,256]{1,0:T(8,128)S(1)}, f32[8,256]{1,0:T(8,128)S(1)}, u32[]{:S(2)}, u32[]{:S(2)}) collective-permute-start(f32[8,256]{1,0:T(8,128)S(1)} %get-tuple-element.20), channel_id=1, source_target_pairs={{0,4},{1,5},{2,6},{3,7},{4,8},{5,9},{6,10},{7,11},{8,12},{9,13},{1... | collective-permute-start | bytes 24584 | tf_op jit(solution)/shard_map/ppermute | solution.py:624
  20.0 1.3 %collective-permute-done.1 = f32[8,256]{1,0:T(8,128)S(1)} collective-permute-done((f32[8,256]{1,0:T(8,128)S(1)}, f32[8,256]{1,0:T(8,128)S(1)}, u32[]{:S(2)}, u32[]{:S(2)}) %collective-permute-start.1) | collective-permute-done | bytes 8224 | tf_op jit(solution)/shard_map/ppermute | solution.py:624
  21.3 9.1 %all_to_all.15.gathered = f32[8,16,256]{2,1,0:T(8,128)S(1)} all-to-all(f32[8,16,256]{2,1,0:T(8,128)S(1)} %broadcast_in_dim.16), channel_id=1, replica_groups=mesh['mirror'=2,'y'=4,'z'=16,'x'=4] {'mirror','x'}, dimensions={0} | all-to-all | bytes 262144 | tf_op jit(solution)/shard_map/all_to_all | solution.py:626
  30.4 1.6 %shard_map.68 = (f32[3,4,8,128]{3,2,1,0:T(8,128)S(1)}, f32[3,4,8,128]{3,2,1,0:T(8,128)S(1)}, f32[3,8,128]{2,1,0:T(8,128)S(1)}, f32[4,8,128]{2,1,0:T(8,128)S(1)}, f32[16,1,128]{2,1,0:T(1,128)S(1)}) custom-call(s32[4]{0:T(128)S(1)} %pad_add_fusion.info, f32[3,5,8,256]{3,2,1,0:T(8,128)S(1)} %get-tuple-element.16.smooth, ...), custom_call_target="tpu_custom_call" | custom-call | tf_op jit(solution)/shard_map/pallas_call | solution.py:569
  32.0 22.5 %all_to_all.16 = f32[16,1,128]{2,1,0:T(1,128)S(1)} all-to-all(f32[16,1,128]{2,1,0:T(1,128)S(1)} %get-tuple-element.21), channel_id=1, replica_groups=mesh['mirror'=2,'y'=4,'z'=16,'x'=4] {'y','x'}, dimensions={0} | all-to-all | bytes 16384 | tf_op jit(solution)/shard_map/all_to_all | solution.py:632
  54.5 0.0 copy-start.1
  54.5 0.6 broadcast_in_dim.17
  55.1 7.9 %all-to-all-start.2 = ((f32[16,1,128]{2,1,0:T(1,128)}), f32[16,1,128]{2,1,0:T(1,128)S(1)}, u32[]{:S(2)}, u32[]{:S(2)}) async-start(f32[16,1,128]{2,1,0:T(1,128)} %broadcast_in_dim.17), calls=%async_computation.2 | async-start | bytes 16384 | tf_op jit(solution)/shard_map/all_to_all | solution.py:635
  63.0 2.5 %collective-permute-start.2 = (f32[3,8,128]{2,1,0:T(8,128)S(1)}, f32[3,8,128]{2,1,0:T(8,128)S(1)}, u32[]{:S(2)}, u32[]{:S(2)}) collective-permute-start(f32[3,8,128]{2,1,0:T(8,128)S(1)} %get-tuple-element.24), channel_id=1, source_target_pairs={{0,1},{1,2},{2,3},{3,4},{4,5},{5,6},{6,7},{7,8},{8,9},{9,10},{10,1... | collective-permute-start | bytes 36872 | tf_op jit(solution)/shard_map/ppermute | solution.py:582
  65.5 3.1 %collective-permute-done.2.arrived = f32[3,8,128]{2,1,0:T(8,128)S(1)} collective-permute-done((f32[3,8,128]{2,1,0:T(8,128)S(1)}, f32[3,8,128]{2,1,0:T(8,128)S(1)}, u32[]{:S(2)}, u32[]{:S(2)}) %collective-permute-start.2) | collective-permute-done | bytes 12320 | tf_op jit(solution)/shard_map/ppermute | solution.py:582
  68.6 6.8 %all-to-all-done.2.totals = f32[16,1,128]{2,1,0:T(1,128)S(1)} async-done(((f32[16,1,128]{2,1,0:T(1,128)}), f32[16,1,128]{2,1,0:T(1,128)S(1)}, u32[]{:S(2)}, u32[]{:S(2)}) %all-to-all-start.2) | async-done | bytes 8224 | tf_op jit(solution)/shard_map/all_to_all | solution.py:635
  75.4 0.0 copy-done.1
  75.4 0.7 shard_map.69
  (6 shorter events, 0.1 us)
Async XLA Ops:
  0.6 0.7 copy-start
  1.4 0.7 copy-start.2
  4.0 9.8 %collective-permute-start = (f32[6,4,8,128]{3,2,1,0:T(8,128)S(1)}, f32[6,4,8,128]{3,2,1,0:T(8,128)S(1)}, u32[]{:S(2)}, u32[]{:S(2)}) collective-permute-start(f32[6,4,8,128]{3,2,1,0:T(8,128)S(1)} %all-gather.own), channel_id=1, source_target_pairs={{0,1},{1,2},{2,3},{3,4},{4,5},{5,6},{6,7},{7,8},{8,9},{9,10},{10,1... | collective-permute-start | bytes 294920 | tf_op jit(solution)/shard_map/ppermute | solution.py:617
  7.4 0.7 copy-start.3
  18.7 2.6 %collective-permute-start.1 = (f32[8,256]{1,0:T(8,128)S(1)}, f32[8,256]{1,0:T(8,128)S(1)}, u32[]{:S(2)}, u32[]{:S(2)}) collective-permute-start(f32[8,256]{1,0:T(8,128)S(1)} %get-tuple-element.20), channel_id=1, source_target_pairs={{0,4},{1,5},{2,6},{3,7},{4,8},{5,9},{6,10},{7,11},{8,12},{9,13},{1... | collective-permute-start | bytes 24584 | tf_op jit(solution)/shard_map/ppermute | solution.py:624
  54.5 20.9 %copy-start.1 = (s32[1,4,8,128]{3,2,1,0:T(8,128)S(1)}, s32[1,4,8,128]{3,2,1,0:T(8,128)}, u32[]{:S(2)}) copy-start(s32[1,4,8,128]{3,2,1,0:T(8,128)} %load.1) | copy-start | bytes 49156
  55.1 20.3 %all-to-all-start.2 = ((f32[16,1,128]{2,1,0:T(1,128)}), f32[16,1,128]{2,1,0:T(1,128)S(1)}, u32[]{:S(2)}, u32[]{:S(2)}) async-start(f32[16,1,128]{2,1,0:T(1,128)} %broadcast_in_dim.17), calls=%async_computation.2 | async-start | bytes 16384 | tf_op jit(solution)/shard_map/all_to_all | solution.py:635
  63.0 5.6 %collective-permute-start.2 = (f32[3,8,128]{2,1,0:T(8,128)S(1)}, f32[3,8,128]{2,1,0:T(8,128)S(1)}, u32[]{:S(2)}, u32[]{:S(2)}) collective-permute-start(f32[3,8,128]{2,1,0:T(8,128)S(1)} %get-tuple-element.24), channel_id=1, source_target_pairs={{0,1},{1,2},{2,3},{3,4},{4,5},{5,6},{6,7},{7,8},{8,9},{9,10},{10,1... | collective-permute-start | bytes 36872 | tf_op jit(solution)/shard_map/ppermute | solution.py:582
